TPU v7x, 256 devices: a whole 4x4x8 slice. The times are simulated.
256 devices in a mesh: fsdp: 16 (over x_hi, y, core), tensor: 16 (over x_lo, z).
Axes of the slice: x: 4 (x_hi: 2, x_lo: 2; x = x_hi * 2 + x_lo), y: 4, z: 8, core: 2. Of those that a mesh axis runs over, the one named last changes fastest.
Arguments:
- tokens: bfloat16 [2048, 4096], P(('fsdp', 'tensor')), may hold values from -19 to 19
- targets: bfloat16 [2048, 4096], P(('fsdp', 'tensor')), may hold values from -6 to 6
- gate_up: bfloat16 [4096, 2, 7168], P(None, None, 'tensor'), may hold values from -0.09375 to 0.09375
- down_weight: bfloat16 [7168, 4096], P('tensor'), may hold values from -0.0625 to 0.0625
- direction: bfloat16 [4096, 2, 7168], P('fsdp', None, 'tensor'), may hold values from -47 to 47
- previous: bfloat16 [4096, 2, 7168], P('fsdp', None, 'tensor'), may hold values from -47 to 47
- beta_prev: float32 [], replicated, may hold values from 0.5 to 2
Outputs:
- new_direction: bfloat16 [4096, 2, 7168], P('fsdp', None, 'tensor')
- tri_diagonal: float32 [], replicated
- tri_offdiagonal: float32 [], replicated
All inputs are finite; a program needn't handle non-finite values.
Results may differ from a plain program's by a relative error of at most 0.025.
Values may be sent and summed in bfloat16 or wider, within the bound.
No kernel may reach another device: no remote copies, remote signals or barrier semaphores. Data moves between devices by JAX's collectives and lax.ppermute only.
A program may use at most 64 MiB of HBM per device.

v0:
```python
import jax
import jax.numpy as jnp
from jax import lax
from jax.experimental import pallas as pl
from jax.experimental.pallas import tpu as pltpu
from jax.sharding import Mesh, PartitionSpec as P

BF = jnp.bfloat16
F32 = jnp.float32
AXES = ("x_hi", "y", "core", "x_lo", "z")
SIZES = (2, 4, 2, 2, 8)


def swap(value, axis, step=1):
    size = lax.axis_size(axis)
    return lax.ppermute(value, axis, [(i, i ^ step) for i in range(size)])


def silu_parts(gate_pre):
    sigma_gate = jax.nn.sigmoid(gate_pre)
    silu_value = gate_pre * sigma_gate
    silu_slope = sigma_gate * (1.0 + gate_pre * (1.0 - sigma_gate))
    silu_curve = sigma_gate * (1.0 - sigma_gate) * (2.0 + gate_pre * (1.0 - 2.0 * sigma_gate))
    return (silu_value, silu_slope, silu_curve)


def neighbour(value):
    return lax.ppermute(value, "z", [(i, (i + 1) % 8 if i % 2 else (i - 1) % 8) for i in range(8)])


def by_pair(value):
    at = lax.axis_index("z") % 4
    return jnp.where((at == 1) | (at == 2), value[jnp.array([1, 0, 3, 2])], value[::-1])


def gather_even(block):
    return jnp.stack([block] + [swap(block, "z", d) for d in (2, 4, 6)])


def gather_z(even):
    half = even.shape[2] // 2
    odd = jnp.concatenate([swap(even[..., :half], "z"), by_pair(neighbour(even[..., half:]))], 2)
    return even, odd


def gather_x(even, odd):
    return jnp.concatenate([even, odd, swap(even, "x_lo"), swap(odd, "x_lo")], 0)


def fold_x(partial):
    rows, width = partial.shape
    halves = partial.reshape(2, 2, 4, rows // 16, width)
    other = swap(halves[1], "x_lo")
    return (halves[0].astype(F32) + other.astype(F32)).astype(BF)


def fold_z(folded):
    half = folded.shape[-1] // 2
    even, odd = folded[0], folded[1]
    other = jnp.concatenate([swap(odd[..., :half], "z"), by_pair(neighbour(odd[..., half:]))], 2)
    even = (even.astype(F32) + other.astype(F32)).astype(BF)
    total = even[0].astype(F32)
    for at in range(1, 4):
        total = total + swap(even[at], "z", 2 * at).astype(F32)
    return total


def dot(a, b, dims):
    return lax.dot_general(a, b, (dims, ((), ())), preferred_element_type=F32)


def tangent_kernel(first, index_ref, rows_ref, other_ref, pieces_ref, *refs):
    before, outs = refs[:first], refs[first:]
    for k in range(2):
        total = before[0][k] if before else 0.0
        for at in range(4):
            start = pl.multiple_of(index_ref[4 * first + at] * 256, 256)
            rows = jnp.concatenate([ref[:, pl.ds(start, 256)] for ref in (rows_ref, other_ref)], 0)
            total = total + dot(pieces_ref[at, k], rows, ((1,), (1,)))
        width = outs[0].shape[2]
        for at, out in enumerate(outs):
            out[k] = total[:, at * width : (at + 1) * width]


def act_kernel(projected_ref, own_ref, other_ref, tangent_ref, act_ref):
    gate, up = [own_ref[k] + other_ref[k] for k in range(2)]
    tangent_ref[0], tangent_ref[1] = gate, up
    silu_value, silu_slope, _ = silu_parts(projected_ref[0])
    act_ref[...] = (silu_slope * gate * projected_ref[1] + silu_value * up).astype(BF)


STEPS = 4


def tangent_call(first, index, rows, pieces, before, out_shape):
    hidden = pieces.shape[2]
    chunk = hidden // STEPS

    def spec(size):
        return pl.BlockSpec((2, chunk, size), lambda i, index: (0, i, 0))

    return pl.pallas_call(
        lambda *refs: tangent_kernel(first, *refs),
        out_shape=out_shape,
        grid_spec=pltpu.PrefetchScalarGridSpec(
            num_scalar_prefetch=1,
            grid=(STEPS,),
            in_specs=[pl.BlockSpec(r.shape, lambda i, index: (0, 0)) for r in rows]
            + [pl.BlockSpec((4, 2, chunk, pieces.shape[3]), lambda i, index: (0, 0, i, 0))]
            + [spec(b.shape[2]) for b in before],
            out_specs=[spec(o.shape[2]) for o in out_shape],
        ),
        compiler_params=pltpu.CompilerParams(vmem_limit_bytes=32 * 2**20),
        cost_estimate=pl.CostEstimate(
            flops=8 * hidden * pieces.shape[3] * rows[0].shape[0] * 4,
            bytes_accessed=pieces.size * 2,
            transcendentals=0,
        ),
    )(index, *rows, pieces, *before)


def curvature_kernel(index_ref, beta_ref, columns_ref, *refs):
    blocks, (current_ref, earlier_ref, shifted_ref, sums_ref) = refs[:4], refs[4:]
    curvature = 0.0
    for at, block in enumerate(blocks):
        rows = jnp.concatenate([columns_ref[index_ref[4 * at + y]] for y in range(4)], 0)
        grads = jnp.concatenate([block[y] for y in range(4)], 1)
        curvature = curvature + dot(grads, rows, ((1,), (0,)))
    current = current_ref[...].astype(F32)
    shifted = curvature - beta_ref[0, 0] * earlier_ref[...].astype(F32)
    shifted_ref[...] = shifted

    def row(product):
        lanes = jnp.sum(product, 0, keepdims=True)
        return lanes[:, :128] + lanes[:, 128:]

    @pl.when(pl.program_id(0) == 0)
    def _():
        sums_ref[...] = jnp.zeros_like(sums_ref)

    parts = [row(p) for p in (curvature * current, shifted * shifted, shifted * current, current * current)]
    sums_ref[...] += jnp.concatenate(parts + [jnp.zeros((4, 128), F32)], 0)


def scale_kernel(entry_count, sums_ref, shifted_ref, current_ref, out_ref, rayleigh_ref, offdiagonal_ref):
    sums = jnp.sum(jnp.sum(sums_ref[...], 0), 1, keepdims=True)
    inner, square, mixed, norm = [sums[k : k + 1] for k in range(4)]
    rayleigh = inner / entry_count
    square = (square - 2.0 * rayleigh * mixed + rayleigh * rayleigh * norm) / entry_count
    offdiagonal = jnp.sqrt(jnp.maximum(square, 0.0) + 1e-06)
    rayleigh_ref[...] = jnp.broadcast_to(rayleigh, rayleigh_ref.shape)
    offdiagonal_ref[...] = jnp.broadcast_to(offdiagonal, offdiagonal_ref.shape)
    residual = shifted_ref[...] - rayleigh * current_ref[...].astype(F32)
    out_ref[...] = (residual / offdiagonal).astype(BF)


def per_device(tokens, targets, gate_up, down_weight, direction, previous, beta_prev):
    width = tokens.shape[1]
    hidden = down_weight.shape[0]
    own_rows = direction.shape[0]
    token_total = tokens.shape[0] * 256
    gate_up_t = gate_up.transpose(1, 2, 0).reshape(2 * hidden, width)
    current_t = direction.transpose(1, 2, 0).reshape(2 * hidden, own_rows)
    earlier_t = previous.transpose(1, 2, 0).reshape(2 * hidden, own_rows)
    x_hi, y_at, core, x_lo, z_at = (lax.axis_index(n) for n in AXES)

    def owner(a, y, c):
        return ((x_hi ^ a) * 4 + y) * 2 + (core ^ c)

    index = jnp.stack([owner(0, y, 0) for y in range(4)] + [owner(1, y, 0) for y in range(4)])

    current_far = swap(current_t, "x_hi")
    near = lax.all_gather(current_t, "y")
    far = lax.all_gather(current_far, "y")

    even, current_far = lax.optimization_barrier((gather_even(tokens), current_far))
    group_rows = gather_x(*gather_z(even)).reshape(-1, width)
    other_rows = swap(group_rows, "core")

    projected = dot(gate_up_t, group_rows, ((1,), (1,)))
    projected, near = lax.optimization_barrier((projected, near))
    gate_pre, up_pre = projected[:hidden], projected[hidden:]
    silu_value, silu_slope, silu_curve = silu_parts(gate_pre)
    hidden_act = (silu_value * up_pre).astype(BF)
    output_part = dot(hidden_act, down_weight, ((0,), (0,))).astype(BF)
    output_fold = fold_x(output_part)

    def cut(value, start, size):
        return lax.dynamic_slice_in_dim(value, start * own_rows, size * own_rows, value.ndim - 1)

    both = jnp.stack([cut(group_rows, x_hi * 8, 8), swap(cut(group_rows, 8 - x_hi * 8, 8), "x_hi")])

    def halves(value):
        return value.reshape(2, hidden, value.shape[1])

    chunk = hidden // STEPS
    count = group_rows.shape[0]

    def sum_of(size):
        return jax.ShapeDtypeStruct((2, hidden, size), F32)

    own_shape = sum_of(count)
    rows_pair = (group_rows, other_rows)
    near_sums = tangent_call(0, index, rows_pair, near.reshape(4, 2, hidden, -1), [], [sum_of(2 * count)])
    own_sums, other_sums = tangent_call(
        1, index, rows_pair, far.reshape(4, 2, hidden, -1), near_sums, [own_shape, own_shape]
    )
    step_spec = pl.BlockSpec((2, chunk, count), lambda i: (0, i, 0))
    tangent, tangent_act = pl.pallas_call(
        act_kernel,
        out_shape=(own_shape, jax.ShapeDtypeStruct((hidden, count), BF)),
        grid=(STEPS,),
        in_specs=[step_spec] * 3,
        out_specs=(step_spec, pl.BlockSpec((chunk, count), lambda i: (i, 0))),
        compiler_params=pltpu.CompilerParams(vmem_limit_bytes=32 * 2**20),
        cost_estimate=pl.CostEstimate(flops=2**20, bytes_accessed=2 * 2**20, transcendentals=2**16),
    )(halves(projected), own_sums, swap(other_sums, "core"))
    tangent_gate, tangent_up = tangent[0], tangent[1]
    tangent_part = dot(tangent_act, down_weight, ((0,), (0,))).astype(BF)
    tangent_fold = fold_x(tangent_part)


    output_sum = fold_z(output_fold)
    tangent_sum = fold_z(tangent_fold)
    error_rows = ((output_sum - targets.astype(F32)) / token_total).astype(BF)
    tangent_error = (tangent_sum / token_total).astype(BF)
    errors = jnp.concatenate([error_rows, tangent_error], 0)
    errors, both = lax.optimization_barrier((errors, both))
    own_columns = jnp.stack(
        [cut(both, y_at * 2, 2)] + [swap(cut(both, (y_at ^ d) * 2, 2), "y", d) for d in range(1, 4)], 1
    )
    own_columns = jnp.stack(
        [cut(own_columns, core, 1), swap(cut(own_columns, 1 - core, 1), "core")], 1
    ).reshape(16, count, own_rows)
    errors = gather_x(*gather_z(gather_even(errors))).reshape(16, 2, -1, width)
    back_error = dot(down_weight, errors[:, 0].reshape(-1, width), ((1,), (1,)))
    back_tangent = dot(down_weight, errors[:, 1].reshape(-1, width), ((1,), (1,)))

    grad_gate = back_tangent * up_pre * silu_slope + back_error * (
        tangent_up * silu_slope + up_pre * silu_curve * tangent_gate
    )
    grad_up = back_tangent * silu_value + back_error * silu_slope * tangent_gate
    tangent_grad = jnp.concatenate([grad_gate, grad_up], 0).astype(BF)
    grad_far = swap(tangent_grad, "x_hi")
    blocks = []
    for piece in (tangent_grad, grad_far):
        piece = lax.all_gather(piece, "y")
        blocks += [piece, swap(piece, "core")]
    groups = jnp.stack([(a * 2 + c) * 4 + (y_at ^ y) for a in range(2) for c in range(2) for y in range(4)])
    rows = 2 * hidden // STEPS
    row_spec = pl.BlockSpec((rows, own_rows), lambda i, index: (i, 0))
    shifted, sums = pl.pallas_call(
        curvature_kernel,
        out_shape=(
            jax.ShapeDtypeStruct((2 * hidden, own_rows), F32),
            jax.ShapeDtypeStruct((8, 128), F32),
        ),
        grid_spec=pltpu.PrefetchScalarGridSpec(
            num_scalar_prefetch=1,
            grid=(STEPS,),
            in_specs=[
                pl.BlockSpec(memory_space=pltpu.SMEM),
                pl.BlockSpec(own_columns.shape, lambda i, index: (0, 0, 0)),
            ]
            + [pl.BlockSpec((4, rows, count), lambda i, index: (0, i, 0))] * 4
            + [row_spec] * 2,
            out_specs=(row_spec, pl.BlockSpec((8, 128), lambda i, index: (0, 0))),
        ),
        compiler_params=pltpu.CompilerParams(vmem_limit_bytes=32 * 2**20),
        cost_estimate=pl.CostEstimate(flops=2**30, bytes_accessed=7 * 2**20, transcendentals=0),
    )(groups, beta_prev.reshape(1, 1), own_columns, *blocks, current_t, earlier_t)

    for axes in (("z",), AXES[:4]):
        size = lax.axis_size(axes)
        if axes != ("z",):
            sums = sums.sum(0)
        sums = lax.all_to_all(jnp.broadcast_to(sums[None], (size, 8, 128)), axes, 0, 0, tiled=True)

    row_spec = pl.BlockSpec((rows, own_rows), lambda i: (i, 0))
    one_spec = pl.BlockSpec((1, 128), lambda i: (0, 0))
    new_direction, rayleigh, offdiagonal = pl.pallas_call(
        lambda *refs: scale_kernel(2 * own_rows * hidden * 256, *refs),
        out_shape=(
            jax.ShapeDtypeStruct((2 * hidden, own_rows), BF),
            jax.ShapeDtypeStruct((1, 128), F32),
            jax.ShapeDtypeStruct((1, 128), F32),
        ),
        grid=(STEPS,),
        in_specs=[pl.BlockSpec(sums.shape, lambda i: (0, 0, 0)), row_spec, row_spec],
        out_specs=(row_spec, one_spec, one_spec),
        compiler_params=pltpu.CompilerParams(vmem_limit_bytes=32 * 2**20),
        cost_estimate=pl.CostEstimate(flops=2**20, bytes_accessed=2 * 2**20, transcendentals=0),
    )(sums, shifted, current_t)
    rayleigh, offdiagonal = rayleigh[0, 0], offdiagonal[0, 0]
    new_direction = new_direction.reshape(2, hidden, own_rows).transpose(2, 0, 1)
    return (new_direction, rayleigh, offdiagonal)


def solution(mesh):
    fine = Mesh(mesh.devices.reshape(SIZES), AXES)
    fsdp, tensor = AXES[:3], AXES[3:]
    placed = (
        P(fsdp + tensor, None),
        P(fsdp + tensor, None),
        P(None, None, tensor),
        P(tensor, None),
        P(fsdp, None, tensor),
        P(fsdp, None, tensor),
        P(),
    )
    return jax.shard_map(
        per_device,
        mesh=fine,
        in_specs=placed,
        out_specs=(P(fsdp, None, tensor), P(), P()),
        check_vma=False,
    )
```

profile of v0, /device:TPU:1, one launch (start us, length us, event | category | flops | bytes accessed | tf_op | source)
XLA Modules:
  0.0 259.4 jit_solution(6526357135098632621)
XLA Ops:
  7.9 6.9 %collective-permute-start.2 = (bf16[8,4096]{1,0:T(8,128)(2,1)}, bf16[8,4096]{1,0:T(8,128)(2,1)S(1)}, u32[]{:S(2)}, u32[]{:S(2)}) collective-permute-start(bf16[8,4096]{1,0:T(8,128)(2,1)} %param.11), channel_id=1, source_target_pairs={{0,6},{1,7},{2,4},{3,5},{4,2},{5,3},{6,0},{7,1},{8,14},{9,15},{10,... | collective-permute-start | bytes 196616 | tf_op jit(solution)/shard_map/ppermute | solution.py:16
  15.9 1.2 collective-permute-start
  17.1 2.7 %collective-permute-start.3 = (bf16[896,256]{1,0:T(8,128)(2,1)}, bf16[896,256]{1,0:T(8,128)(2,1)S(1)}, u32[]{:S(2)}, u32[]{:S(2)}) collective-permute-start(bf16[896,256]{1,0:T(8,128)(2,1)} %bitcast.162), channel_id=1, source_target_pairs={{0,128},{128,0},{1,129},{129,1},{2,130},{130,2},{3,131},{131,3},{4... | collective-permute-start | bytes 1376264 | tf_op jit(solution)/shard_map/ppermute | solution.py:16
  19.8 2.8 %collective-permute-done.1 = bf16[8,4096]{1,0:T(8,128)(2,1)S(1)} collective-permute-done((bf16[8,4096]{1,0:T(8,128)(2,1)}, bf16[8,4096]{1,0:T(8,128)(2,1)S(1)}, u32[]{:S(2)}, u32[]{:S(2)}) %collective-permute-start.1) | collective-permute-done | bytes 65568 | tf_op jit(solution)/shard_map/ppermute | solution.py:16
  22.6 1.4 collective-permute-done
  24.9 4.7 %collective-permute-done.3 = bf16[896,256]{1,0:T(8,128)(2,1)S(1)} collective-permute-done((bf16[896,256]{1,0:T(8,128)(2,1)}, bf16[896,256]{1,0:T(8,128)(2,1)S(1)}, u32[]{:S(2)}, u32[]{:S(2)}) %collective-permute-start.3) | collective-permute-done | bytes 458784 | tf_op jit(solution)/shard_map/ppermute | solution.py:16
  29.6 2.8 %collective-permute-start.5 = (bf16[4,8,2048]{2,1,0:T(8,128)(2,1)S(1)}, bf16[4,8,2048]{2,1,0:T(8,128)(2,1)S(1)}, u32[]{:S(2)}, u32[]{:S(2)}) collective-permute-start(bf16[4,8,2048]{2,1,0:T(8,128)(2,1)S(1)} %get-tuple-element.58), channel_id=1, source_target_pairs={{0,7},{1,2},{2,1},{3,4},{4,3},{5,6},{6,5},{7,0},{8,15},{9,10},{10,... | collective-permute-start | bytes 393224 | tf_op jit(solution)/shard_map/ppermute | solution.py:28
  33.1 1.2 collective-permute-start.6
  35.8 2.7 %collective-permute-done.4 = bf16[4,8,2048]{2,1,0:T(8,128)(2,1)S(1)} collective-permute-done((bf16[4,8,2048]{2,1,0:T(8,128)(2,1)S(1)}, bf16[4,8,2048]{2,1,0:T(8,128)(2,1)S(1)}, u32[]{:S(2)}, u32[]{:S(2)}) %collective-permute-start.4) | collective-permute-done | bytes 131104 | tf_op jit(solution)/shard_map/ppermute | solution.py:16
  38.9 5.8 %collective-permute-done.7 = bf16[4,8,4096]{2,1,0:T(8,128)(2,1)} collective-permute-done((bf16[4,8,4096]{2,1,0:T(8,128)(2,1)S(1)}, bf16[4,8,4096]{2,1,0:T(8,128)(2,1)}, u32[]{:S(2)}, u32[]{:S(2)}) %collective-permute-start.7) | collective-permute-done | bytes 262176 | tf_op jit(solution)/shard_map/ppermute | solution.py:16
  44.7 1.0 maximum_bitcast_fusion.refs_1_
  45.7 4.2 %collective-permute-start.14 = (bf16[128,4096]{1,0:T(8,128)(2,1)S(1)}, bf16[128,4096]{1,0:T(8,128)(2,1)S(1)}, u32[]{:S(2)}, u32[]{:S(2)}) collective-permute-start(bf16[128,4096]{1,0:T(8,128)(2,1)S(1)} %maximum_bitcast_fusion.refs_1_), channel_id=1, source_target_pairs={{0,16},{16,0},{1,17},{17,1},{2,18},{18,2},{3,19},{19,3},{4,20},{20... | collective-permute-start | bytes 3145736 | tf_op jit(solution)/shard_map/ppermute | solution.py:16
  49.9 5.2 %convolution_bitcast_fusion = f32[896,128]{1,0:T(8,128)S(1)} fusion(bf16[896,4096]{1,0:T(8,128)(2,1)} %bitcast.184, bf16[4,8,4096]{2,1,0:T(8,128)(2,1)} %collective-permute-done.7, bf16[4,8,4096]{2,1,0:T(8,128)(2,1)S(1)} %collective-permute-done.6, bf16[4,8,2048]{2,1,0:T(8,128)(2,1)S(1)} %reverse_select_fusion.3, ...), kind=kOutput, calls=%fused_computation.6 | convolution fusion | flops 944766976 | bytes 8847360 | tf_op jit(solution)/shard_map/dot_general | solution.py:69
  55.2 2.8 %convolution_convert_fusion.1 = bf16[128,4096]{1,0:T(8,128)(2,1)S(1)} fusion(bf16[448,4096]{1,0:T(8,128)(2,1)} %param.14, f32[896,128]{1,0:T(8,128)S(1)} %convolution_bitcast_fusion), kind=kOutput, calls=%fused_computation.5 | convolution fusion | flops 470630400 | bytes 5177344 | tf_op jit(solution)/shard_map/dot_general | solution.py:69
  58.0 1.1 fusion.27
  59.5 1.1 dynamic-slice_bitcast_fusion.1
  60.6 2.7 %collective-permute-start.22 = (bf16[128,2048]{1,0:T(8,128)(2,1)}, bf16[128,2048]{1,0:T(8,128)(2,1)}, u32[]{:S(2)}, u32[]{:S(2)}) collective-permute-start(bf16[128,2048]{1,0:T(8,128)(2,1)} %get-tuple-element.40), channel_id=1, source_target_pairs={{0,128},{128,0},{1,129},{129,1},{2,130},{130,2},{3,131},{131,3},{4... | collective-permute-start | bytes 1572872 | tf_op jit(solution)/shard_map/ppermute | solution.py:16
  63.3 2.7 %shard_map.130.refs_4_ = f32[2,448,256]{2,1,0:T(8,128)S(1)} custom-call(s32[8]{0:T(128)S(1)} %stack.171.refs_0_, bf16[128,4096]{1,0:T(8,128)(2,1)S(1)} %maximum_bitcast_fusion.refs_1_, bf16[128,4096]{1,0:T(8,128)(2,1)S(1)} %collective-permute-done.14.refs_2_, bf16[4,2,448,256]{3,2,1,0:T(8,128)(2,1)S(1)} %bitcast.167), custom_call_target="tpu_custom_call" | custom-call | flops 469762048 | bytes 1835008 | tf_op jit(solution)/shard_map/pallas_call | solution.py:102
  66.0 12.5 %all-gather.7.cloned.1.call-done = bf16[3584,256]{1,0:T(8,128)(2,1)} async-done(((bf16[896,256]{1,0:T(8,128)(2,1)}), bf16[3584,256]{1,0:T(8,128)(2,1)}) %all-gather.7.cloned.1.call-update) | async-done | bytes 1835024 | tf_op jit(solution)/shard_map/all_gather | solution.py:174
  78.5 1.5 copy-done.2
  80.0 3.5 %shard_map.131 = (f32[2,448,128]{2,1,0:T(8,128)S(1)}, f32[2,448,128]{2,1,0:T(8,128)}) custom-call(s32[8]{0:T(128)S(1)} %stack.171.refs_0_, bf16[128,4096]{1,0:T(8,128)(2,1)S(1)} %maximum_bitcast_fusion.refs_1_, bf16[128,4096]{1,0:T(8,128)(2,1)S(1)} %collective-permute-done.14.refs_2_, bf16[4,2,448,256]{3,2,1,0:T(8,128)(2,1)S(1)} %bitcast.168, ...), custom_call_target="tpu_custom_call" | custom-call | flops 469762048 | bytes 1835008 | tf_op jit(solution)/shard_map/pallas_call | solution.py:102
  84.2 1.2 fusion.1
  85.4 3.1 %collective-permute-start.10 = (bf16[4,8,2048]{2,1,0:T(8,128)(2,1)S(1)}, bf16[4,8,2048]{2,1,0:T(8,128)(2,1)S(1)}, u32[]{:S(2)}, u32[]{:S(2)}) collective-permute-start(bf16[4,8,2048]{2,1,0:T(8,128)(2,1)S(1)} %get-tuple-element.51), channel_id=1, source_target_pairs={{0,7},{1,2},{2,1},{3,4},{4,3},{5,6},{6,5},{7,0},{8,15},{9,10},{10,... | collective-permute-start | bytes 393224 | tf_op jit(solution)/shard_map/ppermute | solution.py:28
  88.6 1.1 pad_maximum_fusion
  90.0 2.3 collective-permute-done.10
  94.3 2.8 %convolution_convert_fusion = bf16[128,4096]{1,0:T(8,128)(2,1)S(1)} fusion(bf16[448,128]{1,0:T(8,128)(2,1)S(1)} %get-tuple-element.22, bf16[448,4096]{1,0:T(8,128)(2,1)} %param.14), kind=kOutput, calls=%fused_computation.4 | convolution fusion | flops 470286336 | bytes 4833280 | tf_op jit(solution)/shard_map/dot_general | solution.py:69
  97.2 1.3 collective-permute-start.16
  98.5 11.5 %collective-permute-done.16 = bf16[2,4,8,4096]{3,2,1,0:T(8,128)(2,1)S(1)} collective-permute-done((bf16[2,4,8,4096]{3,2,1,0:T(8,128)(2,1)S(1)}, bf16[2,4,8,4096]{3,2,1,0:T(8,128)(2,1)S(1)}, u32[]{:S(2)}, u32[]{:S(2)}) %collective-permute-start.16) | collective-permute-done | bytes 524320 | tf_op jit(solution)/shard_map/ppermute | solution.py:16
  110.2 2.1 collective-permute-start.18
  113.6 1.9 collective-permute-start.12
  115.6 3.0 %collective-permute-start.11 = (bf16[8,4096]{1,0:T(8,128)(2,1)S(1)}, bf16[8,4096]{1,0:T(8,128)(2,1)}, u32[]{:S(2)}, u32[]{:S(2)}) collective-permute-start(bf16[8,4096]{1,0:T(8,128)(2,1)S(1)} %get-tuple-element.47), channel_id=1, source_target_pairs={{0,2},{1,3},{2,0},{3,1},{4,6},{5,7},{6,4},{7,5},{8,10},{9,11},{10,... | collective-permute-start | bytes 196616 | tf_op jit(solution)/shard_map/ppermute | solution.py:16
  119.9 4.4 %collective-permute-done.17 = bf16[4,8,2048]{2,1,0:T(8,128)(2,1)S(1)} collective-permute-done((bf16[4,8,2048]{2,1,0:T(8,128)(2,1)S(1)}, bf16[4,8,2048]{2,1,0:T(8,128)(2,1)S(1)}, u32[]{:S(2)}, u32[]{:S(2)}) %collective-permute-start.17) | collective-permute-done | bytes 131104 | tf_op jit(solution)/shard_map/ppermute | solution.py:16
  124.4 2.2 collective-permute-start.21
  126.6 2.1 collective-permute-start.20
  128.8 1.4 collective-permute-start.19
  131.0 4.0 %collective-permute-done.20 = bf16[8,4096]{1,0:T(8,128)(2,1)S(1)} collective-permute-done((bf16[8,4096]{1,0:T(8,128)(2,1)S(1)}, bf16[8,4096]{1,0:T(8,128)(2,1)S(1)}, u32[]{:S(2)}, u32[]{:S(2)}) %collective-permute-start.20) | collective-permute-done | bytes 65568 | tf_op jit(solution)/shard_map/ppermute | solution.py:16
  135.1 1.3 collective-permute-start.27
  136.4 1.9 collective-permute-start.28
  138.3 2.5 collective-permute-start.29
  143.1 1.3 collective-permute-start.24
  144.4 1.3 collective-permute-start.23
  146.1 1.2 collective-permute-done.29
  147.4 1.4 collective-permute-start.32
  148.8 4.2 %collective-permute-start.31 = (bf16[4,16,2048]{2,1,0:T(8,128)(2,1)S(1)}, bf16[4,16,2048]{2,1,0:T(8,128)(2,1)S(1)}, u32[]{:S(2)}, u32[]{:S(2)}) collective-permute-start(bf16[4,16,2048]{2,1,0:T(8,128)(2,1)S(1)} %get-tuple-element.46), channel_id=1, source_target_pairs={{0,7},{1,2},{2,1},{3,4},{4,3},{5,6},{6,5},{7,0},{8,15},{9,10},{10,... | collective-permute-start | bytes 786440 | tf_op jit(solution)/shard_map/ppermute | solution.py:28
  154.9 2.2 collective-permute-done.31
  158.8 3.6 %collective-permute-done.30 = bf16[4,16,2048]{2,1,0:T(8,128)(2,1)S(1)} collective-permute-done((bf16[4,16,2048]{2,1,0:T(8,128)(2,1)S(1)}, bf16[4,16,2048]{2,1,0:T(8,128)(2,1)S(1)}, u32[]{:S(2)}, u32[]{:S(2)}) %collective-permute-start.30) | collective-permute-done | bytes 262176 | tf_op jit(solution)/shard_map/ppermute | solution.py:16
  162.4 1.1 collective-permute-start.33
  165.2 5.6 %collective-permute-done.33 = bf16[4,16,4096]{2,1,0:T(8,128)(2,1)S(1)} collective-permute-done((bf16[4,16,4096]{2,1,0:T(8,128)(2,1)S(1)}, bf16[4,16,4096]{2,1,0:T(8,128)(2,1)S(1)}, u32[]{:S(2)}, u32[]{:S(2)}) %collective-permute-start.33) | collective-permute-done | bytes 524320 | tf_op jit(solution)/shard_map/ppermute | solution.py:16
  171.6 2.3 convolution_bitcast_fusion.2
  173.9 2.4 fusion.12
  176.4 2.4 collective-permute-start.35
  178.8 11.0 %all_gather.22.refs_0_ = bf16[4,896,128]{2,1,0:T(8,128)(2,1)S(1)} all-gather(bf16[1,896,128]{2,1,0:T(8,128)(2,1)S(1)} %pad_maximum_fusion.7), channel_id=1, replica_groups=mesh['x_hi'=2,'y'=4,'core'=2,'x_lo'=2,'z'=8] {'y'}, dimensions={0}, use_global_device_ids=true | all-gather | bytes 1146880 | tf_op jit(solution)/shard_map/all_gather | solution.py:247
  189.8 10.4 %collective-permute-start.34 = (bf16[4,896,128]{2,1,0:T(8,128)(2,1)S(1)}, bf16[4,896,128]{2,1,0:T(8,128)(2,1)S(1)}, u32[]{:S(2)}, u32[]{:S(2)}) collective-permute-start(bf16[4,896,128]{2,1,0:T(8,128)(2,1)S(1)} %all_gather.22.refs_0_), channel_id=1, source_target_pairs={{0,16},{16,0},{1,17},{17,1},{2,18},{18,2},{3,19},{19,3},{4,20},{20... | collective-permute-start | bytes 2752520 | tf_op jit(solution)/shard_map/ppermute | solution.py:16
  200.2 12.8 %all-gather.1 = bf16[3584,128]{1,0:T(8,128)(2,1)S(1)} all-gather(bf16[896,128]{1,0:T(8,128)(2,1)S(1)} %collective-permute-done.35), channel_id=3, replica_groups=mesh['x_hi'=2,'y'=4,'core'=2,'x_lo'=2,'z'=8] {'y'}, dimensions={0}, use_global_device_ids=true | all-gather | bytes 1146880 | tf_op jit(solution)/shard_map/all_gather | solution.py:247
  212.9 2.0 collective-permute-start.36
  214.9 1.2 pad_maximum_fusion.1
  216.2 1.1 dynamic-slice_bitcast_fusion
  218.0 1.5 collective-permute-done.26
  219.5 1.4 pad_maximum_fusion.2
  221.9 1.2 copy-done.4
  223.1 4.2 %shard_map.133 = (f32[896,256]{1,0:T(8,128)S(1)}, f32[8,128]{1,0:T(8,128)S(1)}) custom-call(s32[16]{0:T(128)S(1)} %stack.157.index_ref, f32[1,1]{1,0:T(1,128)} %bitcast.159.beta_ref, bf16[16,128,256]{2,1,0:T(8,128)(2,1)S(1)} %bitcast.160, bf16[4,896,128]{2,1,0:T(8,128)(2,1)S(1)} %all_gather.22.refs_0_, bf16[4,896,128]{2,1,0:T(8,128)(2,1)S(1)} %copy-done.4, ...), custom_call_target="tpu_custom_call" | custom-call | flops 1073741824 | bytes 7340032 | tf_op jit(solution)/shard_map/pallas_call | solution.py:252
  227.3 11.5 %all_to_all.10 = f32[8,8,128]{2,1,0:T(8,128)S(1)} all-to-all(f32[8,8,128]{2,1,0:T(8,128)S(1)} %broadcast_in_dim.28), channel_id=1, replica_groups=mesh['x_hi'=2,'y'=4,'core'=2,'x_lo'=2,'z'=8] {'z'}, dimensions={0} | all-to-all | bytes 65536 | tf_op jit(solution)/shard_map/all_to_all | solution.py:277
  238.7 12.0 %all_to_all.11.refs_0_ = f32[32,8,128]{2,1,0:T(8,128)S(1)} all-to-all(f32[32,8,128]{2,1,0:T(8,128)S(1)} %broadcast_in_dim.29), channel_id=1, replica_groups=mesh['x_hi'=2,'y'=4,'core'=2,'x_lo'=2,'z'=8] {'x_hi','y','core','x_lo'}, dimensions={0} | all-to-all | bytes 262144 | tf_op jit(solution)/shard_map/all_to_all | solution.py:277
  250.7 1.9 shard_map.134
  (108 shorter events, 22.5 us)
Async XLA Ops:
  7.2 48.1 %all-gather.5.cloned.1.call-start = ((), (), s32[]{:S(2)}) async-start(), calls=%async_computation.2 | async-start | bytes 2293760 | tf_op jit(solution)/shard_map/all_gather | solution.py:173
  7.9 70.6 %all-gather.7.cloned.1.call-start = ((), (), s32[]{:S(2)}) async-start(), calls=%async_computation.3 | async-start | bytes 2293760 | tf_op jit(solution)/shard_map/all_gather | solution.py:174
  7.9 11.9 %collective-permute-start.2 = (bf16[8,4096]{1,0:T(8,128)(2,1)}, bf16[8,4096]{1,0:T(8,128)(2,1)S(1)}, u32[]{:S(2)}, u32[]{:S(2)}) collective-permute-start(bf16[8,4096]{1,0:T(8,128)(2,1)} %param.11), channel_id=1, source_target_pairs={{0,6},{1,7},{2,4},{3,5},{4,2},{5,3},{6,0},{7,1},{8,14},{9,15},{10,... | collective-permute-start | bytes 196616 | tf_op jit(solution)/shard_map/ppermute | solution.py:16
  14.9 7.7 %collective-permute-start.1 = (bf16[8,4096]{1,0:T(8,128)(2,1)}, bf16[8,4096]{1,0:T(8,128)(2,1)S(1)}, u32[]{:S(2)}, u32[]{:S(2)}) collective-permute-start(bf16[8,4096]{1,0:T(8,128)(2,1)} %param.11), channel_id=1, source_target_pairs={{0,4},{1,5},{2,6},{3,7},{4,0},{5,1},{6,2},{7,3},{8,12},{9,13},{10,... | collective-permute-start | bytes 196616 | tf_op jit(solution)/shard_map/ppermute | solution.py:16
  15.9 8.1 %collective-permute-start = (bf16[8,4096]{1,0:T(8,128)(2,1)}, bf16[8,4096]{1,0:T(8,128)(2,1)S(1)}, u32[]{:S(2)}, u32[]{:S(2)}) collective-permute-start(bf16[8,4096]{1,0:T(8,128)(2,1)} %param.11), channel_id=1, source_target_pairs={{0,2},{1,3},{2,0},{3,1},{4,6},{5,7},{6,4},{7,5},{8,10},{9,11},{10,... | collective-permute-start | bytes 196616 | tf_op jit(solution)/shard_map/ppermute | solution.py:16
  17.1 12.5 %collective-permute-start.3 = (bf16[896,256]{1,0:T(8,128)(2,1)}, bf16[896,256]{1,0:T(8,128)(2,1)S(1)}, u32[]{:S(2)}, u32[]{:S(2)}) collective-permute-start(bf16[896,256]{1,0:T(8,128)(2,1)} %bitcast.162), channel_id=1, source_target_pairs={{0,128},{128,0},{1,129},{129,1},{2,130},{130,2},{3,131},{131,3},{4... | collective-permute-start | bytes 1376264 | tf_op jit(solution)/shard_map/ppermute | solution.py:16
  29.6 9.3 %copy-start.11 = (bf16[896,256]{1,0:T(8,128)(2,1)}, bf16[896,256]{1,0:T(8,128)(2,1)S(1)}, u32[]{:S(2)}) copy-start(bf16[896,256]{1,0:T(8,128)(2,1)S(1)} %collective-permute-done.3) | copy-start | bytes 1376260
  29.6 5.6 %collective-permute-start.5 = (bf16[4,8,2048]{2,1,0:T(8,128)(2,1)S(1)}, bf16[4,8,2048]{2,1,0:T(8,128)(2,1)S(1)}, u32[]{:S(2)}, u32[]{:S(2)}) collective-permute-start(bf16[4,8,2048]{2,1,0:T(8,128)(2,1)S(1)} %get-tuple-element.58), channel_id=1, source_target_pairs={{0,7},{1,2},{2,1},{3,4},{4,3},{5,6},{6,5},{7,0},{8,15},{9,10},{10,... | collective-permute-start | bytes 393224 | tf_op jit(solution)/shard_map/ppermute | solution.py:28
  33.1 5.8 %collective-permute-start.6 = (bf16[4,8,4096]{2,1,0:T(8,128)(2,1)S(1)}, bf16[4,8,4096]{2,1,0:T(8,128)(2,1)S(1)}, u32[]{:S(2)}, u32[]{:S(2)}) collective-permute-start(bf16[4,8,4096]{2,1,0:T(8,128)(2,1)S(1)} %pad_maximum_fusion.5), channel_id=1, source_target_pairs={{0,8},{8,0},{1,9},{9,1},{2,10},{10,2},{3,11},{11,3},{4,12},{12,4},... | collective-permute-start | bytes 786440 | tf_op jit(solution)/shard_map/ppermute | solution.py:16
  34.3 4.2 %collective-permute-start.4 = (bf16[4,8,2048]{2,1,0:T(8,128)(2,1)S(1)}, bf16[4,8,2048]{2,1,0:T(8,128)(2,1)S(1)}, u32[]{:S(2)}, u32[]{:S(2)}) collective-permute-start(bf16[4,8,2048]{2,1,0:T(8,128)(2,1)S(1)} %get-tuple-element.57), channel_id=1, source_target_pairs={{0,1},{1,0},{2,3},{3,2},{4,5},{5,4},{6,7},{7,6},{8,9},{9,8},{10,11... | collective-permute-start | bytes 393224 | tf_op jit(solution)/shard_map/ppermute | solution.py:16
  38.5 6.2 %collective-permute-start.7 = (bf16[4,8,4096]{2,1,0:T(8,128)(2,1)S(1)}, bf16[4,8,4096]{2,1,0:T(8,128)(2,1)}, u32[]{:S(2)}, u32[]{:S(2)}) collective-permute-start(bf16[4,8,4096]{2,1,0:T(8,128)(2,1)S(1)} %pad_maximum_fusion.6), channel_id=1, source_target_pairs={{0,8},{8,0},{1,9},{9,1},{2,10},{10,2},{3,11},{11,3},{4,12},{12,4},... | collective-permute-start | bytes 786440 | tf_op jit(solution)/shard_map/ppermute | solution.py:16
  45.7 17.6 %collective-permute-start.14 = (bf16[128,4096]{1,0:T(8,128)(2,1)S(1)}, bf16[128,4096]{1,0:T(8,128)(2,1)S(1)}, u32[]{:S(2)}, u32[]{:S(2)}) collective-permute-start(bf16[128,4096]{1,0:T(8,128)(2,1)S(1)} %maximum_bitcast_fusion.refs_1_), channel_id=1, source_target_pairs={{0,16},{16,0},{1,17},{17,1},{2,18},{18,2},{3,19},{19,3},{4,20},{20... | collective-permute-start | bytes 3145736 | tf_op jit(solution)/shard_map/ppermute | solution.py:16
  59.1 25.1 %collective-permute-start.8 = (bf16[2,4,8,4096]{3,2,1,0:T(8,128)(2,1)}, bf16[2,4,8,4096]{3,2,1,0:T(8,128)(2,1)}, u32[]{:S(2)}, u32[]{:S(2)}) collective-permute-start(bf16[2,4,8,4096]{3,2,1,0:T(8,128)(2,1)} %bitcast.29), channel_id=1, source_target_pairs={{0,8},{8,0},{1,9},{9,1},{2,10},{10,2},{3,11},{11,3},{4,12},{12,4},... | collective-permute-start | bytes 1572872 | tf_op jit(solution)/shard_map/ppermute | solution.py:16
  59.5 3.8 %copy-start.1 = (bf16[4,896,256]{2,1,0:T(8,128)(2,1)S(1)}, bf16[4,896,256]{2,1,0:T(8,128)(2,1)}, u32[]{:S(2)}) copy-start(bf16[4,896,256]{2,1,0:T(8,128)(2,1)} %all-gather.5.cloned.1.call-done) | copy-start | bytes 5505028
  60.6 28.0 %collective-permute-start.22 = (bf16[128,2048]{1,0:T(8,128)(2,1)}, bf16[128,2048]{1,0:T(8,128)(2,1)}, u32[]{:S(2)}, u32[]{:S(2)}) collective-permute-start(bf16[128,2048]{1,0:T(8,128)(2,1)} %get-tuple-element.40), channel_id=1, source_target_pairs={{0,128},{128,0},{1,129},{129,1},{2,130},{130,2},{3,131},{131,3},{4... | collective-permute-start | bytes 1572872 | tf_op jit(solution)/shard_map/ppermute | solution.py:16
  78.5 1.5 copy-start.2
  80.0 4.2 %copy-start.9 = (bf16[64,4096]{1,0:T(8,128)(2,1)S(1)}, bf16[64,4096]{1,0:T(8,128)(2,1)}, u32[]{:S(2)}) copy-start(bf16[64,4096]{1,0:T(8,128)(2,1)} %get-tuple-element.42) | copy-start | bytes 1572868
  83.5 6.2 %copy-start.6 = (f32[2,448,128]{2,1,0:T(8,128)}, f32[2,448,128]{2,1,0:T(8,128)S(1)}, u32[]{:S(2)}) copy-start(f32[2,448,128]{2,1,0:T(8,128)S(1)} %get-tuple-element.20.own_ref) | copy-start | bytes 1376260
  83.5 5.0 %copy-start.10 = (bf16[1,128,2048]{2,1,0:T(8,128)(2,1)S(1)}, bf16[1,128,2048]{2,1,0:T(8,128)(2,1)}, u32[]{:S(2)}) copy-start(bf16[1,128,2048]{2,1,0:T(8,128)(2,1)} %get-tuple-element.39) | copy-start | bytes 1572868
  83.5 9.4 %collective-permute-start.15 = (f32[2,448,128]{2,1,0:T(8,128)}, f32[2,448,128]{2,1,0:T(8,128)S(1)}, u32[]{:S(2)}, u32[]{:S(2)}) collective-permute-start(f32[2,448,128]{2,1,0:T(8,128)} %get-tuple-element.21), channel_id=1, source_target_pairs={{0,16},{16,0},{1,17},{17,1},{2,18},{18,2},{3,19},{19,3},{4,20},{20... | collective-permute-start | bytes 1376264 | tf_op jit(solution)/shard_map/ppermute | solution.py:16
  85.4 6.9 %collective-permute-start.10 = (bf16[4,8,2048]{2,1,0:T(8,128)(2,1)S(1)}, bf16[4,8,2048]{2,1,0:T(8,128)(2,1)S(1)}, u32[]{:S(2)}, u32[]{:S(2)}) collective-permute-start(bf16[4,8,2048]{2,1,0:T(8,128)(2,1)S(1)} %get-tuple-element.51), channel_id=1, source_target_pairs={{0,7},{1,2},{2,1},{3,4},{4,3},{5,6},{6,5},{7,0},{8,15},{9,10},{10,... | collective-permute-start | bytes 393224 | tf_op jit(solution)/shard_map/ppermute | solution.py:28
  89.7 8.8 %collective-permute-start.9 = (bf16[4,8,2048]{2,1,0:T(8,128)(2,1)S(1)}, bf16[4,8,2048]{2,1,0:T(8,128)(2,1)S(1)}, u32[]{:S(2)}, u32[]{:S(2)}) collective-permute-start(bf16[4,8,2048]{2,1,0:T(8,128)(2,1)S(1)} %get-tuple-element.50), channel_id=1, source_target_pairs={{0,1},{1,0},{2,3},{3,2},{4,5},{5,4},{6,7},{7,6},{8,9},{9,8},{10,11... | collective-permute-start | bytes 393224 | tf_op jit(solution)/shard_map/ppermute | solution.py:16
  92.9 1.0 copy-start.7
  97.2 12.9 %collective-permute-start.16 = (bf16[2,4,8,4096]{3,2,1,0:T(8,128)(2,1)S(1)}, bf16[2,4,8,4096]{3,2,1,0:T(8,128)(2,1)S(1)}, u32[]{:S(2)}, u32[]{:S(2)}) collective-permute-start(bf16[2,4,8,4096]{3,2,1,0:T(8,128)(2,1)S(1)} %bitcast.174), channel_id=1, source_target_pairs={{0,8},{8,0},{1,9},{9,1},{2,10},{10,2},{3,11},{11,3},{4,12},{12,4},... | collective-permute-start | bytes 1572872 | tf_op jit(solution)/shard_map/ppermute | solution.py:16
  110.1 20.1 %copy-start.12 = (bf16[8,4096]{1,0:T(8,128)(2,1)S(1)}, bf16[8,4096]{1,0:T(8,128)(2,1)}, u32[]{:S(2)}) copy-start(bf16[8,4096]{1,0:T(8,128)(2,1)} %param.12) | copy-start | bytes 196612
  110.2 9.0 %collective-permute-start.18 = (bf16[4,8,2048]{2,1,0:T(8,128)(2,1)S(1)}, bf16[4,8,2048]{2,1,0:T(8,128)(2,1)S(1)}, u32[]{:S(2)}, u32[]{:S(2)}) collective-permute-start(bf16[4,8,2048]{2,1,0:T(8,128)(2,1)S(1)} %get-tuple-element.56), channel_id=1, source_target_pairs={{0,7},{1,2},{2,1},{3,4},{4,3},{5,6},{6,5},{7,0},{8,15},{9,10},{10,... | collective-permute-start | bytes 393224 | tf_op jit(solution)/shard_map/ppermute | solution.py:28
  113.0 15.8 %collective-permute-start.13 = (bf16[8,4096]{1,0:T(8,128)(2,1)}, bf16[8,4096]{1,0:T(8,128)(2,1)S(1)}, u32[]{:S(2)}, u32[]{:S(2)}) collective-permute-start(bf16[8,4096]{1,0:T(8,128)(2,1)} %get-tuple-element.48), channel_id=1, source_target_pairs={{0,6},{1,7},{2,4},{3,5},{4,2},{5,3},{6,0},{7,1},{8,14},{9,15},{10,... | collective-permute-start | bytes 196616 | tf_op jit(solution)/shard_map/ppermute | solution.py:16
  113.6 16.5 %collective-permute-start.12 = (bf16[8,4096]{1,0:T(8,128)(2,1)}, bf16[8,4096]{1,0:T(8,128)(2,1)S(1)}, u32[]{:S(2)}, u32[]{:S(2)}) collective-permute-start(bf16[8,4096]{1,0:T(8,128)(2,1)} %get-tuple-element.49), channel_id=1, source_target_pairs={{0,4},{1,5},{2,6},{3,7},{4,0},{5,1},{6,2},{7,3},{8,12},{9,13},{10,... | collective-permute-start | bytes 196616 | tf_op jit(solution)/shard_map/ppermute | solution.py:16
  115.6 14.5 %collective-permute-start.11 = (bf16[8,4096]{1,0:T(8,128)(2,1)S(1)}, bf16[8,4096]{1,0:T(8,128)(2,1)}, u32[]{:S(2)}, u32[]{:S(2)}) collective-permute-start(bf16[8,4096]{1,0:T(8,128)(2,1)S(1)} %get-tuple-element.47), channel_id=1, source_target_pairs={{0,2},{1,3},{2,0},{3,1},{4,6},{5,7},{6,4},{7,5},{8,10},{9,11},{10,... | collective-permute-start | bytes 196616 | tf_op jit(solution)/shard_map/ppermute | solution.py:16
  118.6 5.7 %collective-permute-start.17 = (bf16[4,8,2048]{2,1,0:T(8,128)(2,1)S(1)}, bf16[4,8,2048]{2,1,0:T(8,128)(2,1)S(1)}, u32[]{:S(2)}, u32[]{:S(2)}) collective-permute-start(bf16[4,8,2048]{2,1,0:T(8,128)(2,1)S(1)} %get-tuple-element.55), channel_id=1, source_target_pairs={{0,1},{1,0},{2,3},{3,2},{4,5},{5,4},{6,7},{7,6},{8,9},{9,8},{10,11... | collective-permute-start | bytes 393224 | tf_op jit(solution)/shard_map/ppermute | solution.py:16
  124.4 6.7 %collective-permute-start.21 = (bf16[8,4096]{1,0:T(8,128)(2,1)S(1)}, bf16[8,4096]{1,0:T(8,128)(2,1)S(1)}, u32[]{:S(2)}, u32[]{:S(2)}) collective-permute-start(bf16[8,4096]{1,0:T(8,128)(2,1)S(1)} %get-tuple-element.53), channel_id=1, source_target_pairs={{0,6},{1,7},{2,4},{3,5},{4,2},{5,3},{6,0},{7,1},{8,14},{9,15},{10,... | collective-permute-start | bytes 196616 | tf_op jit(solution)/shard_map/ppermute | solution.py:16
  126.6 8.4 %collective-permute-start.20 = (bf16[8,4096]{1,0:T(8,128)(2,1)S(1)}, bf16[8,4096]{1,0:T(8,128)(2,1)S(1)}, u32[]{:S(2)}, u32[]{:S(2)}) collective-permute-start(bf16[8,4096]{1,0:T(8,128)(2,1)S(1)} %get-tuple-element.54), channel_id=1, source_target_pairs={{0,4},{1,5},{2,6},{3,7},{4,0},{5,1},{6,2},{7,3},{8,12},{9,13},{10,... | collective-permute-start | bytes 196616 | tf_op jit(solution)/shard_map/ppermute | solution.py:16
  128.8 6.3 %collective-permute-start.19 = (bf16[8,4096]{1,0:T(8,128)(2,1)S(1)}, bf16[8,4096]{1,0:T(8,128)(2,1)S(1)}, u32[]{:S(2)}, u32[]{:S(2)}) collective-permute-start(bf16[8,4096]{1,0:T(8,128)(2,1)S(1)} %get-tuple-element.52), channel_id=1, source_target_pairs={{0,2},{1,3},{2,0},{3,1},{4,6},{5,7},{6,4},{7,5},{8,10},{9,11},{10,... | collective-permute-start | bytes 196616 | tf_op jit(solution)/shard_map/ppermute | solution.py:16
  135.1 9.3 %collective-permute-start.27 = (bf16[16,4096]{1,0:T(8,128)(2,1)S(1)}, bf16[16,4096]{1,0:T(8,128)(2,1)S(1)}, u32[]{:S(2)}, u32[]{:S(2)}) collective-permute-start(bf16[16,4096]{1,0:T(8,128)(2,1)S(1)} %pad_maximum_fusion.9), channel_id=1, source_target_pairs={{0,2},{1,3},{2,0},{3,1},{4,6},{5,7},{6,4},{7,5},{8,10},{9,11},{10,... | collective-permute-start | bytes 393224 | tf_op jit(solution)/shard_map/ppermute | solution.py:16
  136.4 9.7 %collective-permute-start.28 = (bf16[16,4096]{1,0:T(8,128)(2,1)S(1)}, bf16[16,4096]{1,0:T(8,128)(2,1)S(1)}, u32[]{:S(2)}, u32[]{:S(2)}) collective-permute-start(bf16[16,4096]{1,0:T(8,128)(2,1)S(1)} %pad_maximum_fusion.9), channel_id=1, source_target_pairs={{0,4},{1,5},{2,6},{3,7},{4,0},{5,1},{6,2},{7,3},{8,12},{9,13},{10,... | collective-permute-start | bytes 393224 | tf_op jit(solution)/shard_map/ppermute | solution.py:16
  138.3 8.9 %collective-permute-start.29 = (bf16[16,4096]{1,0:T(8,128)(2,1)S(1)}, bf16[16,4096]{1,0:T(8,128)(2,1)S(1)}, u32[]{:S(2)}, u32[]{:S(2)}) collective-permute-start(bf16[16,4096]{1,0:T(8,128)(2,1)S(1)} %pad_maximum_fusion.9), channel_id=1, source_target_pairs={{0,6},{1,7},{2,4},{3,5},{4,2},{5,3},{6,0},{7,1},{8,14},{9,15},{10,... | collective-permute-start | bytes 393224 | tf_op jit(solution)/shard_map/ppermute | solution.py:16
  142.4 72.5 %collective-permute-start.25 = (bf16[2,128,512]{2,1,0:T(8,128)(2,1)}, bf16[2,128,512]{2,1,0:T(8,128)(2,1)}, u32[]{:S(2)}, u32[]{:S(2)}) collective-permute-start(bf16[2,128,512]{2,1,0:T(8,128)(2,1)} %get-tuple-element.36), channel_id=1, source_target_pairs={{0,96},{32,64},{64,32},{96,0},{1,97},{33,65},{65,33},{97,1},{2,98}... | collective-permute-start | bytes 786440 | tf_op jit(solution)/shard_map/ppermute | solution.py:16
  143.1 71.8 %collective-permute-start.24 = (bf16[2,128,512]{2,1,0:T(8,128)(2,1)}, bf16[2,128,512]{2,1,0:T(8,128)(2,1)}, u32[]{:S(2)}, u32[]{:S(2)}) collective-permute-start(bf16[2,128,512]{2,1,0:T(8,128)(2,1)} %get-tuple-element.37), channel_id=1, source_target_pairs={{0,64},{32,96},{64,0},{96,32},{1,65},{33,97},{65,1},{97,33},{2,66}... | collective-permute-start | bytes 786440 | tf_op jit(solution)/shard_map/ppermute | solution.py:16
  144.4 70.5 %collective-permute-start.23 = (bf16[2,128,512]{2,1,0:T(8,128)(2,1)}, bf16[2,128,512]{2,1,0:T(8,128)(2,1)}, u32[]{:S(2)}, u32[]{:S(2)}) collective-permute-start(bf16[2,128,512]{2,1,0:T(8,128)(2,1)} %get-tuple-element.38), channel_id=1, source_target_pairs={{0,32},{32,0},{64,96},{96,64},{1,33},{33,1},{65,97},{97,65},{2,34}... | collective-permute-start | bytes 786440 | tf_op jit(solution)/shard_map/ppermute | solution.py:16
  147.4 17.0 %collective-permute-start.32 = (bf16[4,16,4096]{2,1,0:T(8,128)(2,1)S(1)}, bf16[4,16,4096]{2,1,0:T(8,128)(2,1)S(1)}, u32[]{:S(2)}, u32[]{:S(2)}) collective-permute-start(bf16[4,16,4096]{2,1,0:T(8,128)(2,1)S(1)} %pad_maximum_fusion.3), channel_id=1, source_target_pairs={{0,8},{8,0},{1,9},{9,1},{2,10},{10,2},{3,11},{11,3},{4,12},{12,4},... | collective-permute-start | bytes 1572872 | tf_op jit(solution)/shard_map/ppermute | solution.py:16
  148.8 8.3 %collective-permute-start.31 = (bf16[4,16,2048]{2,1,0:T(8,128)(2,1)S(1)}, bf16[4,16,2048]{2,1,0:T(8,128)(2,1)S(1)}, u32[]{:S(2)}, u32[]{:S(2)}) collective-permute-start(bf16[4,16,2048]{2,1,0:T(8,128)(2,1)S(1)} %get-tuple-element.46), channel_id=1, source_target_pairs={{0,7},{1,2},{2,1},{3,4},{4,3},{5,6},{6,5},{7,0},{8,15},{9,10},{10,... | collective-permute-start | bytes 786440 | tf_op jit(solution)/shard_map/ppermute | solution.py:28
  157.1 5.2 %collective-permute-start.30 = (bf16[4,16,2048]{2,1,0:T(8,128)(2,1)S(1)}, bf16[4,16,2048]{2,1,0:T(8,128)(2,1)S(1)}, u32[]{:S(2)}, u32[]{:S(2)}) collective-permute-start(bf16[4,16,2048]{2,1,0:T(8,128)(2,1)S(1)} %get-tuple-element.45), channel_id=1, source_target_pairs={{0,1},{1,0},{2,3},{3,2},{4,5},{5,4},{6,7},{7,6},{8,9},{9,8},{10,11... | collective-permute-start | bytes 786440 | tf_op jit(solution)/shard_map/ppermute | solution.py:16
  158.8 12.8 %copy-start.8 = (bf16[448,4096]{1,0:T(8,128)(2,1)S(1)}, bf16[448,4096]{1,0:T(8,128)(2,1)}, u32[]{:S(2)}) copy-start(bf16[448,4096]{1,0:T(8,128)(2,1)} %param.14) | copy-start | bytes 11010052
  162.4 8.3 %collective-permute-start.33 = (bf16[4,16,4096]{2,1,0:T(8,128)(2,1)S(1)}, bf16[4,16,4096]{2,1,0:T(8,128)(2,1)S(1)}, u32[]{:S(2)}, u32[]{:S(2)}) collective-permute-start(bf16[4,16,4096]{2,1,0:T(8,128)(2,1)S(1)} %pad_maximum_fusion.4), channel_id=1, source_target_pairs={{0,8},{8,0},{1,9},{9,1},{2,10},{10,2},{3,11},{11,3},{4,12},{12,4},... | collective-permute-start | bytes 1572872 | tf_op jit(solution)/shard_map/ppermute | solution.py:16
  176.4 23.8 %collective-permute-start.35 = (bf16[896,128]{1,0:T(8,128)(2,1)S(1)}, bf16[896,128]{1,0:T(8,128)(2,1)S(1)}, u32[]{:S(2)}, u32[]{:S(2)}) collective-permute-start(bf16[896,128]{1,0:T(8,128)(2,1)S(1)} %pad_maximum_fusion.8), channel_id=1, source_target_pairs={{0,128},{128,0},{1,129},{129,1},{2,130},{130,2},{3,131},{131,3},{4... | collective-permute-start | bytes 688136 | tf_op jit(solution)/shard_map/ppermute | solution.py:16
  189.8 31.2 %collective-permute-start.34 = (bf16[4,896,128]{2,1,0:T(8,128)(2,1)S(1)}, bf16[4,896,128]{2,1,0:T(8,128)(2,1)S(1)}, u32[]{:S(2)}, u32[]{:S(2)}) collective-permute-start(bf16[4,896,128]{2,1,0:T(8,128)(2,1)S(1)} %all_gather.22.refs_0_), channel_id=1, source_target_pairs={{0,16},{16,0},{1,17},{17,1},{2,18},{18,2},{3,19},{19,3},{4,20},{20... | collective-permute-start | bytes 2752520 | tf_op jit(solution)/shard_map/ppermute | solution.py:16
  212.9 9.0 %collective-permute-start.36 = (bf16[4,896,128]{2,1,0:T(8,128)(2,1)S(1)}, bf16[4,896,128]{2,1,0:T(8,128)(2,1)}, u32[]{:S(2)}, u32[]{:S(2)}) collective-permute-start(bf16[4,896,128]{2,1,0:T(8,128)(2,1)S(1)} %bitcast.165), channel_id=1, source_target_pairs={{0,16},{16,0},{1,17},{17,1},{2,18},{18,2},{3,19},{19,3},{4,20},{20... | collective-permute-start | bytes 2752520 | tf_op jit(solution)/shard_map/ppermute | solution.py:16
  217.2 2.3 collective-permute-start.26
  219.5 2.4 copy-start
  219.5 2.4 copy-start.5
  221.0 0.9 copy-start.3
  221.9 1.2 copy-start.4
Sparse Core Ops, SparseCore 0:
  9.8 35.0 all-gather.4
  47.3 31.2 all-gather.6
where the time goes:
time: 260 us; the launch traced here: 259 us
  starting transfers between devices  74.5 us (29%)
  waiting for transfers between devices  68.3 us (26%)
  blocking collectives  47.2 us (18%)
  local copies, waits for them, and re-layouts  16.4 us (6%)
  matrix products  15.6 us (6%)
  between operations  15.1 us (6%)
  Pallas kernels  12.6 us (5%)
  other arithmetic  9.83 us (4%)
    ppermute x33, starting transfers between devices, swap(): return lax.ppermute(value, axis, [(i, i ^ step) for i in range(size)])  62.3 us
    ppermute x33, waiting for transfers between devices, swap(): return lax.ppermute(value, axis, [(i, i ^ step) for i in range(size)])  49.6 us
    all_gather x2, blocking collectives, per_device(): piece = lax.all_gather(piece, 'y')  23.8 us
    all_to_all x2, blocking collectives, per_device(): lax.all_to_all(jnp.broadcast_to(sums[None], (size, 8, 128)), axes, 0, 0,...  23.5 us
    dot_general x5, matrix products, dot(): return lax.dot_general(a, b, (dims, ((), ())), preferred_element_type=F32)  15.6 us
    all_gather x1, waiting for transfers between devices, per_device(): far = lax.all_gather(current_far, 'y')  12.5 us
    ppermute x4, starting transfers between devices, neighbour(): lax.ppermute(value, 'z', [(i, (i + 1) % 8 if i % 2 else (i - 1) % 8) for...  12.2 us
    unnamed x31, local copies, waits for them, and re-layouts  8.09 us
  transfers between devices with their start and end apart: 39, of which 17 were waited for; matrix products, arithmetic and copies ran while one was open for 14% of the time, Pallas kernels for 3%

commit v1 on v0

--- a/solution.py
+++ b/solution.py
@@ -69,17 +69,28 @@
     return lax.dot_general(a, b, (dims, ((), ())), preferred_element_type=F32)
 
 
-def tangent_kernel(first, index_ref, rows_ref, other_ref, pieces_ref, *refs):
-    before, outs = refs[:first], refs[first:]
+def tangent_kernel(first, index_ref, rows_ref, other_ref, *refs):
+    if first:
+        pieces, before_ref, outs = refs[:4], refs[4], refs[5:]
+        at = 4
+    else:
+        pieces_ref, before_ref, outs = refs[0], None, refs[1:]
+        at = 0
     for k in range(2):
-        total = before[0][k] if before else 0.0
-        for at in range(4):
-            start = pl.multiple_of(index_ref[4 * first + at] * 256, 256)
+        if first:
+            blocks = [pieces[2 * k + i // 2][i % 2] for i in range(4)]
+        else:
+            blocks = [pieces_ref[i, k] for i in range(4)]
+            at = 0
+        total = before_ref[k] if first else 0.0
+        for block in blocks:
+            start = pl.multiple_of(index_ref[at] * 256, 256)
             rows = jnp.concatenate([ref[:, pl.ds(start, 256)] for ref in (rows_ref, other_ref)], 0)
-            total = total + dot(pieces_ref[at, k], rows, ((1,), (1,)))
+            total = total + dot(block, rows, ((1,), (1,)))
+            at += 1
         width = outs[0].shape[2]
-        for at, out in enumerate(outs):
-            out[k] = total[:, at * width : (at + 1) * width]
+        for place, out in enumerate(outs):
+            out[k] = total[:, place * width : (place + 1) * width]
 
 
 def act_kernel(projected_ref, own_ref, other_ref, tangent_ref, act_ref):
@@ -93,12 +104,16 @@
 
 
 def tangent_call(first, index, rows, pieces, before, out_shape):
-    hidden = pieces.shape[2]
+    hidden, depth = pieces[0].shape[-2:]
     chunk = hidden // STEPS
 
     def spec(size):
         return pl.BlockSpec((2, chunk, size), lambda i, index: (0, i, 0))
 
+    if first:
+        piece_specs = [spec(depth)] * 4
+    else:
+        piece_specs = [pl.BlockSpec((4, 2, chunk, depth), lambda i, index: (0, 0, i, 0))]
     return pl.pallas_call(
         lambda *refs: tangent_kernel(first, *refs),
         out_shape=out_shape,
@@ -106,17 +121,17 @@
             num_scalar_prefetch=1,
             grid=(STEPS,),
             in_specs=[pl.BlockSpec(r.shape, lambda i, index: (0, 0)) for r in rows]
-            + [pl.BlockSpec((4, 2, chunk, pieces.shape[3]), lambda i, index: (0, 0, i, 0))]
+            + piece_specs
             + [spec(b.shape[2]) for b in before],
             out_specs=[spec(o.shape[2]) for o in out_shape],
         ),
         compiler_params=pltpu.CompilerParams(vmem_limit_bytes=32 * 2**20),
         cost_estimate=pl.CostEstimate(
-            flops=8 * hidden * pieces.shape[3] * rows[0].shape[0] * 4,
-            bytes_accessed=pieces.size * 2,
+            flops=8 * hidden * depth * rows[0].shape[0] * 4,
+            bytes_accessed=16 * hidden * depth,
             transcendentals=0,
         ),
-    )(index, *rows, pieces, *before)
+    )(index, *rows, *pieces, *before)
 
 
 def curvature_kernel(index_ref, beta_ref, columns_ref, *refs):
@@ -167,13 +182,16 @@
     def owner(a, y, c):
         return ((x_hi ^ a) * 4 + y) * 2 + (core ^ c)
 
-    index = jnp.stack([owner(0, y, 0) for y in range(4)] + [owner(1, y, 0) for y in range(4)])
+    index = jnp.stack([owner(0, y, 0) for y in range(4)] + [owner(1, y_at ^ d, 0) for d in (0, 1, 3, 2, 0, 3, 1, 2)])
 
     current_far = swap(current_t, "x_hi")
     near = lax.all_gather(current_t, "y")
-    far = lax.all_gather(current_far, "y")
 
     even, current_far = lax.optimization_barrier((gather_even(tokens), current_far))
+    far = []
+    for rows, step in ((current_far[:hidden], 1), (current_far[hidden:], 3)):
+        pair = jnp.stack([rows, swap(rows, "y", step)])
+        far += [pair, swap(pair, "y", 4 - step)]
     group_rows = gather_x(*gather_z(even)).reshape(-1, width)
     other_rows = swap(group_rows, "core")
 
@@ -183,13 +201,14 @@
     silu_value, silu_slope, silu_curve = silu_parts(gate_pre)
     hidden_act = (silu_value * up_pre).astype(BF)
     output_part = dot(hidden_act, down_weight, ((0,), (0,))).astype(BF)
-    output_fold = fold_x(output_part)
-
     def cut(value, start, size):
         return lax.dynamic_slice_in_dim(value, start * own_rows, size * own_rows, value.ndim - 1)
 
     both = jnp.stack([cut(group_rows, x_hi * 8, 8), swap(cut(group_rows, 8 - x_hi * 8, 8), "x_hi")])
 
+    output_part, both, *far = lax.optimization_barrier((output_part, both, *far))
+    output_fold = fold_x(output_part)
+
     def halves(value):
         return value.reshape(2, hidden, value.shape[1])
 
@@ -201,10 +220,11 @@
 
     own_shape = sum_of(count)
     rows_pair = (group_rows, other_rows)
-    near_sums = tangent_call(0, index, rows_pair, near.reshape(4, 2, hidden, -1), [], [sum_of(2 * count)])
+    near_sums = tangent_call(0, index, rows_pair, [near.reshape(4, 2, hidden, -1)], [], [sum_of(2 * count)])
     own_sums, other_sums = tangent_call(
-        1, index, rows_pair, far.reshape(4, 2, hidden, -1), near_sums, [own_shape, own_shape]
-    )
+        1, index, rows_pair, far, near_sums, [own_shape, own_shape]
+    )
+    own_sums, output_fold = lax.optimization_barrier((own_sums, output_fold))
     step_spec = pl.BlockSpec((2, chunk, count), lambda i: (0, i, 0))
     tangent, tangent_act = pl.pallas_call(
         act_kernel,
@@ -220,8 +240,8 @@
     tangent_fold = fold_x(tangent_part)
 
 
-    output_sum = fold_z(output_fold)
-    tangent_sum = fold_z(tangent_fold)
+    sums = fold_z(jnp.concatenate([output_fold, tangent_fold], 2))
+    output_sum, tangent_sum = sums[: targets.shape[0]], sums[targets.shape[0] :]
     error_rows = ((output_sum - targets.astype(F32)) / token_total).astype(BF)
     tangent_error = (tangent_sum / token_total).astype(BF)
     errors = jnp.concatenate([error_rows, tangent_error], 0)
@@ -241,6 +261,7 @@
     )
     grad_up = back_tangent * silu_value + back_error * silu_slope * tangent_gate
     tangent_grad = jnp.concatenate([grad_gate, grad_up], 0).astype(BF)
+    tangent_grad, own_columns = lax.optimization_barrier((tangent_grad, own_columns))
     grad_far = swap(tangent_grad, "x_hi")
     blocks = []
     for piece in (tangent_grad, grad_far):

time: 260 us -> 252 us (0.969)
  waiting for transfers between devices: 68.3 us -> 59.6 us
  starting transfers between devices: 74.5 us -> 70.7 us
  blocking collectives: 47.2 us -> 49.9 us
    all_gather x1 -> x0, waiting for transfers between devices: 12.5 us -> none  [per_device(): far = lax.all_gather(current_far, 'y')]
    ppermute x33, waiting for transfers between devices: 49.6 us -> 55.6 us  [swap(): return lax.ppermute(value, axis, [(i, i ^ step) for i in range(size)])]
    ppermute x4 -> x3, starting transfers between devices: 12.2 us -> 7.34 us  [neighbour(): lax.ppermute(value, 'z', [(i, (i + 1) % 8 if i % 2 else (i - 1) % 8) for...]
    ppermute x4 -> x3, waiting for transfers between devices: 5.41 us -> 3.96 us  [neighbour(): lax.ppermute(value, 'z', [(i, (i + 1) % 8 if i % 2 else (i - 1) % 8) for...]
    unnamed x31 -> x41, local copies, waits for them, and re-layouts: 8.09 us -> 9.29 us
  transfers between devices with their start and end apart: 39 -> 37, of which waited for: 17 -> 16; matrix products, arithmetic and copies ran while one was open for 14% -> 10% of each run, Pallas kernels for 3% -> 3%
where the time goes in v1:
time: 252 us; the launch traced here: 251 us
  starting transfers between devices  70.7 us (28%)
  waiting for transfers between devices  59.6 us (24%)
  blocking collectives  49.9 us (20%)
  local copies, waits for them, and re-layouts  16.9 us (7%)
  between operations  15.2 us (6%)
  matrix products  13.6 us (5%)
  Pallas kernels  13.6 us (5%)
  other arithmetic  11.5 us (5%)
    ppermute x33, starting transfers between devices, swap(): return lax.ppermute(value, axis, [(i, i ^ step) for i in range(size)])  63.4 us
    ppermute x33, waiting for transfers between devices, swap(): return lax.ppermute(value, axis, [(i, i ^ step) for i in range(size)])  55.6 us
    all_gather x2, blocking collectives, per_device(): piece = lax.all_gather(piece, 'y')  25.9 us
    all_to_all x2, blocking collectives, per_device(): lax.all_to_all(jnp.broadcast_to(sums[None], (size, 8, 128)), axes, 0, 0,...  24 us
    dot_general x5, matrix products, dot(): return lax.dot_general(a, b, (dims, ((), ())), preferred_element_type=F32)  13.6 us
    unnamed x41, local copies, waits for them, and re-layouts  9.29 us
    ppermute x3, starting transfers between devices, neighbour(): lax.ppermute(value, 'z', [(i, (i + 1) % 8 if i % 2 else (i - 1) % 8) for...  7.34 us
    pallas_call x2, Pallas kernels, tangent_call(): pl.pallas_call(lambda *refs: tangent_kernel(first, *refs), out_shape=out_...  7.07 us
  transfers between devices with their start and end apart: 37, of which 16 were waited for; matrix products, arithmetic and copies ran while one was open for 10% of the time, Pallas kernels for 3%

profile of v1, /device:TPU:1, one launch (start us, length us, event | category | flops | bytes accessed | tf_op | source)
XLA Modules:
  0.0 251.0 jit_solution(18137321989353548312)
XLA Ops:
  7.2 3.9 %collective-permute-start = (bf16[8,4096]{1,0:T(8,128)(2,1)}, bf16[8,4096]{1,0:T(8,128)(2,1)S(1)}, u32[]{:S(2)}, u32[]{:S(2)}) collective-permute-start(bf16[8,4096]{1,0:T(8,128)(2,1)} %param.10), channel_id=1, source_target_pairs={{0,2},{1,3},{2,0},{3,1},{4,6},{5,7},{6,4},{7,5},{8,10},{9,11},{10,... | collective-permute-start | bytes 196616 | tf_op jit(solution)/shard_map/ppermute | solution.py:16
  11.1 5.1 %collective-permute-start.1 = (bf16[8,4096]{1,0:T(8,128)(2,1)}, bf16[8,4096]{1,0:T(8,128)(2,1)S(1)}, u32[]{:S(2)}, u32[]{:S(2)}) collective-permute-start(bf16[8,4096]{1,0:T(8,128)(2,1)} %param.10), channel_id=1, source_target_pairs={{0,4},{1,5},{2,6},{3,7},{4,0},{5,1},{6,2},{7,3},{8,12},{9,13},{10,... | collective-permute-start | bytes 196616 | tf_op jit(solution)/shard_map/ppermute | solution.py:16
  16.2 2.7 %collective-permute-start.3 = (bf16[896,256]{1,0:T(8,128)(2,1)}, bf16[896,256]{1,0:T(8,128)(2,1)S(1)}, u32[]{:S(2)}, u32[]{:S(2)}) collective-permute-start(bf16[896,256]{1,0:T(8,128)(2,1)} %bitcast.147), channel_id=1, source_target_pairs={{0,128},{128,0},{1,129},{129,1},{2,130},{130,2},{3,131},{131,3},{4... | collective-permute-start | bytes 1376264 | tf_op jit(solution)/shard_map/ppermute | solution.py:16
  19.7 2.4 collective-permute-done.2
  22.9 5.8 %collective-permute-done.3 = bf16[896,256]{1,0:T(8,128)(2,1)S(1)} collective-permute-done((bf16[896,256]{1,0:T(8,128)(2,1)}, bf16[896,256]{1,0:T(8,128)(2,1)S(1)}, u32[]{:S(2)}, u32[]{:S(2)}) %collective-permute-start.3) | collective-permute-done | bytes 458784 | tf_op jit(solution)/shard_map/ppermute | solution.py:16
  28.7 1.3 collective-permute-start.6
  30.0 2.8 %collective-permute-start.5 = (bf16[4,8,2048]{2,1,0:T(8,128)(2,1)S(1)}, bf16[4,8,2048]{2,1,0:T(8,128)(2,1)S(1)}, u32[]{:S(2)}, u32[]{:S(2)}) collective-permute-start(bf16[4,8,2048]{2,1,0:T(8,128)(2,1)S(1)} %get-tuple-element.81), channel_id=1, source_target_pairs={{0,7},{1,2},{2,1},{3,4},{4,3},{5,6},{6,5},{7,0},{8,15},{9,10},{10,... | collective-permute-start | bytes 393224 | tf_op jit(solution)/shard_map/ppermute | solution.py:28
  33.0 1.4 collective-permute-start.10
  34.3 1.9 collective-permute-start.12
  37.5 6.8 %collective-permute-done.10 = bf16[448,256]{1,0:T(8,128)(2,1)S(1)} collective-permute-done((bf16[448,256]{1,0:T(8,128)(2,1)S(1)}, bf16[448,256]{1,0:T(8,128)(2,1)S(1)}, u32[]{:S(2)}, u32[]{:S(2)}) %collective-permute-start.10) | collective-permute-done | bytes 229408 | tf_op jit(solution)/shard_map/ppermute | solution.py:16
  44.3 3.0 %collective-permute-start.11 = (bf16[2,448,256]{2,1,0:T(8,128)(2,1)S(1)}, bf16[2,448,256]{2,1,0:T(8,128)(2,1)}, u32[]{:S(2)}, u32[]{:S(2)}) collective-permute-start(bf16[2,448,256]{2,1,0:T(8,128)(2,1)S(1)} %pad_maximum_fusion.6.refs_3_), channel_id=1, source_target_pairs={{0,96},{32,64},{64,32},{96,0},{1,97},{33,65},{65,33},{97,1},{2,98}... | collective-permute-start | bytes 1376264 | tf_op jit(solution)/shard_map/ppermute | solution.py:16
  47.7 4.3 %collective-permute-start.8 = (bf16[128,4096]{1,0:T(8,128)(2,1)S(1)}, bf16[128,4096]{1,0:T(8,128)(2,1)S(1)}, u32[]{:S(2)}, u32[]{:S(2)}) collective-permute-start(bf16[128,4096]{1,0:T(8,128)(2,1)S(1)} %maximum_bitcast_fusion.refs_1_), channel_id=1, source_target_pairs={{0,16},{16,0},{1,17},{17,1},{2,18},{18,2},{3,19},{19,3},{4,20},{20... | collective-permute-start | bytes 3145736 | tf_op jit(solution)/shard_map/ppermute | solution.py:16
  52.1 2.5 %collective-permute-start.9 = (bf16[128,2048]{1,0:T(8,128)(2,1)S(1)}, bf16[128,2048]{1,0:T(8,128)(2,1)S(1)}, u32[]{:S(2)}, u32[]{:S(2)}) collective-permute-start(bf16[128,2048]{1,0:T(8,128)(2,1)S(1)} %get-tuple-element.66), channel_id=1, source_target_pairs={{0,128},{128,0},{1,129},{129,1},{2,130},{130,2},{3,131},{131,3},{4... | collective-permute-start | bytes 1572872 | tf_op jit(solution)/shard_map/ppermute | solution.py:16
  54.7 5.3 %convolution_bitcast_fusion = f32[896,128]{1,0:T(8,128)S(1)} fusion(bf16[896,4096]{1,0:T(8,128)(2,1)} %bitcast.175, bf16[4,8,4096]{2,1,0:T(8,128)(2,1)} %copy-done.16, bf16[4,8,4096]{2,1,0:T(8,128)(2,1)} %copy-done.15, bf16[4,8,2048]{2,1,0:T(8,128)(2,1)S(1)} %copy-done.12, bf16[4,8,2048]{2,1,0:T(8,128)(2,1)S(1)} %copy-done.14, ...), kind=kOutput, calls=%fused_computation.5 | convolution fusion | flops 944766976 | bytes 8847360 | tf_op jit(solution)/shard_map/dot_general | solution.py:69
  60.0 6.9 %collective-permute-done.9 = bf16[128,2048]{1,0:T(8,128)(2,1)S(1)} collective-permute-done((bf16[128,2048]{1,0:T(8,128)(2,1)S(1)}, bf16[128,2048]{1,0:T(8,128)(2,1)S(1)}, u32[]{:S(2)}, u32[]{:S(2)}) %collective-permute-start.9) | collective-permute-done | bytes 524320 | tf_op jit(solution)/shard_map/ppermute | solution.py:16
  66.9 1.1 pad_maximum_fusion
  68.0 2.8 %convolution_convert_fusion.1 = bf16[128,4096]{1,0:T(8,128)(2,1)S(1)} fusion(bf16[448,4096]{1,0:T(8,128)(2,1)} %param.13, f32[896,128]{1,0:T(8,128)S(1)} %convolution_bitcast_fusion), kind=kOutput, calls=%fused_computation.4 | convolution fusion | flops 470630400 | bytes 5177344 | tf_op jit(solution)/shard_map/dot_general | solution.py:69
  70.8 1.1 fusion.26
  72.3 1.5 copy-done.1
  73.8 2.7 %shard_map.121.refs_7_ = f32[2,448,256]{2,1,0:T(8,128)S(1)} custom-call(s32[12]{0:T(128)S(1)} %stack.188.refs_0_, bf16[128,4096]{1,0:T(8,128)(2,1)S(1)} %maximum_bitcast_fusion.refs_1_, bf16[128,4096]{1,0:T(8,128)(2,1)S(1)} %collective-permute-done.8.refs_2_, bf16[4,2,448,256]{3,2,1,0:T(8,128)(2,1)S(1)} %bitcast.155), custom_call_target="tpu_custom_call" | custom-call | flops 469762048 | bytes 1835008 | tf_op jit(solution)/shard_map/pallas_call | solution.py:117
  76.5 4.4 %shard_map.122 = (f32[2,448,128]{2,1,0:T(8,128)S(1)}, f32[2,448,128]{2,1,0:T(8,128)S(1)}) custom-call(s32[12]{0:T(128)S(1)} %stack.188.refs_0_, bf16[128,4096]{1,0:T(8,128)(2,1)S(1)} %maximum_bitcast_fusion.refs_1_, bf16[128,4096]{1,0:T(8,128)(2,1)S(1)} %collective-permute-done.8.refs_2_, bf16[2,448,256]{2,1,0:T(8,128)(2,1)S(1)} %pad_maximum_fusion.6.refs_3_, ...), custom_call_target="tpu_custom_call" | custom-call | flops 469762048 | bytes 1835008 | tf_op jit(solution)/shard_map/pallas_call | solution.py:117
  80.9 1.5 collective-permute-start.15
  82.4 2.0 collective-permute-done.14
  84.4 1.2 fusion.2
  87.2 11.0 %collective-permute-done.16 = bf16[2,4,8,4096]{3,2,1,0:T(8,128)(2,1)S(1)} collective-permute-done((bf16[2,4,8,4096]{3,2,1,0:T(8,128)(2,1)S(1)}, bf16[2,4,8,4096]{3,2,1,0:T(8,128)(2,1)S(1)}, u32[]{:S(2)}, u32[]{:S(2)}) %collective-permute-start.16) | collective-permute-done | bytes 524320 | tf_op jit(solution)/shard_map/ppermute | solution.py:16
  99.2 1.8 collective-permute-start.18
  101.7 4.0 %collective-permute-done.18 = bf16[4,16,2048]{2,1,0:T(8,128)(2,1)S(1)} collective-permute-done((bf16[4,16,2048]{2,1,0:T(8,128)(2,1)S(1)}, bf16[4,16,2048]{2,1,0:T(8,128)(2,1)S(1)}, u32[]{:S(2)}, u32[]{:S(2)}) %collective-permute-start.18) | collective-permute-done | bytes 262176 | tf_op jit(solution)/shard_map/ppermute | solution.py:28
  106.7 1.9 fusion
  108.6 1.1 slice_bitcast_fusion.6
  109.7 1.2 collective-permute-start.19
  110.9 1.7 collective-permute-start.20
  112.6 2.8 %collective-permute-start.21 = (bf16[16,4096]{1,0:T(8,128)(2,1)S(1)}, bf16[16,4096]{1,0:T(8,128)(2,1)S(1)}, u32[]{:S(2)}, u32[]{:S(2)}) collective-permute-start(bf16[16,4096]{1,0:T(8,128)(2,1)S(1)} %get-tuple-element.70), channel_id=1, source_target_pairs={{0,6},{1,7},{2,4},{3,5},{4,2},{5,3},{6,0},{7,1},{8,14},{9,15},{10,... | collective-permute-start | bytes 393224 | tf_op jit(solution)/shard_map/ppermute | solution.py:16
  115.4 2.0 collective-permute-done.19
  117.4 2.1 collective-permute-done.20
  119.5 2.4 collective-permute-done.21
  122.8 6.9 %collective-permute-start.22 = (bf16[16,4096]{1,0:T(8,128)(2,1)S(1)}, bf16[16,4096]{1,0:T(8,128)(2,1)S(1)}, u32[]{:S(2)}, u32[]{:S(2)}) collective-permute-start(bf16[16,4096]{1,0:T(8,128)(2,1)S(1)} %pad_maximum_fusion.11), channel_id=1, source_target_pairs={{0,2},{1,3},{2,0},{3,1},{4,6},{5,7},{6,4},{7,5},{8,10},{9,11},{10,... | collective-permute-start | bytes 393224 | tf_op jit(solution)/shard_map/ppermute | solution.py:16
  129.7 1.1 collective-permute-start.23
  130.8 2.3 collective-permute-start.24
  133.9 1.7 collective-permute-start.29
  135.6 1.5 collective-permute-start.30
  138.1 4.3 %collective-permute-done.23 = bf16[16,4096]{1,0:T(8,128)(2,1)S(1)} collective-permute-done((bf16[16,4096]{1,0:T(8,128)(2,1)S(1)}, bf16[16,4096]{1,0:T(8,128)(2,1)S(1)}, u32[]{:S(2)}, u32[]{:S(2)}) %collective-permute-start.23) | collective-permute-done | bytes 131104 | tf_op jit(solution)/shard_map/ppermute | solution.py:16
  143.3 2.7 %collective-permute-start.26 = (bf16[4,16,2048]{2,1,0:T(8,128)(2,1)S(1)}, bf16[4,16,2048]{2,1,0:T(8,128)(2,1)S(1)}, u32[]{:S(2)}, u32[]{:S(2)}) collective-permute-start(bf16[4,16,2048]{2,1,0:T(8,128)(2,1)S(1)} %get-tuple-element.68), channel_id=1, source_target_pairs={{0,7},{1,2},{2,1},{3,4},{4,3},{5,6},{6,5},{7,0},{8,15},{9,10},{10,... | collective-permute-start | bytes 786440 | tf_op jit(solution)/shard_map/ppermute | solution.py:28
  148.0 2.6 %collective-permute-start.25 = (bf16[4,16,2048]{2,1,0:T(8,128)(2,1)}, bf16[4,16,2048]{2,1,0:T(8,128)(2,1)}, u32[]{:S(2)}, u32[]{:S(2)}) collective-permute-start(bf16[4,16,2048]{2,1,0:T(8,128)(2,1)} %get-tuple-element.67), channel_id=1, source_target_pairs={{0,1},{1,0},{2,3},{3,2},{4,5},{5,4},{6,7},{7,6},{8,9},{9,8},{10,11... | collective-permute-start | bytes 786440 | tf_op jit(solution)/shard_map/ppermute | solution.py:16
  151.6 2.2 collective-permute-start.32
  154.5 2.1 collective-permute-done.25
  157.6 1.2 collective-permute-start.28
  158.8 1.8 bitcast_dynamic-update-slice_fusion.2
  160.6 1.9 bitcast_dynamic-update-slice_fusion.1
  162.5 1.3 pad_maximum_fusion.2
  163.9 5.6 %collective-permute-done.28 = bf16[4,16,4096]{2,1,0:T(8,128)(2,1)S(1)} collective-permute-done((bf16[4,16,4096]{2,1,0:T(8,128)(2,1)S(1)}, bf16[4,16,4096]{2,1,0:T(8,128)(2,1)S(1)}, u32[]{:S(2)}, u32[]{:S(2)}) %collective-permute-start.28) | collective-permute-done | bytes 524320 | tf_op jit(solution)/shard_map/ppermute | solution.py:16
  170.3 2.3 convolution_bitcast_fusion.2
  172.7 2.4 fusion.16
  176.0 13.1 %all-gather = bf16[3584,128]{1,0:T(8,128)(2,1)S(1)} all-gather(bf16[896,128]{1,0:T(8,128)(2,1)S(1)} %pad_maximum_fusion.10), channel_id=2, replica_groups=mesh['x_hi'=2,'y'=4,'core'=2,'x_lo'=2,'z'=8] {'y'}, dimensions={0}, use_global_device_ids=true | all-gather | bytes 1146880 | tf_op jit(solution)/shard_map/all_gather | solution.py:268
  189.2 4.7 %collective-permute-start.33 = (bf16[4,896,128]{2,1,0:T(8,128)(2,1)S(1)}, bf16[4,896,128]{2,1,0:T(8,128)(2,1)}, u32[]{:S(2)}, u32[]{:S(2)}) collective-permute-start(bf16[4,896,128]{2,1,0:T(8,128)(2,1)S(1)} %bitcast.151), channel_id=1, source_target_pairs={{0,16},{16,0},{1,17},{17,1},{2,18},{18,2},{3,19},{19,3},{4,20},{20... | collective-permute-start | bytes 2752520 | tf_op jit(solution)/shard_map/ppermute | solution.py:16
  193.9 12.8 %all-gather.1 = bf16[3584,128]{1,0:T(8,128)(2,1)S(1)} all-gather(bf16[896,128]{1,0:T(8,128)(2,1)S(1)} %collective-permute-done.34), channel_id=3, replica_groups=mesh['x_hi'=2,'y'=4,'core'=2,'x_lo'=2,'z'=8] {'y'}, dimensions={0}, use_global_device_ids=true | all-gather | bytes 1146880 | tf_op jit(solution)/shard_map/all_gather | solution.py:268
  206.7 1.9 collective-permute-start.35
  209.3 1.5 collective-permute-done.35.refs_3_
  210.8 1.0 copy-done.4
  211.8 4.3 %shard_map.124 = (f32[896,256]{1,0:T(8,128)S(1)}, f32[8,128]{1,0:T(8,128)S(1)}) custom-call(s32[16]{0:T(128)S(1)} %stack.179.index_ref, f32[1,1]{1,0:T(1,128)} %bitcast.145.beta_ref, bf16[16,128,256]{2,1,0:T(8,128)(2,1)S(1)} %bitcast.146, bf16[4,896,128]{2,1,0:T(8,128)(2,1)S(1)} %bitcast.152, bf16[4,896,128]{2,1,0:T(8,128)(2,1)} %collective-permute-done.33.refs_1_, ...), custom_call_target="tpu_custom_call" | custom-call | flops 1073741824 | bytes 7340032 | tf_op jit(solution)/shard_map/pallas_call | solution.py:273
  216.1 1.0 copy-done.2
  217.1 11.3 %all_to_all.10 = f32[8,8,128]{2,1,0:T(8,128)S(1)} all-to-all(f32[8,8,128]{2,1,0:T(8,128)S(1)} %broadcast_in_dim.24), channel_id=1, replica_groups=mesh['x_hi'=2,'y'=4,'core'=2,'x_lo'=2,'z'=8] {'z'}, dimensions={0} | all-to-all | bytes 65536 | tf_op jit(solution)/shard_map/all_to_all | solution.py:298
  228.5 12.7 %all_to_all.11.refs_0_ = f32[32,8,128]{2,1,0:T(8,128)S(1)} all-to-all(f32[32,8,128]{2,1,0:T(8,128)S(1)} %broadcast_in_dim.25), channel_id=1, replica_groups=mesh['x_hi'=2,'y'=4,'core'=2,'x_lo'=2,'z'=8] {'x_hi','y','core','x_lo'}, dimensions={0} | all-to-all | bytes 262144 | tf_op jit(solution)/shard_map/all_to_all | solution.py:298
  241.2 1.2 copy-done.3
  242.3 1.9 shard_map.125
  (109 shorter events, 18.1 us)
Async XLA Ops:
  7.2 60.8 %all-gather.4.cloned.1.call-start = ((), (), s32[]{:S(2)}) async-start(), calls=%async_computation.2 | async-start | bytes 2293760 | tf_op jit(solution)/shard_map/all_gather | solution.py:188
  7.2 12.5 %collective-permute-start = (bf16[8,4096]{1,0:T(8,128)(2,1)}, bf16[8,4096]{1,0:T(8,128)(2,1)S(1)}, u32[]{:S(2)}, u32[]{:S(2)}) collective-permute-start(bf16[8,4096]{1,0:T(8,128)(2,1)} %param.10), channel_id=1, source_target_pairs={{0,2},{1,3},{2,0},{3,1},{4,6},{5,7},{6,4},{7,5},{8,10},{9,11},{10,... | collective-permute-start | bytes 196616 | tf_op jit(solution)/shard_map/ppermute | solution.py:16
  11.1 8.6 %collective-permute-start.1 = (bf16[8,4096]{1,0:T(8,128)(2,1)}, bf16[8,4096]{1,0:T(8,128)(2,1)S(1)}, u32[]{:S(2)}, u32[]{:S(2)}) collective-permute-start(bf16[8,4096]{1,0:T(8,128)(2,1)} %param.10), channel_id=1, source_target_pairs={{0,4},{1,5},{2,6},{3,7},{4,0},{5,1},{6,2},{7,3},{8,12},{9,13},{10,... | collective-permute-start | bytes 196616 | tf_op jit(solution)/shard_map/ppermute | solution.py:16
  16.2 5.8 %collective-permute-start.2 = (bf16[8,4096]{1,0:T(8,128)(2,1)}, bf16[8,4096]{1,0:T(8,128)(2,1)S(1)}, u32[]{:S(2)}, u32[]{:S(2)}) collective-permute-start(bf16[8,4096]{1,0:T(8,128)(2,1)} %param.10), channel_id=1, source_target_pairs={{0,6},{1,7},{2,4},{3,5},{4,2},{5,3},{6,0},{7,1},{8,14},{9,15},{10,... | collective-permute-start | bytes 196616 | tf_op jit(solution)/shard_map/ppermute | solution.py:16
  16.2 12.5 %collective-permute-start.3 = (bf16[896,256]{1,0:T(8,128)(2,1)}, bf16[896,256]{1,0:T(8,128)(2,1)S(1)}, u32[]{:S(2)}, u32[]{:S(2)}) collective-permute-start(bf16[896,256]{1,0:T(8,128)(2,1)} %bitcast.147), channel_id=1, source_target_pairs={{0,128},{128,0},{1,129},{129,1},{2,130},{130,2},{3,131},{131,3},{4... | collective-permute-start | bytes 1376264 | tf_op jit(solution)/shard_map/ppermute | solution.py:16
  22.9 24.6 %copy-start.8 = (bf16[4,8,4096]{2,1,0:T(8,128)(2,1)}, bf16[4,8,4096]{2,1,0:T(8,128)(2,1)S(1)}, u32[]{:S(2)}) copy-start(bf16[4,8,4096]{2,1,0:T(8,128)(2,1)S(1)} %pad_maximum_fusion.8) | copy-start | bytes 786436
  28.7 18.8 %collective-permute-start.6 = (bf16[4,8,4096]{2,1,0:T(8,128)(2,1)S(1)}, bf16[4,8,4096]{2,1,0:T(8,128)(2,1)S(1)}, u32[]{:S(2)}, u32[]{:S(2)}) collective-permute-start(bf16[4,8,4096]{2,1,0:T(8,128)(2,1)S(1)} %pad_maximum_fusion.8), channel_id=1, source_target_pairs={{0,8},{8,0},{1,9},{9,1},{2,10},{10,2},{3,11},{11,3},{4,12},{12,4},... | collective-permute-start | bytes 786440 | tf_op jit(solution)/shard_map/ppermute | solution.py:16
  30.0 6.2 %collective-permute-start.5 = (bf16[4,8,2048]{2,1,0:T(8,128)(2,1)S(1)}, bf16[4,8,2048]{2,1,0:T(8,128)(2,1)S(1)}, u32[]{:S(2)}, u32[]{:S(2)}) collective-permute-start(bf16[4,8,2048]{2,1,0:T(8,128)(2,1)S(1)} %get-tuple-element.81), channel_id=1, source_target_pairs={{0,7},{1,2},{2,1},{3,4},{4,3},{5,6},{6,5},{7,0},{8,15},{9,10},{10,... | collective-permute-start | bytes 393224 | tf_op jit(solution)/shard_map/ppermute | solution.py:28
  32.9 4.2 %collective-permute-start.4 = (bf16[4,8,2048]{2,1,0:T(8,128)(2,1)S(1)}, bf16[4,8,2048]{2,1,0:T(8,128)(2,1)S(1)}, u32[]{:S(2)}, u32[]{:S(2)}) collective-permute-start(bf16[4,8,2048]{2,1,0:T(8,128)(2,1)S(1)} %get-tuple-element.80), channel_id=1, source_target_pairs={{0,1},{1,0},{2,3},{3,2},{4,5},{5,4},{6,7},{7,6},{8,9},{9,8},{10,11... | collective-permute-start | bytes 393224 | tf_op jit(solution)/shard_map/ppermute | solution.py:16
  33.0 11.3 %collective-permute-start.10 = (bf16[448,256]{1,0:T(8,128)(2,1)S(1)}, bf16[448,256]{1,0:T(8,128)(2,1)S(1)}, u32[]{:S(2)}, u32[]{:S(2)}) collective-permute-start(bf16[448,256]{1,0:T(8,128)(2,1)S(1)} %get-tuple-element.77), channel_id=1, source_target_pairs={{0,32},{32,0},{64,96},{96,64},{1,33},{33,1},{65,97},{97,65},{2,34}... | collective-permute-start | bytes 688136 | tf_op jit(solution)/shard_map/ppermute | solution.py:16
  34.3 13.0 %collective-permute-start.12 = (bf16[448,256]{1,0:T(8,128)(2,1)S(1)}, bf16[448,256]{1,0:T(8,128)(2,1)S(1)}, u32[]{:S(2)}, u32[]{:S(2)}) collective-permute-start(bf16[448,256]{1,0:T(8,128)(2,1)S(1)} %get-tuple-element.76), channel_id=1, source_target_pairs={{0,96},{32,64},{64,32},{96,0},{1,97},{33,65},{65,33},{97,1},{2,98}... | collective-permute-start | bytes 688136 | tf_op jit(solution)/shard_map/ppermute | solution.py:16
  36.8 10.7 %copy-start.11 = (bf16[4,8,2048]{2,1,0:T(8,128)(2,1)}, bf16[4,8,2048]{2,1,0:T(8,128)(2,1)S(1)}, u32[]{:S(2)}) copy-start(bf16[4,8,2048]{2,1,0:T(8,128)(2,1)S(1)} %reverse_select_fusion.2) | copy-start | bytes 393220
  37.1 10.5 %copy-start.13 = (bf16[4,8,2048]{2,1,0:T(8,128)(2,1)}, bf16[4,8,2048]{2,1,0:T(8,128)(2,1)S(1)}, u32[]{:S(2)}) copy-start(bf16[4,8,2048]{2,1,0:T(8,128)(2,1)S(1)} %collective-permute-done.4) | copy-start | bytes 393220
  37.1 10.4 %collective-permute-start.7 = (bf16[4,8,4096]{2,1,0:T(8,128)(2,1)S(1)}, bf16[4,8,4096]{2,1,0:T(8,128)(2,1)S(1)}, u32[]{:S(2)}, u32[]{:S(2)}) collective-permute-start(bf16[4,8,4096]{2,1,0:T(8,128)(2,1)S(1)} %pad_maximum_fusion.9), channel_id=1, source_target_pairs={{0,8},{8,0},{1,9},{9,1},{2,10},{10,2},{3,11},{11,3},{4,12},{12,4},... | collective-permute-start | bytes 786440 | tf_op jit(solution)/shard_map/ppermute | solution.py:16
  44.3 26.5 %collective-permute-start.11 = (bf16[2,448,256]{2,1,0:T(8,128)(2,1)S(1)}, bf16[2,448,256]{2,1,0:T(8,128)(2,1)}, u32[]{:S(2)}, u32[]{:S(2)}) collective-permute-start(bf16[2,448,256]{2,1,0:T(8,128)(2,1)S(1)} %pad_maximum_fusion.6.refs_3_), channel_id=1, source_target_pairs={{0,96},{32,64},{64,32},{96,0},{1,97},{33,65},{65,33},{97,1},{2,98}... | collective-permute-start | bytes 1376264 | tf_op jit(solution)/shard_map/ppermute | solution.py:16
  47.4 23.4 %collective-permute-start.13 = (bf16[2,448,256]{2,1,0:T(8,128)(2,1)S(1)}, bf16[2,448,256]{2,1,0:T(8,128)(2,1)}, u32[]{:S(2)}, u32[]{:S(2)}) collective-permute-start(bf16[2,448,256]{2,1,0:T(8,128)(2,1)S(1)} %pad_maximum_fusion.7.refs_5_), channel_id=1, source_target_pairs={{0,32},{32,0},{64,96},{96,64},{1,33},{33,1},{65,97},{97,65},{2,34}... | collective-permute-start | bytes 1376264 | tf_op jit(solution)/shard_map/ppermute | solution.py:16
  47.5 4.6 %copy-start.15 = (bf16[4,8,4096]{2,1,0:T(8,128)(2,1)}, bf16[4,8,4096]{2,1,0:T(8,128)(2,1)S(1)}, u32[]{:S(2)}) copy-start(bf16[4,8,4096]{2,1,0:T(8,128)(2,1)S(1)} %collective-permute-done.6) | copy-start | bytes 786436
  47.6 4.5 %copy-start.16 = (bf16[4,8,4096]{2,1,0:T(8,128)(2,1)}, bf16[4,8,4096]{2,1,0:T(8,128)(2,1)S(1)}, u32[]{:S(2)}) copy-start(bf16[4,8,4096]{2,1,0:T(8,128)(2,1)S(1)} %collective-permute-done.7) | copy-start | bytes 786436
  47.7 7.0 %copy-start.9 = (bf16[4,8,4096]{2,1,0:T(8,128)(2,1)S(1)}, bf16[4,8,4096]{2,1,0:T(8,128)(2,1)}, u32[]{:S(2)}) copy-start(bf16[4,8,4096]{2,1,0:T(8,128)(2,1)} %copy-done.8) | copy-start | bytes 786436
  47.7 6.9 %copy-start.12 = (bf16[4,8,2048]{2,1,0:T(8,128)(2,1)S(1)}, bf16[4,8,2048]{2,1,0:T(8,128)(2,1)}, u32[]{:S(2)}) copy-start(bf16[4,8,2048]{2,1,0:T(8,128)(2,1)} %copy-done.11) | copy-start | bytes 393220
  47.7 6.9 %copy-start.14 = (bf16[4,8,2048]{2,1,0:T(8,128)(2,1)S(1)}, bf16[4,8,2048]{2,1,0:T(8,128)(2,1)}, u32[]{:S(2)}) copy-start(bf16[4,8,2048]{2,1,0:T(8,128)(2,1)} %copy-done.13) | copy-start | bytes 393220
  47.7 24.5 %collective-permute-start.8 = (bf16[128,4096]{1,0:T(8,128)(2,1)S(1)}, bf16[128,4096]{1,0:T(8,128)(2,1)S(1)}, u32[]{:S(2)}, u32[]{:S(2)}) collective-permute-start(bf16[128,4096]{1,0:T(8,128)(2,1)S(1)} %maximum_bitcast_fusion.refs_1_), channel_id=1, source_target_pairs={{0,16},{16,0},{1,17},{17,1},{2,18},{18,2},{3,19},{19,3},{4,20},{20... | collective-permute-start | bytes 3145736 | tf_op jit(solution)/shard_map/ppermute | solution.py:16
  52.1 14.8 %collective-permute-start.9 = (bf16[128,2048]{1,0:T(8,128)(2,1)S(1)}, bf16[128,2048]{1,0:T(8,128)(2,1)S(1)}, u32[]{:S(2)}, u32[]{:S(2)}) collective-permute-start(bf16[128,2048]{1,0:T(8,128)(2,1)S(1)} %get-tuple-element.66), channel_id=1, source_target_pairs={{0,128},{128,0},{1,129},{129,1},{2,130},{130,2},{3,131},{131,3},{4... | collective-permute-start | bytes 1572872 | tf_op jit(solution)/shard_map/ppermute | solution.py:16
  71.9 12.6 %collective-permute-start.14 = (bf16[2,4,8,4096]{3,2,1,0:T(8,128)(2,1)}, bf16[2,4,8,4096]{3,2,1,0:T(8,128)(2,1)}, u32[]{:S(2)}, u32[]{:S(2)}) collective-permute-start(bf16[2,4,8,4096]{3,2,1,0:T(8,128)(2,1)} %bitcast.44), channel_id=1, source_target_pairs={{0,8},{8,0},{1,9},{9,1},{2,10},{10,2},{3,11},{11,3},{4,12},{12,4},... | collective-permute-start | bytes 1572872 | tf_op jit(solution)/shard_map/ppermute | solution.py:16
  72.3 1.5 copy-start.1
  76.5 8.0 %copy-start.10 = (bf16[64,4096]{1,0:T(8,128)(2,1)S(1)}, bf16[64,4096]{1,0:T(8,128)(2,1)}, u32[]{:S(2)}) copy-start(bf16[64,4096]{1,0:T(8,128)(2,1)} %get-tuple-element.64) | copy-start | bytes 1572868
  76.5 9.5 %copy-start.5 = (bf16[448,4096]{1,0:T(8,128)(2,1)S(1)}, bf16[448,4096]{1,0:T(8,128)(2,1)}, u32[]{:S(2)}) copy-start(bf16[448,4096]{1,0:T(8,128)(2,1)} %param.13) | copy-start | bytes 11010052
  80.9 4.7 %collective-permute-start.15 = (f32[2,448,128]{2,1,0:T(8,128)S(1)}, f32[2,448,128]{2,1,0:T(8,128)S(1)}, u32[]{:S(2)}, u32[]{:S(2)}) collective-permute-start(f32[2,448,128]{2,1,0:T(8,128)S(1)} %get-tuple-element.40), channel_id=1, source_target_pairs={{0,16},{16,0},{1,17},{17,1},{2,18},{18,2},{3,19},{19,3},{4,20},{20... | collective-permute-start | bytes 1376264 | tf_op jit(solution)/shard_map/ppermute | solution.py:16
  86.9 11.4 %collective-permute-start.16 = (bf16[2,4,8,4096]{3,2,1,0:T(8,128)(2,1)S(1)}, bf16[2,4,8,4096]{3,2,1,0:T(8,128)(2,1)S(1)}, u32[]{:S(2)}, u32[]{:S(2)}) collective-permute-start(bf16[2,4,8,4096]{3,2,1,0:T(8,128)(2,1)S(1)} %bitcast.162), channel_id=1, source_target_pairs={{0,8},{8,0},{1,9},{9,1},{2,10},{10,2},{3,11},{11,3},{4,12},{12,4},... | collective-permute-start | bytes 1572872 | tf_op jit(solution)/shard_map/ppermute | solution.py:16
  99.2 6.4 %collective-permute-start.18 = (bf16[4,16,2048]{2,1,0:T(8,128)(2,1)S(1)}, bf16[4,16,2048]{2,1,0:T(8,128)(2,1)S(1)}, u32[]{:S(2)}, u32[]{:S(2)}) collective-permute-start(bf16[4,16,2048]{2,1,0:T(8,128)(2,1)S(1)} %get-tuple-element.73), channel_id=1, source_target_pairs={{0,7},{1,2},{2,1},{3,4},{4,3},{5,6},{6,5},{7,0},{8,15},{9,10},{10,... | collective-permute-start | bytes 786440 | tf_op jit(solution)/shard_map/ppermute | solution.py:28
  101.0 5.7 %collective-permute-start.17 = (bf16[4,16,2048]{2,1,0:T(8,128)(2,1)}, bf16[4,16,2048]{2,1,0:T(8,128)(2,1)}, u32[]{:S(2)}, u32[]{:S(2)}) collective-permute-start(bf16[4,16,2048]{2,1,0:T(8,128)(2,1)} %get-tuple-element.72), channel_id=1, source_target_pairs={{0,1},{1,0},{2,3},{3,2},{4,5},{5,4},{6,7},{7,6},{8,9},{9,8},{10,11... | collective-permute-start | bytes 786440 | tf_op jit(solution)/shard_map/ppermute | solution.py:16
  106.2 16.6 %copy-start.17 = (bf16[8,4096]{1,0:T(8,128)(2,1)S(1)}, bf16[8,4096]{1,0:T(8,128)(2,1)}, u32[]{:S(2)}) copy-start(bf16[8,4096]{1,0:T(8,128)(2,1)} %param.11) | copy-start | bytes 196612
  106.3 27.5 %copy-start.7 = (bf16[2,128,2048]{2,1,0:T(8,128)(2,1)S(1)}, bf16[2,128,2048]{2,1,0:T(8,128)(2,1)}, u32[]{:S(2)}) copy-start(bf16[2,128,2048]{2,1,0:T(8,128)(2,1)} %pad_maximum_fusion) | copy-start | bytes 3145732
  109.7 7.7 %collective-permute-start.19 = (bf16[16,4096]{1,0:T(8,128)(2,1)S(1)}, bf16[16,4096]{1,0:T(8,128)(2,1)S(1)}, u32[]{:S(2)}, u32[]{:S(2)}) collective-permute-start(bf16[16,4096]{1,0:T(8,128)(2,1)S(1)} %get-tuple-element.69), channel_id=1, source_target_pairs={{0,2},{1,3},{2,0},{3,1},{4,6},{5,7},{6,4},{7,5},{8,10},{9,11},{10,... | collective-permute-start | bytes 393224 | tf_op jit(solution)/shard_map/ppermute | solution.py:16
  110.9 8.6 %collective-permute-start.20 = (bf16[16,4096]{1,0:T(8,128)(2,1)S(1)}, bf16[16,4096]{1,0:T(8,128)(2,1)S(1)}, u32[]{:S(2)}, u32[]{:S(2)}) collective-permute-start(bf16[16,4096]{1,0:T(8,128)(2,1)S(1)} %get-tuple-element.71), channel_id=1, source_target_pairs={{0,4},{1,5},{2,6},{3,7},{4,0},{5,1},{6,2},{7,3},{8,12},{9,13},{10,... | collective-permute-start | bytes 393224 | tf_op jit(solution)/shard_map/ppermute | solution.py:16
  112.6 9.2 %collective-permute-start.21 = (bf16[16,4096]{1,0:T(8,128)(2,1)S(1)}, bf16[16,4096]{1,0:T(8,128)(2,1)S(1)}, u32[]{:S(2)}, u32[]{:S(2)}) collective-permute-start(bf16[16,4096]{1,0:T(8,128)(2,1)S(1)} %get-tuple-element.70), channel_id=1, source_target_pairs={{0,6},{1,7},{2,4},{3,5},{4,2},{5,3},{6,0},{7,1},{8,14},{9,15},{10,... | collective-permute-start | bytes 393224 | tf_op jit(solution)/shard_map/ppermute | solution.py:16
  122.8 14.3 %collective-permute-start.22 = (bf16[16,4096]{1,0:T(8,128)(2,1)S(1)}, bf16[16,4096]{1,0:T(8,128)(2,1)S(1)}, u32[]{:S(2)}, u32[]{:S(2)}) collective-permute-start(bf16[16,4096]{1,0:T(8,128)(2,1)S(1)} %pad_maximum_fusion.11), channel_id=1, source_target_pairs={{0,2},{1,3},{2,0},{3,1},{4,6},{5,7},{6,4},{7,5},{8,10},{9,11},{10,... | collective-permute-start | bytes 393224 | tf_op jit(solution)/shard_map/ppermute | solution.py:16
  129.7 12.7 %collective-permute-start.23 = (bf16[16,4096]{1,0:T(8,128)(2,1)S(1)}, bf16[16,4096]{1,0:T(8,128)(2,1)S(1)}, u32[]{:S(2)}, u32[]{:S(2)}) collective-permute-start(bf16[16,4096]{1,0:T(8,128)(2,1)S(1)} %pad_maximum_fusion.11), channel_id=1, source_target_pairs={{0,4},{1,5},{2,6},{3,7},{4,0},{5,1},{6,2},{7,3},{8,12},{9,13},{10,... | collective-permute-start | bytes 393224 | tf_op jit(solution)/shard_map/ppermute | solution.py:16
  130.8 11.6 %collective-permute-start.24 = (bf16[16,4096]{1,0:T(8,128)(2,1)S(1)}, bf16[16,4096]{1,0:T(8,128)(2,1)S(1)}, u32[]{:S(2)}, u32[]{:S(2)}) collective-permute-start(bf16[16,4096]{1,0:T(8,128)(2,1)S(1)} %pad_maximum_fusion.11), channel_id=1, source_target_pairs={{0,6},{1,7},{2,4},{3,5},{4,2},{5,3},{6,0},{7,1},{8,14},{9,15},{10,... | collective-permute-start | bytes 393224 | tf_op jit(solution)/shard_map/ppermute | solution.py:16
  133.9 14.1 %collective-permute-start.29 = (bf16[2,128,512]{2,1,0:T(8,128)(2,1)S(1)}, bf16[2,128,512]{2,1,0:T(8,128)(2,1)S(1)}, u32[]{:S(2)}, u32[]{:S(2)}) collective-permute-start(bf16[2,128,512]{2,1,0:T(8,128)(2,1)S(1)} %get-tuple-element.60), channel_id=1, source_target_pairs={{0,32},{32,0},{64,96},{96,64},{1,33},{33,1},{65,97},{97,65},{2,34}... | collective-permute-start | bytes 786440 | tf_op jit(solution)/shard_map/ppermute | solution.py:16
  135.6 15.0 %collective-permute-start.30 = (bf16[2,128,512]{2,1,0:T(8,128)(2,1)S(1)}, bf16[2,128,512]{2,1,0:T(8,128)(2,1)S(1)}, u32[]{:S(2)}, u32[]{:S(2)}) collective-permute-start(bf16[2,128,512]{2,1,0:T(8,128)(2,1)S(1)} %get-tuple-element.59), channel_id=1, source_target_pairs={{0,64},{32,96},{64,0},{96,32},{1,65},{33,97},{65,1},{97,33},{2,66}... | collective-permute-start | bytes 786440 | tf_op jit(solution)/shard_map/ppermute | solution.py:16
  137.1 13.5 %collective-permute-start.31 = (bf16[2,128,512]{2,1,0:T(8,128)(2,1)S(1)}, bf16[2,128,512]{2,1,0:T(8,128)(2,1)S(1)}, u32[]{:S(2)}, u32[]{:S(2)}) collective-permute-start(bf16[2,128,512]{2,1,0:T(8,128)(2,1)S(1)} %get-tuple-element.58), channel_id=1, source_target_pairs={{0,96},{32,64},{64,32},{96,0},{1,97},{33,65},{65,33},{97,1},{2,98}... | collective-permute-start | bytes 786440 | tf_op jit(solution)/shard_map/ppermute | solution.py:16
  143.2 17.3 %collective-permute-start.27 = (bf16[4,16,4096]{2,1,0:T(8,128)(2,1)S(1)}, bf16[4,16,4096]{2,1,0:T(8,128)(2,1)}, u32[]{:S(2)}, u32[]{:S(2)}) collective-permute-start(bf16[4,16,4096]{2,1,0:T(8,128)(2,1)S(1)} %pad_maximum_fusion.4), channel_id=1, source_target_pairs={{0,8},{8,0},{1,9},{9,1},{2,10},{10,2},{3,11},{11,3},{4,12},{12,4},... | collective-permute-start | bytes 1572872 | tf_op jit(solution)/shard_map/ppermute | solution.py:16
  143.3 10.6 %collective-permute-start.26 = (bf16[4,16,2048]{2,1,0:T(8,128)(2,1)S(1)}, bf16[4,16,2048]{2,1,0:T(8,128)(2,1)S(1)}, u32[]{:S(2)}, u32[]{:S(2)}) collective-permute-start(bf16[4,16,2048]{2,1,0:T(8,128)(2,1)S(1)} %get-tuple-element.68), channel_id=1, source_target_pairs={{0,7},{1,2},{2,1},{3,4},{4,3},{5,6},{6,5},{7,0},{8,15},{9,10},{10,... | collective-permute-start | bytes 786440 | tf_op jit(solution)/shard_map/ppermute | solution.py:28
  148.0 8.6 %collective-permute-start.25 = (bf16[4,16,2048]{2,1,0:T(8,128)(2,1)}, bf16[4,16,2048]{2,1,0:T(8,128)(2,1)}, u32[]{:S(2)}, u32[]{:S(2)}) collective-permute-start(bf16[4,16,2048]{2,1,0:T(8,128)(2,1)} %get-tuple-element.67), channel_id=1, source_target_pairs={{0,1},{1,0},{2,3},{3,2},{4,5},{5,4},{6,7},{7,6},{8,9},{9,8},{10,11... | collective-permute-start | bytes 786440 | tf_op jit(solution)/shard_map/ppermute | solution.py:16
  151.6 10.9 %collective-permute-start.32 = (bf16[2,4,128,256]{3,2,0,1:T(8,128)(2,1)}, bf16[2,4,128,256]{3,2,0,1:T(8,128)(2,1)}, u32[]{:S(2)}, u32[]{:S(2)}) collective-permute-start(bf16[2,4,128,256]{3,2,0,1:T(8,128)(2,1)} %get-tuple-element.56), channel_id=1, source_target_pairs={{0,16},{16,0},{1,17},{17,1},{2,18},{18,2},{3,19},{19,3},{4,20},{20... | collective-permute-start | bytes 1572872 | tf_op jit(solution)/shard_map/ppermute | solution.py:16
  157.6 11.9 %collective-permute-start.28 = (bf16[4,16,4096]{2,1,0:T(8,128)(2,1)S(1)}, bf16[4,16,4096]{2,1,0:T(8,128)(2,1)S(1)}, u32[]{:S(2)}, u32[]{:S(2)}) collective-permute-start(bf16[4,16,4096]{2,1,0:T(8,128)(2,1)S(1)} %pad_maximum_fusion.5), channel_id=1, source_target_pairs={{0,8},{8,0},{1,9},{9,1},{2,10},{10,2},{3,11},{11,3},{4,12},{12,4},... | collective-permute-start | bytes 1572872 | tf_op jit(solution)/shard_map/ppermute | solution.py:16
  162.5 7.9 %copy-start.6 = (bf16[448,4096]{1,0:T(8,128)(2,1)S(1)}, bf16[448,4096]{1,0:T(8,128)(2,1)}, u32[]{:S(2)}) copy-start(bf16[448,4096]{1,0:T(8,128)(2,1)} %param.13) | copy-start | bytes 11010052
  175.1 35.7 %copy-start = (bf16[256,2,448]{0,2,1:T(8,128)(2,1)S(1)}, bf16[256,2,448]{0,2,1:T(8,128)(2,1)}, u32[]{:S(2)}) copy-start(bf16[256,2,448]{0,2,1:T(8,128)(2,1)} %param.14) | copy-start | bytes 1376260
  175.1 18.8 %collective-permute-start.34 = (bf16[896,128]{1,0:T(8,128)(2,1)S(1)}, bf16[896,128]{1,0:T(8,128)(2,1)S(1)}, u32[]{:S(2)}, u32[]{:S(2)}) collective-permute-start(bf16[896,128]{1,0:T(8,128)(2,1)S(1)} %pad_maximum_fusion.10), channel_id=1, source_target_pairs={{0,128},{128,0},{1,129},{129,1},{2,130},{130,2},{3,131},{131,3},{4... | collective-permute-start | bytes 688136 | tf_op jit(solution)/shard_map/ppermute | solution.py:16
  189.2 20.1 %collective-permute-start.33 = (bf16[4,896,128]{2,1,0:T(8,128)(2,1)S(1)}, bf16[4,896,128]{2,1,0:T(8,128)(2,1)}, u32[]{:S(2)}, u32[]{:S(2)}) collective-permute-start(bf16[4,896,128]{2,1,0:T(8,128)(2,1)S(1)} %bitcast.151), channel_id=1, source_target_pairs={{0,16},{16,0},{1,17},{17,1},{2,18},{18,2},{3,19},{19,3},{4,20},{20... | collective-permute-start | bytes 2752520 | tf_op jit(solution)/shard_map/ppermute | solution.py:16
  206.7 4.1 %collective-permute-start.35 = (bf16[4,896,128]{2,1,0:T(8,128)(2,1)S(1)}, bf16[4,896,128]{2,1,0:T(8,128)(2,1)}, u32[]{:S(2)}, u32[]{:S(2)}) collective-permute-start(bf16[4,896,128]{2,1,0:T(8,128)(2,1)S(1)} %bitcast.153), channel_id=1, source_target_pairs={{0,16},{16,0},{1,17},{17,1},{2,18},{18,2},{3,19},{19,3},{4,20},{20... | collective-permute-start | bytes 2752520 | tf_op jit(solution)/shard_map/ppermute | solution.py:16
  210.8 1.0 copy-start.4
  216.1 1.0 copy-start.2
  241.2 1.2 copy-start.3
Sparse Core Ops, SparseCore 0:
  19.1 40.2 all-gather.3

commit v2 on v1

--- a/solution.py
+++ b/solution.py
@@ -30,7 +30,9 @@
 
 def by_pair(value):
     at = lax.axis_index("z") % 4
-    return jnp.where((at == 1) | (at == 2), value[jnp.array([1, 0, 3, 2])], value[::-1])
+    pairs = value.reshape(2, 2, *value.shape[1:])
+    turned = jnp.where((at == 1) | (at == 2), lax.rev(pairs, (1,)), lax.rev(pairs, (0, 1)))
+    return turned.reshape(value.shape)
 
 
 def gather_even(block):
@@ -45,6 +47,19 @@
 
 def gather_x(even, odd):
     return jnp.concatenate([even, odd, swap(even, "x_lo"), swap(odd, "x_lo")], 0)
+
+
+def gather_both(block):
+    half = block.shape[1] // 2
+    rest = [swap(block, "z", d) for d in (2, 4, 6)]
+    across = swap(block, "x_lo")[None]
+    near = jnp.stack([block] + rest)
+    across = jnp.concatenate([across, swap(jnp.stack(rest), "x_lo")], 0)
+    left, right = [], []
+    for even in (near, across):
+        left += [even[..., :half], swap(even[..., :half], "z")]
+        right += [even[..., half:], by_pair(neighbour(even[..., half:]))]
+    return [jnp.concatenate(pieces, 0).reshape(-1, half) for pieces in (left, right)]
 
 
 def fold_x(partial):
@@ -206,7 +221,7 @@
 
     both = jnp.stack([cut(group_rows, x_hi * 8, 8), swap(cut(group_rows, 8 - x_hi * 8, 8), "x_hi")])
 
-    output_part, both, *far = lax.optimization_barrier((output_part, both, *far))
+    near, both, *far = lax.optimization_barrier((near, both, *far))
     output_fold = fold_x(output_part)
 
     def halves(value):
@@ -244,7 +259,7 @@
     output_sum, tangent_sum = sums[: targets.shape[0]], sums[targets.shape[0] :]
     error_rows = ((output_sum - targets.astype(F32)) / token_total).astype(BF)
     tangent_error = (tangent_sum / token_total).astype(BF)
-    errors = jnp.concatenate([error_rows, tangent_error], 0)
+    errors = jnp.concatenate([error_rows, tangent_error], 1)
     errors, both = lax.optimization_barrier((errors, both))
     own_columns = jnp.stack(
         [cut(both, y_at * 2, 2)] + [swap(cut(both, (y_at ^ d) * 2, 2), "y", d) for d in range(1, 4)], 1
@@ -252,9 +267,9 @@
     own_columns = jnp.stack(
         [cut(own_columns, core, 1), swap(cut(own_columns, 1 - core, 1), "core")], 1
     ).reshape(16, count, own_rows)
-    errors = gather_x(*gather_z(gather_even(errors))).reshape(16, 2, -1, width)
-    back_error = dot(down_weight, errors[:, 0].reshape(-1, width), ((1,), (1,)))
-    back_tangent = dot(down_weight, errors[:, 1].reshape(-1, width), ((1,), (1,)))
+    error_rows, tangent_error = gather_both(errors)
+    back_error = dot(down_weight, error_rows, ((1,), (1,)))
+    back_tangent = dot(down_weight, tangent_error, ((1,), (1,)))
 
     grad_gate = back_tangent * up_pre * silu_slope + back_error * (
         tangent_up * silu_slope + up_pre * silu_curve * tangent_gate

time: 252 us -> 239 us (0.948)
  waiting for transfers between devices: 59.6 us -> 75.3 us
  local copies, waits for them, and re-layouts: 16.9 us -> 6.07 us
  other arithmetic: 11.5 us -> 5.48 us
  starting transfers between devices: 70.7 us -> 65.3 us
  blocking collectives: 49.9 us -> 45.7 us
    ppermute x3 -> x4, waiting for transfers between devices: 3.96 us -> 12.5 us  [neighbour(): lax.ppermute(value, 'z', [(i, (i + 1) % 8 if i % 2 else (i - 1) % 8) for...]
    ppermute x33 -> x34, waiting for transfers between devices: 55.6 us -> 62.7 us  [swap(): return lax.ppermute(value, axis, [(i, i ^ step) for i in range(size)])]
    unnamed x41 -> x36, local copies, waits for them, and re-layouts: 9.29 us -> 3.24 us
    ppermute x33 -> x34, starting transfers between devices: 63.4 us -> 58.5 us  [swap(): return lax.ppermute(value, axis, [(i, i ^ step) for i in range(size)])]
    ppermute x3 -> x4, starting transfers between devices: 7.34 us -> 6.82 us  [neighbour(): lax.ppermute(value, 'z', [(i, (i + 1) % 8 if i % 2 else (i - 1) % 8) for...]
  transfers between devices with their start and end apart: 37 -> 39, of which waited for: 16 -> 20; matrix products, arithmetic and copies ran while one was open for 10% -> 7% of each run, Pallas kernels for 3% -> 3%
where the time goes in v2:
time: 239 us; the launch traced here: 238 us
  waiting for transfers between devices  75.3 us (32%)
  starting transfers between devices  65.3 us (27%)
  blocking collectives  45.7 us (19%)
  between operations  15.3 us (6%)
  Pallas kernels  13.6 us (6%)
  matrix products  11.2 us (5%)
  local copies, waits for them, and re-layouts  6.07 us (3%)
  other arithmetic  5.48 us (2%)
    ppermute x34, waiting for transfers between devices, swap(): return lax.ppermute(value, axis, [(i, i ^ step) for i in range(size)])  62.7 us
    ppermute x34, starting transfers between devices, swap(): return lax.ppermute(value, axis, [(i, i ^ step) for i in range(size)])  58.5 us
    all_gather x2, blocking collectives, per_device(): piece = lax.all_gather(piece, 'y')  23.8 us
    all_to_all x2, blocking collectives, per_device(): lax.all_to_all(jnp.broadcast_to(sums[None], (size, 8, 128)), axes, 0, 0,...  22 us
    ppermute x4, waiting for transfers between devices, neighbour(): lax.ppermute(value, 'z', [(i, (i + 1) % 8 if i % 2 else (i - 1) % 8) for...  12.5 us
    dot_general x5, matrix products, dot(): return lax.dot_general(a, b, (dims, ((), ())), preferred_element_type=F32)  11.2 us
    pallas_call x2, Pallas kernels, tangent_call(): pl.pallas_call(lambda *refs: tangent_kernel(first, *refs), out_shape=out_...  7.07 us
    ppermute x4, starting transfers between devices, neighbour(): lax.ppermute(value, 'z', [(i, (i + 1) % 8 if i % 2 else (i - 1) % 8) for...  6.82 us
  transfers between devices with their start and end apart: 39, of which 20 were waited for; matrix products, arithmetic and copies ran while one was open for 7% of the time, Pallas kernels for 3%

profile of v2, /device:TPU:1, one launch (start us, length us, event | category | flops | bytes accessed | tf_op | source)
XLA Modules:
  0.0 238.0 jit_solution(1492792456798550042)
XLA Ops:
  7.2 3.9 %collective-permute-start = (bf16[8,4096]{1,0:T(8,128)(2,1)}, bf16[8,4096]{1,0:T(8,128)(2,1)S(1)}, u32[]{:S(2)}, u32[]{:S(2)}) collective-permute-start(bf16[8,4096]{1,0:T(8,128)(2,1)} %param.7), channel_id=1, source_target_pairs={{0,2},{1,3},{2,0},{3,1},{4,6},{5,7},{6,4},{7,5},{8,10},{9,11},{10,... | collective-permute-start | bytes 196616 | tf_op jit(solution)/shard_map/ppermute | solution.py:16
  11.1 5.1 %collective-permute-start.1 = (bf16[8,4096]{1,0:T(8,128)(2,1)}, bf16[8,4096]{1,0:T(8,128)(2,1)S(1)}, u32[]{:S(2)}, u32[]{:S(2)}) collective-permute-start(bf16[8,4096]{1,0:T(8,128)(2,1)} %param.7), channel_id=1, source_target_pairs={{0,4},{1,5},{2,6},{3,7},{4,0},{5,1},{6,2},{7,3},{8,12},{9,13},{10,... | collective-permute-start | bytes 196616 | tf_op jit(solution)/shard_map/ppermute | solution.py:16
  16.2 2.7 %collective-permute-start.3 = (bf16[896,256]{1,0:T(8,128)(2,1)}, bf16[896,256]{1,0:T(8,128)(2,1)S(1)}, u32[]{:S(2)}, u32[]{:S(2)}) collective-permute-start(bf16[896,256]{1,0:T(8,128)(2,1)} %bitcast.142), channel_id=1, source_target_pairs={{0,128},{128,0},{1,129},{129,1},{2,130},{130,2},{3,131},{131,3},{4... | collective-permute-start | bytes 1376264 | tf_op jit(solution)/shard_map/ppermute | solution.py:16
  19.2 2.8 %collective-permute-done.2 = bf16[8,4096]{1,0:T(8,128)(2,1)S(1)} collective-permute-done((bf16[8,4096]{1,0:T(8,128)(2,1)}, bf16[8,4096]{1,0:T(8,128)(2,1)S(1)}, u32[]{:S(2)}, u32[]{:S(2)}) %collective-permute-start.2) | collective-permute-done | bytes 65568 | tf_op jit(solution)/shard_map/ppermute | solution.py:16
  22.0 0.9 pad_maximum_fusion.9
  22.9 5.8 %collective-permute-done.3 = bf16[896,256]{1,0:T(8,128)(2,1)S(1)} collective-permute-done((bf16[896,256]{1,0:T(8,128)(2,1)}, bf16[896,256]{1,0:T(8,128)(2,1)S(1)}, u32[]{:S(2)}, u32[]{:S(2)}) %collective-permute-start.3) | collective-permute-done | bytes 458784 | tf_op jit(solution)/shard_map/ppermute | solution.py:16
  28.7 1.2 collective-permute-start.6
  30.0 2.9 %collective-permute-start.5 = (bf16[4,8,2048]{2,1,0:T(8,128)(2,1)S(1)}, bf16[4,8,2048]{2,1,0:T(8,128)(2,1)S(1)}, u32[]{:S(2)}, u32[]{:S(2)}) collective-permute-start(bf16[4,8,2048]{2,1,0:T(8,128)(2,1)S(1)} %get-tuple-element.83), channel_id=1, source_target_pairs={{0,7},{1,2},{2,1},{3,4},{4,3},{5,6},{6,5},{7,0},{8,15},{9,10},{10,... | collective-permute-start | bytes 393224 | tf_op jit(solution)/shard_map/ppermute | solution.py:28
  33.0 1.4 collective-permute-start.10
  34.3 1.9 collective-permute-start.12
  36.3 0.8 collective-permute-done.4
  37.5 6.8 %collective-permute-done.10 = bf16[448,256]{1,0:T(8,128)(2,1)S(1)} collective-permute-done((bf16[448,256]{1,0:T(8,128)(2,1)S(1)}, bf16[448,256]{1,0:T(8,128)(2,1)S(1)}, u32[]{:S(2)}, u32[]{:S(2)}) %collective-permute-start.10) | collective-permute-done | bytes 229408 | tf_op jit(solution)/shard_map/ppermute | solution.py:16
  44.3 3.0 %collective-permute-start.11 = (bf16[2,448,256]{2,1,0:T(8,128)(2,1)S(1)}, bf16[2,448,256]{2,1,0:T(8,128)(2,1)}, u32[]{:S(2)}, u32[]{:S(2)}) collective-permute-start(bf16[2,448,256]{2,1,0:T(8,128)(2,1)S(1)} %pad_maximum_fusion.5.refs_3_), channel_id=1, source_target_pairs={{0,96},{32,64},{64,32},{96,0},{1,97},{33,65},{65,33},{97,1},{2,98}... | collective-permute-start | bytes 1376264 | tf_op jit(solution)/shard_map/ppermute | solution.py:16
  47.7 4.3 %collective-permute-start.8 = (bf16[128,4096]{1,0:T(8,128)(2,1)S(1)}, bf16[128,4096]{1,0:T(8,128)(2,1)S(1)}, u32[]{:S(2)}, u32[]{:S(2)}) collective-permute-start(bf16[128,4096]{1,0:T(8,128)(2,1)S(1)} %maximum_bitcast_fusion.refs_1_), channel_id=1, source_target_pairs={{0,16},{16,0},{1,17},{17,1},{2,18},{18,2},{3,19},{19,3},{4,20},{20... | collective-permute-start | bytes 3145736 | tf_op jit(solution)/shard_map/ppermute | solution.py:16
  52.0 1.0 dynamic-slice_bitcast_fusion.1
  53.1 2.5 %collective-permute-start.9 = (bf16[128,2048]{1,0:T(8,128)(2,1)}, bf16[128,2048]{1,0:T(8,128)(2,1)}, u32[]{:S(2)}, u32[]{:S(2)}) collective-permute-start(bf16[128,2048]{1,0:T(8,128)(2,1)} %get-tuple-element.66), channel_id=1, source_target_pairs={{0,128},{128,0},{1,129},{129,1},{2,130},{130,2},{3,131},{131,3},{4... | collective-permute-start | bytes 1572872 | tf_op jit(solution)/shard_map/ppermute | solution.py:16
  55.5 5.3 %convolution_bitcast_fusion = f32[896,128]{1,0:T(8,128)S(1)} fusion(bf16[896,4096]{1,0:T(8,128)(2,1)} %bitcast.184, bf16[4,8,4096]{2,1,0:T(8,128)(2,1)} %copy-done.16, bf16[4,8,4096]{2,1,0:T(8,128)(2,1)} %copy-done.15, bf16[4,8,2048]{2,1,0:T(8,128)(2,1)S(1)} %bitcast.157, bf16[4,8,2048]{2,1,0:T(8,128)(2,1)S(1)} %copy-done.14, ...), kind=kOutput, calls=%fused_computation.2 | convolution fusion | flops 944766976 | bytes 8847360 | tf_op jit(solution)/shard_map/dot_general | solution.py:84
  60.9 2.8 %convolution_convert_fusion.1 = bf16[128,4096]{1,0:T(8,128)(2,1)S(1)} fusion(bf16[448,4096]{1,0:T(8,128)(2,1)} %param.10, f32[896,128]{1,0:T(8,128)S(1)} %convolution_bitcast_fusion), kind=kOutput, calls=%fused_computation.1 | convolution fusion | flops 470630400 | bytes 5177344 | tf_op jit(solution)/shard_map/dot_general | solution.py:84
  63.7 1.1 fusion.41
  64.8 0.7 collective-permute-start.14
  65.6 2.8 %collective-permute-done.9 = bf16[128,2048]{1,0:T(8,128)(2,1)} collective-permute-done((bf16[128,2048]{1,0:T(8,128)(2,1)}, bf16[128,2048]{1,0:T(8,128)(2,1)}, u32[]{:S(2)}, u32[]{:S(2)}) %collective-permute-start.9) | collective-permute-done | bytes 524320 | tf_op jit(solution)/shard_map/ppermute | solution.py:16
  68.4 2.3 pad_maximum_fusion
  70.7 2.7 %shard_map.94.refs_7_ = f32[2,448,256]{2,1,0:T(8,128)S(1)} custom-call(s32[12]{0:T(128)S(1)} %stack.194.refs_0_, bf16[128,4096]{1,0:T(8,128)(2,1)S(1)} %maximum_bitcast_fusion.refs_1_, bf16[128,4096]{1,0:T(8,128)(2,1)S(1)} %collective-permute-done.8.refs_2_, bf16[4,2,448,256]{3,2,1,0:T(8,128)(2,1)S(1)} %bitcast.150), custom_call_target="tpu_custom_call" | custom-call | flops 469762048 | bytes 1835008 | tf_op jit(solution)/shard_map/pallas_call | solution.py:132
  73.4 4.4 %shard_map.95 = (f32[2,448,128]{2,1,0:T(8,128)S(1)}, f32[2,448,128]{2,1,0:T(8,128)S(1)}) custom-call(s32[12]{0:T(128)S(1)} %stack.194.refs_0_, bf16[128,4096]{1,0:T(8,128)(2,1)S(1)} %maximum_bitcast_fusion.refs_1_, bf16[128,4096]{1,0:T(8,128)(2,1)S(1)} %collective-permute-done.8.refs_2_, bf16[2,448,256]{2,1,0:T(8,128)(2,1)S(1)} %pad_maximum_fusion.5.refs_3_, ...), custom_call_target="tpu_custom_call" | custom-call | flops 469762048 | bytes 1835008 | tf_op jit(solution)/shard_map/pallas_call | solution.py:132
  77.8 0.9 collective-permute-start.15
  79.1 1.2 fusion.14
  80.6 0.8 convolution_convert_fusion
  81.5 1.6 collective-permute-start.16
  83.1 11.3 %collective-permute-done.16 = bf16[2,4,8,4096]{3,2,1,0:T(8,128)(2,1)S(1)} collective-permute-done((bf16[2,4,8,4096]{3,2,1,0:T(8,128)(2,1)S(1)}, bf16[2,4,8,4096]{3,2,1,0:T(8,128)(2,1)S(1)}, u32[]{:S(2)}, u32[]{:S(2)}) %collective-permute-start.16) | collective-permute-done | bytes 524320 | tf_op jit(solution)/shard_map/ppermute | solution.py:16
  94.6 1.6 collective-permute-start.18
  96.1 0.9 collective-permute-start.17
  97.0 5.0 %collective-permute-done.18 = bf16[4,16,2048]{2,1,0:T(8,128)(2,1)S(1)} collective-permute-done((bf16[4,16,2048]{2,1,0:T(8,128)(2,1)S(1)}, bf16[4,16,2048]{2,1,0:T(8,128)(2,1)S(1)}, u32[]{:S(2)}, u32[]{:S(2)}) %collective-permute-start.18) | collective-permute-done | bytes 262176 | tf_op jit(solution)/shard_map/ppermute | solution.py:28
  102.3 3.9 %collective-permute-start.19 = (bf16[16,4096]{1,0:T(8,128)(2,1)S(1)}, bf16[16,4096]{1,0:T(8,128)(2,1)S(1)}, u32[]{:S(2)}, u32[]{:S(2)}) collective-permute-start(bf16[16,4096]{1,0:T(8,128)(2,1)S(1)} %get-tuple-element.71), channel_id=1, source_target_pairs={{0,2},{1,3},{2,0},{3,1},{4,6},{5,7},{6,4},{7,5},{8,10},{9,11},{10,... | collective-permute-start | bytes 393224 | tf_op jit(solution)/shard_map/ppermute | solution.py:16
  106.2 2.3 collective-permute-start.20
  108.4 1.1 collective-permute-start.21
  110.0 5.0 %collective-permute-done.20 = bf16[16,4096]{1,0:T(8,128)(2,1)S(1)} collective-permute-done((bf16[16,4096]{1,0:T(8,128)(2,1)S(1)}, bf16[16,4096]{1,0:T(8,128)(2,1)S(1)}, u32[]{:S(2)}, u32[]{:S(2)}) %collective-permute-start.20) | collective-permute-done | bytes 131104 | tf_op jit(solution)/shard_map/ppermute | solution.py:16
  115.1 4.7 %collective-permute-done.21 = bf16[16,4096]{1,0:T(8,128)(2,1)S(1)} collective-permute-done((bf16[16,4096]{1,0:T(8,128)(2,1)S(1)}, bf16[16,4096]{1,0:T(8,128)(2,1)S(1)}, u32[]{:S(2)}, u32[]{:S(2)}) %collective-permute-start.21) | collective-permute-done | bytes 131104 | tf_op jit(solution)/shard_map/ppermute | solution.py:16
  119.9 4.8 %collective-permute-start.22 = (bf16[8,8192]{1,0:T(8,128)(2,1)S(1)}, bf16[8,8192]{1,0:T(8,128)(2,1)S(1)}, u32[]{:S(2)}, u32[]{:S(2)}) collective-permute-start(bf16[8,8192]{1,0:T(8,128)(2,1)S(1)} %pad_maximum_fusion.12), channel_id=1, source_target_pairs={{0,2},{1,3},{2,0},{3,1},{4,6},{5,7},{6,4},{7,5},{8,10},{9,11},{10,... | collective-permute-start | bytes 393224 | tf_op jit(solution)/shard_map/ppermute | solution.py:16
  124.7 1.8 collective-permute-start.23
  126.6 1.6 collective-permute-start.24
  129.0 7.8 %collective-permute-done.22 = bf16[8,8192]{1,0:T(8,128)(2,1)S(1)} collective-permute-done((bf16[8,8192]{1,0:T(8,128)(2,1)S(1)}, bf16[8,8192]{1,0:T(8,128)(2,1)S(1)}, u32[]{:S(2)}, u32[]{:S(2)}) %collective-permute-start.22) | collective-permute-done | bytes 131104 | tf_op jit(solution)/shard_map/ppermute | solution.py:16
  136.8 0.8 collective-permute-done.23
  137.9 1.8 collective-permute-start.27
  139.7 2.2 collective-permute-start.25
  142.0 3.8 %collective-permute-done.32 = bf16[2,128,512]{2,1,0:T(8,128)(2,1)S(1)} collective-permute-done((bf16[2,128,512]{2,1,0:T(8,128)(2,1)S(1)}, bf16[2,128,512]{2,1,0:T(8,128)(2,1)S(1)}, u32[]{:S(2)}, u32[]{:S(2)}) %collective-permute-start.32) | collective-permute-done | bytes 262176 | tf_op jit(solution)/shard_map/ppermute | solution.py:16
  145.7 6.4 %collective-permute-done.33 = bf16[2,128,512]{2,1,0:T(8,128)(2,1)S(1)} collective-permute-done((bf16[2,128,512]{2,1,0:T(8,128)(2,1)S(1)}, bf16[2,128,512]{2,1,0:T(8,128)(2,1)S(1)}, u32[]{:S(2)}, u32[]{:S(2)}) %collective-permute-start.33) | collective-permute-done | bytes 262176 | tf_op jit(solution)/shard_map/ppermute | solution.py:16
  152.4 0.6 collective-permute-start.34
  153.3 1.2 collective-permute-done.34
  154.7 7.5 %collective-permute-done.28 = bf16[4,8,4096]{2,1,0:T(8,128)(2,1)S(1)} collective-permute-done((bf16[4,8,4096]{2,1,0:T(8,128)(2,1)S(1)}, bf16[4,8,4096]{2,1,0:T(8,128)(2,1)S(1)}, u32[]{:S(2)}, u32[]{:S(2)}) %collective-permute-start.28) | collective-permute-done | bytes 262176 | tf_op jit(solution)/shard_map/ppermute | solution.py:28
  162.3 1.1 convolution_bitcast_fusion.2
  163.4 1.2 fusion.29
  164.6 2.1 collective-permute-start.36
  166.8 11.0 %all-gather = bf16[3584,128]{1,0:T(8,128)(2,1)S(1)} all-gather(bf16[896,128]{1,0:T(8,128)(2,1)S(1)} %pad_maximum_fusion.11), channel_id=2, replica_groups=mesh['x_hi'=2,'y'=4,'core'=2,'x_lo'=2,'z'=8] {'y'}, dimensions={0}, use_global_device_ids=true | all-gather | bytes 1146880 | tf_op jit(solution)/shard_map/all_gather | solution.py:283
  177.7 4.9 %collective-permute-start.35 = (bf16[4,896,128]{2,1,0:T(8,128)(2,1)S(1)}, bf16[4,896,128]{2,1,0:T(8,128)(2,1)}, u32[]{:S(2)}, u32[]{:S(2)}) collective-permute-start(bf16[4,896,128]{2,1,0:T(8,128)(2,1)S(1)} %bitcast.146), channel_id=1, source_target_pairs={{0,16},{16,0},{1,17},{17,1},{2,18},{18,2},{3,19},{19,3},{4,20},{20... | collective-permute-start | bytes 2752520 | tf_op jit(solution)/shard_map/ppermute | solution.py:16
  182.6 12.8 %all-gather.1 = bf16[3584,128]{1,0:T(8,128)(2,1)S(1)} all-gather(bf16[896,128]{1,0:T(8,128)(2,1)S(1)} %collective-permute-done.36), channel_id=3, replica_groups=mesh['x_hi'=2,'y'=4,'core'=2,'x_lo'=2,'z'=8] {'y'}, dimensions={0}, use_global_device_ids=true | all-gather | bytes 1146880 | tf_op jit(solution)/shard_map/all_gather | solution.py:283
  195.4 2.1 collective-permute-start.37
  198.3 1.5 collective-permute-done.37.refs_3_
  199.8 1.0 copy-done.4
  200.8 4.3 %shard_map.97 = (f32[896,256]{1,0:T(8,128)S(1)}, f32[8,128]{1,0:T(8,128)S(1)}) custom-call(s32[16]{0:T(128)S(1)} %stack.185.index_ref, f32[1,1]{1,0:T(1,128)} %bitcast.140.beta_ref, bf16[16,128,256]{2,1,0:T(8,128)(2,1)S(1)} %bitcast.141, bf16[4,896,128]{2,1,0:T(8,128)(2,1)S(1)} %bitcast.147, bf16[4,896,128]{2,1,0:T(8,128)(2,1)} %collective-permute-done.35.refs_1_, ...), custom_call_target="tpu_custom_call" | custom-call | flops 1073741824 | bytes 7340032 | tf_op jit(solution)/shard_map/pallas_call | solution.py:288
  205.2 1.0 copy-done.2
  206.1 10.0 %all_to_all.10 = f32[8,8,128]{2,1,0:T(8,128)S(1)} all-to-all(f32[8,8,128]{2,1,0:T(8,128)S(1)} %broadcast_in_dim.7), channel_id=1, replica_groups=mesh['x_hi'=2,'y'=4,'core'=2,'x_lo'=2,'z'=8] {'z'}, dimensions={0} | all-to-all | bytes 65536 | tf_op jit(solution)/shard_map/all_to_all | solution.py:313
  216.1 12.0 %all_to_all.11.refs_0_ = f32[32,8,128]{2,1,0:T(8,128)S(1)} all-to-all(f32[32,8,128]{2,1,0:T(8,128)S(1)} %broadcast_in_dim.8), channel_id=1, replica_groups=mesh['x_hi'=2,'y'=4,'core'=2,'x_lo'=2,'z'=8] {'x_hi','y','core','x_lo'}, dimensions={0} | all-to-all | bytes 262144 | tf_op jit(solution)/shard_map/all_to_all | solution.py:313
  228.1 1.2 copy-done.3
  229.3 1.9 shard_map.98
  (104 shorter events, 5.1 us)
Async XLA Ops:
  7.2 53.7 %all-gather.4.cloned.1.call-start = ((), (), s32[]{:S(2)}) async-start(), calls=%async_computation.2 | async-start | bytes 2293760 | tf_op jit(solution)/shard_map/all_gather | solution.py:203
  7.2 11.8 %collective-permute-start = (bf16[8,4096]{1,0:T(8,128)(2,1)}, bf16[8,4096]{1,0:T(8,128)(2,1)S(1)}, u32[]{:S(2)}, u32[]{:S(2)}) collective-permute-start(bf16[8,4096]{1,0:T(8,128)(2,1)} %param.7), channel_id=1, source_target_pairs={{0,2},{1,3},{2,0},{3,1},{4,6},{5,7},{6,4},{7,5},{8,10},{9,11},{10,... | collective-permute-start | bytes 196616 | tf_op jit(solution)/shard_map/ppermute | solution.py:16
  11.1 8.1 %collective-permute-start.1 = (bf16[8,4096]{1,0:T(8,128)(2,1)}, bf16[8,4096]{1,0:T(8,128)(2,1)S(1)}, u32[]{:S(2)}, u32[]{:S(2)}) collective-permute-start(bf16[8,4096]{1,0:T(8,128)(2,1)} %param.7), channel_id=1, source_target_pairs={{0,4},{1,5},{2,6},{3,7},{4,0},{5,1},{6,2},{7,3},{8,12},{9,13},{10,... | collective-permute-start | bytes 196616 | tf_op jit(solution)/shard_map/ppermute | solution.py:16
  16.2 5.8 %collective-permute-start.2 = (bf16[8,4096]{1,0:T(8,128)(2,1)}, bf16[8,4096]{1,0:T(8,128)(2,1)S(1)}, u32[]{:S(2)}, u32[]{:S(2)}) collective-permute-start(bf16[8,4096]{1,0:T(8,128)(2,1)} %param.7), channel_id=1, source_target_pairs={{0,6},{1,7},{2,4},{3,5},{4,2},{5,3},{6,0},{7,1},{8,14},{9,15},{10,... | collective-permute-start | bytes 196616 | tf_op jit(solution)/shard_map/ppermute | solution.py:16
  16.2 12.5 %collective-permute-start.3 = (bf16[896,256]{1,0:T(8,128)(2,1)}, bf16[896,256]{1,0:T(8,128)(2,1)S(1)}, u32[]{:S(2)}, u32[]{:S(2)}) collective-permute-start(bf16[896,256]{1,0:T(8,128)(2,1)} %bitcast.142), channel_id=1, source_target_pairs={{0,128},{128,0},{1,129},{129,1},{2,130},{130,2},{3,131},{131,3},{4... | collective-permute-start | bytes 1376264 | tf_op jit(solution)/shard_map/ppermute | solution.py:16
  22.9 24.6 %copy-start.8 = (bf16[4,8,4096]{2,1,0:T(8,128)(2,1)}, bf16[4,8,4096]{2,1,0:T(8,128)(2,1)S(1)}, u32[]{:S(2)}) copy-start(bf16[4,8,4096]{2,1,0:T(8,128)(2,1)S(1)} %pad_maximum_fusion.9) | copy-start | bytes 786436
  28.7 18.8 %collective-permute-start.6 = (bf16[4,8,4096]{2,1,0:T(8,128)(2,1)S(1)}, bf16[4,8,4096]{2,1,0:T(8,128)(2,1)S(1)}, u32[]{:S(2)}, u32[]{:S(2)}) collective-permute-start(bf16[4,8,4096]{2,1,0:T(8,128)(2,1)S(1)} %pad_maximum_fusion.9), channel_id=1, source_target_pairs={{0,8},{8,0},{1,9},{9,1},{2,10},{10,2},{3,11},{11,3},{4,12},{12,4},... | collective-permute-start | bytes 786440 | tf_op jit(solution)/shard_map/ppermute | solution.py:16
  30.0 6.3 %collective-permute-start.5 = (bf16[4,8,2048]{2,1,0:T(8,128)(2,1)S(1)}, bf16[4,8,2048]{2,1,0:T(8,128)(2,1)S(1)}, u32[]{:S(2)}, u32[]{:S(2)}) collective-permute-start(bf16[4,8,2048]{2,1,0:T(8,128)(2,1)S(1)} %get-tuple-element.83), channel_id=1, source_target_pairs={{0,7},{1,2},{2,1},{3,4},{4,3},{5,6},{6,5},{7,0},{8,15},{9,10},{10,... | collective-permute-start | bytes 393224 | tf_op jit(solution)/shard_map/ppermute | solution.py:28
  32.9 4.2 %collective-permute-start.4 = (bf16[4,8,2048]{2,1,0:T(8,128)(2,1)S(1)}, bf16[4,8,2048]{2,1,0:T(8,128)(2,1)S(1)}, u32[]{:S(2)}, u32[]{:S(2)}) collective-permute-start(bf16[4,8,2048]{2,1,0:T(8,128)(2,1)S(1)} %get-tuple-element.82), channel_id=1, source_target_pairs={{0,1},{1,0},{2,3},{3,2},{4,5},{5,4},{6,7},{7,6},{8,9},{9,8},{10,11... | collective-permute-start | bytes 393224 | tf_op jit(solution)/shard_map/ppermute | solution.py:16
  33.0 11.3 %collective-permute-start.10 = (bf16[448,256]{1,0:T(8,128)(2,1)S(1)}, bf16[448,256]{1,0:T(8,128)(2,1)S(1)}, u32[]{:S(2)}, u32[]{:S(2)}) collective-permute-start(bf16[448,256]{1,0:T(8,128)(2,1)S(1)} %get-tuple-element.79), channel_id=1, source_target_pairs={{0,32},{32,0},{64,96},{96,64},{1,33},{33,1},{65,97},{97,65},{2,34}... | collective-permute-start | bytes 688136 | tf_op jit(solution)/shard_map/ppermute | solution.py:16
  34.3 13.0 %collective-permute-start.12 = (bf16[448,256]{1,0:T(8,128)(2,1)S(1)}, bf16[448,256]{1,0:T(8,128)(2,1)S(1)}, u32[]{:S(2)}, u32[]{:S(2)}) collective-permute-start(bf16[448,256]{1,0:T(8,128)(2,1)S(1)} %get-tuple-element.78), channel_id=1, source_target_pairs={{0,96},{32,64},{64,32},{96,0},{1,97},{33,65},{65,33},{97,1},{2,98}... | collective-permute-start | bytes 688136 | tf_op jit(solution)/shard_map/ppermute | solution.py:16
  36.3 11.3 %copy-start.11 = (bf16[2,2,8,2048]{3,2,1,0:T(8,128)(2,1)}, bf16[2,2,8,2048]{3,2,1,0:T(8,128)(2,1)S(1)}, u32[]{:S(2)}) copy-start(bf16[2,2,8,2048]{3,2,1,0:T(8,128)(2,1)S(1)} %reverse_select_fusion.3) | copy-start | bytes 393220
  37.1 10.5 %copy-start.13 = (bf16[4,8,2048]{2,1,0:T(8,128)(2,1)}, bf16[4,8,2048]{2,1,0:T(8,128)(2,1)S(1)}, u32[]{:S(2)}) copy-start(bf16[4,8,2048]{2,1,0:T(8,128)(2,1)S(1)} %collective-permute-done.4) | copy-start | bytes 393220
  37.1 10.4 %collective-permute-start.7 = (bf16[4,8,4096]{2,1,0:T(8,128)(2,1)S(1)}, bf16[4,8,4096]{2,1,0:T(8,128)(2,1)S(1)}, u32[]{:S(2)}, u32[]{:S(2)}) collective-permute-start(bf16[4,8,4096]{2,1,0:T(8,128)(2,1)S(1)} %pad_maximum_fusion.10), channel_id=1, source_target_pairs={{0,8},{8,0},{1,9},{9,1},{2,10},{10,2},{3,11},{11,3},{4,12},{12,4},... | collective-permute-start | bytes 786440 | tf_op jit(solution)/shard_map/ppermute | solution.py:16
  44.3 26.4 %collective-permute-start.11 = (bf16[2,448,256]{2,1,0:T(8,128)(2,1)S(1)}, bf16[2,448,256]{2,1,0:T(8,128)(2,1)}, u32[]{:S(2)}, u32[]{:S(2)}) collective-permute-start(bf16[2,448,256]{2,1,0:T(8,128)(2,1)S(1)} %pad_maximum_fusion.5.refs_3_), channel_id=1, source_target_pairs={{0,96},{32,64},{64,32},{96,0},{1,97},{33,65},{65,33},{97,1},{2,98}... | collective-permute-start | bytes 1376264 | tf_op jit(solution)/shard_map/ppermute | solution.py:16
  47.4 23.3 %collective-permute-start.13 = (bf16[2,448,256]{2,1,0:T(8,128)(2,1)S(1)}, bf16[2,448,256]{2,1,0:T(8,128)(2,1)}, u32[]{:S(2)}, u32[]{:S(2)}) collective-permute-start(bf16[2,448,256]{2,1,0:T(8,128)(2,1)S(1)} %pad_maximum_fusion.6.refs_5_), channel_id=1, source_target_pairs={{0,32},{32,0},{64,96},{96,64},{1,33},{33,1},{65,97},{97,65},{2,34}... | collective-permute-start | bytes 1376264 | tf_op jit(solution)/shard_map/ppermute | solution.py:16
  47.5 8.0 %copy-start.15 = (bf16[4,8,4096]{2,1,0:T(8,128)(2,1)}, bf16[4,8,4096]{2,1,0:T(8,128)(2,1)S(1)}, u32[]{:S(2)}) copy-start(bf16[4,8,4096]{2,1,0:T(8,128)(2,1)S(1)} %collective-permute-done.6) | copy-start | bytes 786436
  47.6 7.9 %copy-start.16 = (bf16[4,8,4096]{2,1,0:T(8,128)(2,1)}, bf16[4,8,4096]{2,1,0:T(8,128)(2,1)S(1)}, u32[]{:S(2)}) copy-start(bf16[4,8,4096]{2,1,0:T(8,128)(2,1)S(1)} %collective-permute-done.7) | copy-start | bytes 786436
  47.7 7.8 %copy-start.9 = (bf16[4,8,4096]{2,1,0:T(8,128)(2,1)S(1)}, bf16[4,8,4096]{2,1,0:T(8,128)(2,1)}, u32[]{:S(2)}) copy-start(bf16[4,8,4096]{2,1,0:T(8,128)(2,1)} %copy-done.8) | copy-start | bytes 786436
  47.7 7.8 %copy-start.12 = (bf16[2,2,8,2048]{3,2,1,0:T(8,128)(2,1)S(1)}, bf16[2,2,8,2048]{3,2,1,0:T(8,128)(2,1)}, u32[]{:S(2)}) copy-start(bf16[2,2,8,2048]{3,2,1,0:T(8,128)(2,1)} %copy-done.11) | copy-start | bytes 393220
  47.7 7.8 %copy-start.14 = (bf16[4,8,2048]{2,1,0:T(8,128)(2,1)S(1)}, bf16[4,8,2048]{2,1,0:T(8,128)(2,1)}, u32[]{:S(2)}) copy-start(bf16[4,8,2048]{2,1,0:T(8,128)(2,1)} %copy-done.13) | copy-start | bytes 393220
  47.7 23.0 %collective-permute-start.8 = (bf16[128,4096]{1,0:T(8,128)(2,1)S(1)}, bf16[128,4096]{1,0:T(8,128)(2,1)S(1)}, u32[]{:S(2)}, u32[]{:S(2)}) collective-permute-start(bf16[128,4096]{1,0:T(8,128)(2,1)S(1)} %maximum_bitcast_fusion.refs_1_), channel_id=1, source_target_pairs={{0,16},{16,0},{1,17},{17,1},{2,18},{18,2},{3,19},{19,3},{4,20},{20... | collective-permute-start | bytes 3145736 | tf_op jit(solution)/shard_map/ppermute | solution.py:16
  53.1 15.4 %collective-permute-start.9 = (bf16[128,2048]{1,0:T(8,128)(2,1)}, bf16[128,2048]{1,0:T(8,128)(2,1)}, u32[]{:S(2)}, u32[]{:S(2)}) collective-permute-start(bf16[128,2048]{1,0:T(8,128)(2,1)} %get-tuple-element.66), channel_id=1, source_target_pairs={{0,128},{128,0},{1,129},{129,1},{2,130},{130,2},{3,131},{131,3},{4... | collective-permute-start | bytes 1572872 | tf_op jit(solution)/shard_map/ppermute | solution.py:16
  64.8 14.3 %collective-permute-start.14 = (bf16[2,4,8,4096]{3,2,1,0:T(8,128)(2,1)}, bf16[2,4,8,4096]{3,2,1,0:T(8,128)(2,1)}, u32[]{:S(2)}, u32[]{:S(2)}) collective-permute-start(bf16[2,4,8,4096]{3,2,1,0:T(8,128)(2,1)} %bitcast.46), channel_id=1, source_target_pairs={{0,8},{8,0},{1,9},{9,1},{2,10},{10,2},{3,11},{11,3},{4,12},{12,4},... | collective-permute-start | bytes 1572872 | tf_op jit(solution)/shard_map/ppermute | solution.py:16
  65.6 5.1 %copy-start.1 = (bf16[4,896,256]{2,1,0:T(8,128)(2,1)S(1)}, bf16[4,896,256]{2,1,0:T(8,128)(2,1)}, u32[]{:S(2)}) copy-start(bf16[4,896,256]{2,1,0:T(8,128)(2,1)} %all-gather.4.cloned.1.call-done) | copy-start | bytes 5505028
  73.4 5.7 %copy-start.10 = (bf16[64,4096]{1,0:T(8,128)(2,1)S(1)}, bf16[64,4096]{1,0:T(8,128)(2,1)}, u32[]{:S(2)}) copy-start(bf16[64,4096]{1,0:T(8,128)(2,1)} %get-tuple-element.64) | copy-start | bytes 1572868
  73.4 7.2 %copy-start.5 = (bf16[448,4096]{1,0:T(8,128)(2,1)S(1)}, bf16[448,4096]{1,0:T(8,128)(2,1)}, u32[]{:S(2)}) copy-start(bf16[448,4096]{1,0:T(8,128)(2,1)} %param.10) | copy-start | bytes 11010052
  77.8 2.4 %collective-permute-start.15 = (f32[2,448,128]{2,1,0:T(8,128)S(1)}, f32[2,448,128]{2,1,0:T(8,128)S(1)}, u32[]{:S(2)}, u32[]{:S(2)}) collective-permute-start(f32[2,448,128]{2,1,0:T(8,128)S(1)} %get-tuple-element.40), channel_id=1, source_target_pairs={{0,16},{16,0},{1,17},{17,1},{2,18},{18,2},{3,19},{19,3},{4,20},{20... | collective-permute-start | bytes 1376264 | tf_op jit(solution)/shard_map/ppermute | solution.py:16
  81.5 12.9 %collective-permute-start.16 = (bf16[2,4,8,4096]{3,2,1,0:T(8,128)(2,1)S(1)}, bf16[2,4,8,4096]{3,2,1,0:T(8,128)(2,1)S(1)}, u32[]{:S(2)}, u32[]{:S(2)}) collective-permute-start(bf16[2,4,8,4096]{3,2,1,0:T(8,128)(2,1)S(1)} %bitcast.160), channel_id=1, source_target_pairs={{0,8},{8,0},{1,9},{9,1},{2,10},{10,2},{3,11},{11,3},{4,12},{12,4},... | collective-permute-start | bytes 1572872 | tf_op jit(solution)/shard_map/ppermute | solution.py:16
  94.6 7.5 %collective-permute-start.18 = (bf16[4,16,2048]{2,1,0:T(8,128)(2,1)S(1)}, bf16[4,16,2048]{2,1,0:T(8,128)(2,1)S(1)}, u32[]{:S(2)}, u32[]{:S(2)}) collective-permute-start(bf16[4,16,2048]{2,1,0:T(8,128)(2,1)S(1)} %get-tuple-element.75), channel_id=1, source_target_pairs={{0,7},{1,2},{2,1},{3,4},{4,3},{5,6},{6,5},{7,0},{8,15},{9,10},{10,... | collective-permute-start | bytes 786440 | tf_op jit(solution)/shard_map/ppermute | solution.py:28
  96.1 6.0 %collective-permute-start.17 = (bf16[4,16,2048]{2,1,0:T(8,128)(2,1)S(1)}, bf16[4,16,2048]{2,1,0:T(8,128)(2,1)S(1)}, u32[]{:S(2)}, u32[]{:S(2)}) collective-permute-start(bf16[4,16,2048]{2,1,0:T(8,128)(2,1)S(1)} %get-tuple-element.74), channel_id=1, source_target_pairs={{0,1},{1,0},{2,3},{3,2},{4,5},{5,4},{6,7},{7,6},{8,9},{9,8},{10,11... | collective-permute-start | bytes 786440 | tf_op jit(solution)/shard_map/ppermute | solution.py:16
  102.1 17.8 %copy-start.17 = (bf16[8,4096]{1,0:T(8,128)(2,1)S(1)}, bf16[8,4096]{1,0:T(8,128)(2,1)}, u32[]{:S(2)}) copy-start(bf16[8,4096]{1,0:T(8,128)(2,1)} %param.8) | copy-start | bytes 196612
  102.1 26.4 %copy-start.7 = (bf16[2,128,2048]{2,1,0:T(8,128)(2,1)S(1)}, bf16[2,128,2048]{2,1,0:T(8,128)(2,1)}, u32[]{:S(2)}) copy-start(bf16[2,128,2048]{2,1,0:T(8,128)(2,1)} %pad_maximum_fusion) | copy-start | bytes 3145732
  102.3 7.7 %collective-permute-start.19 = (bf16[16,4096]{1,0:T(8,128)(2,1)S(1)}, bf16[16,4096]{1,0:T(8,128)(2,1)S(1)}, u32[]{:S(2)}, u32[]{:S(2)}) collective-permute-start(bf16[16,4096]{1,0:T(8,128)(2,1)S(1)} %get-tuple-element.71), channel_id=1, source_target_pairs={{0,2},{1,3},{2,0},{3,1},{4,6},{5,7},{6,4},{7,5},{8,10},{9,11},{10,... | collective-permute-start | bytes 393224 | tf_op jit(solution)/shard_map/ppermute | solution.py:16
  106.2 8.9 %collective-permute-start.20 = (bf16[16,4096]{1,0:T(8,128)(2,1)S(1)}, bf16[16,4096]{1,0:T(8,128)(2,1)S(1)}, u32[]{:S(2)}, u32[]{:S(2)}) collective-permute-start(bf16[16,4096]{1,0:T(8,128)(2,1)S(1)} %get-tuple-element.73), channel_id=1, source_target_pairs={{0,4},{1,5},{2,6},{3,7},{4,0},{5,1},{6,2},{7,3},{8,12},{9,13},{10,... | collective-permute-start | bytes 393224 | tf_op jit(solution)/shard_map/ppermute | solution.py:16
  108.4 11.4 %collective-permute-start.21 = (bf16[16,4096]{1,0:T(8,128)(2,1)S(1)}, bf16[16,4096]{1,0:T(8,128)(2,1)S(1)}, u32[]{:S(2)}, u32[]{:S(2)}) collective-permute-start(bf16[16,4096]{1,0:T(8,128)(2,1)S(1)} %get-tuple-element.72), channel_id=1, source_target_pairs={{0,6},{1,7},{2,4},{3,5},{4,2},{5,3},{6,0},{7,1},{8,14},{9,15},{10,... | collective-permute-start | bytes 393224 | tf_op jit(solution)/shard_map/ppermute | solution.py:16
  119.9 16.9 %collective-permute-start.22 = (bf16[8,8192]{1,0:T(8,128)(2,1)S(1)}, bf16[8,8192]{1,0:T(8,128)(2,1)S(1)}, u32[]{:S(2)}, u32[]{:S(2)}) collective-permute-start(bf16[8,8192]{1,0:T(8,128)(2,1)S(1)} %pad_maximum_fusion.12), channel_id=1, source_target_pairs={{0,2},{1,3},{2,0},{3,1},{4,6},{5,7},{6,4},{7,5},{8,10},{9,11},{10,... | collective-permute-start | bytes 393224 | tf_op jit(solution)/shard_map/ppermute | solution.py:16
  124.7 12.9 %collective-permute-start.23 = (bf16[8,8192]{1,0:T(8,128)(2,1)S(1)}, bf16[8,8192]{1,0:T(8,128)(2,1)S(1)}, u32[]{:S(2)}, u32[]{:S(2)}) collective-permute-start(bf16[8,8192]{1,0:T(8,128)(2,1)S(1)} %pad_maximum_fusion.12), channel_id=1, source_target_pairs={{0,4},{1,5},{2,6},{3,7},{4,0},{5,1},{6,2},{7,3},{8,12},{9,13},{10,... | collective-permute-start | bytes 393224 | tf_op jit(solution)/shard_map/ppermute | solution.py:16
  126.6 11.2 %collective-permute-start.24 = (bf16[8,8192]{1,0:T(8,128)(2,1)S(1)}, bf16[8,8192]{1,0:T(8,128)(2,1)S(1)}, u32[]{:S(2)}, u32[]{:S(2)}) collective-permute-start(bf16[8,8192]{1,0:T(8,128)(2,1)S(1)} %pad_maximum_fusion.12), channel_id=1, source_target_pairs={{0,6},{1,7},{2,4},{3,5},{4,2},{5,3},{6,0},{7,1},{8,14},{9,15},{10,... | collective-permute-start | bytes 393224 | tf_op jit(solution)/shard_map/ppermute | solution.py:16
  128.1 24.8 %collective-permute-start.26 = (bf16[8,8192]{1,0:T(8,128)(2,1)S(1)}, bf16[8,8192]{1,0:T(8,128)(2,1)S(1)}, u32[]{:S(2)}, u32[]{:S(2)}) collective-permute-start(bf16[8,8192]{1,0:T(8,128)(2,1)S(1)} %pad_maximum_fusion.12), channel_id=1, source_target_pairs={{0,8},{8,0},{1,9},{9,1},{2,10},{10,2},{3,11},{11,3},{4,12},{12,4},... | collective-permute-start | bytes 393224 | tf_op jit(solution)/shard_map/ppermute | solution.py:16
  128.6 11.1 %collective-permute-start.31 = (bf16[2,128,512]{2,1,0:T(8,128)(2,1)S(1)}, bf16[2,128,512]{2,1,0:T(8,128)(2,1)S(1)}, u32[]{:S(2)}, u32[]{:S(2)}) collective-permute-start(bf16[2,128,512]{2,1,0:T(8,128)(2,1)S(1)} %get-tuple-element.60), channel_id=1, source_target_pairs={{0,32},{32,0},{64,96},{96,64},{1,33},{33,1},{65,97},{97,65},{2,34}... | collective-permute-start | bytes 786440 | tf_op jit(solution)/shard_map/ppermute | solution.py:16
  136.8 8.9 %collective-permute-start.32 = (bf16[2,128,512]{2,1,0:T(8,128)(2,1)S(1)}, bf16[2,128,512]{2,1,0:T(8,128)(2,1)S(1)}, u32[]{:S(2)}, u32[]{:S(2)}) collective-permute-start(bf16[2,128,512]{2,1,0:T(8,128)(2,1)S(1)} %get-tuple-element.59), channel_id=1, source_target_pairs={{0,64},{32,96},{64,0},{96,32},{1,65},{33,97},{65,1},{97,33},{2,66}... | collective-permute-start | bytes 786440 | tf_op jit(solution)/shard_map/ppermute | solution.py:16
  137.6 14.5 %collective-permute-start.33 = (bf16[2,128,512]{2,1,0:T(8,128)(2,1)S(1)}, bf16[2,128,512]{2,1,0:T(8,128)(2,1)S(1)}, u32[]{:S(2)}, u32[]{:S(2)}) collective-permute-start(bf16[2,128,512]{2,1,0:T(8,128)(2,1)S(1)} %get-tuple-element.58), channel_id=1, source_target_pairs={{0,96},{32,64},{64,32},{96,0},{1,97},{33,65},{65,33},{97,1},{2,98}... | collective-permute-start | bytes 786440 | tf_op jit(solution)/shard_map/ppermute | solution.py:16
  137.9 15.0 %collective-permute-start.27 = (bf16[3,8,8192]{2,1,0:T(8,128)(2,1)S(1)}, bf16[3,8,8192]{2,1,0:T(8,128)(2,1)S(1)}, u32[]{:S(2)}, u32[]{:S(2)}) collective-permute-start(bf16[3,8,8192]{2,1,0:T(8,128)(2,1)S(1)} %pad_maximum_fusion.7), channel_id=1, source_target_pairs={{0,8},{8,0},{1,9},{9,1},{2,10},{10,2},{3,11},{11,3},{4,12},{12,4},... | collective-permute-start | bytes 1179656 | tf_op jit(solution)/shard_map/ppermute | solution.py:16
  139.7 13.4 %collective-permute-start.25 = (bf16[4,8,4096]{2,1,0:T(8,128)(2,1)S(1)}, bf16[4,8,4096]{2,1,0:T(8,128)(2,1)S(1)}, u32[]{:S(2)}, u32[]{:S(2)}) collective-permute-start(bf16[4,8,4096]{2,1,0:T(8,128)(2,1)S(1)} %get-tuple-element.67), channel_id=1, source_target_pairs={{0,7},{1,2},{2,1},{3,4},{4,3},{5,6},{6,5},{7,0},{8,15},{9,10},{10,... | collective-permute-start | bytes 786440 | tf_op jit(solution)/shard_map/ppermute | solution.py:28
  145.7 17.7 %collective-permute-start.29 = (bf16[4,8,4096]{2,1,0:T(8,128)(2,1)S(1)}, bf16[4,8,4096]{2,1,0:T(8,128)(2,1)S(1)}, u32[]{:S(2)}, u32[]{:S(2)}) collective-permute-start(bf16[4,8,4096]{2,1,0:T(8,128)(2,1)S(1)} %get-tuple-element.68), channel_id=1, source_target_pairs={{0,1},{1,0},{2,3},{3,2},{4,5},{5,4},{6,7},{7,6},{8,9},{9,8},{10,11... | collective-permute-start | bytes 786440 | tf_op jit(solution)/shard_map/ppermute | solution.py:16
  152.4 2.1 collective-permute-start.34
  153.0 9.2 %collective-permute-start.28 = (bf16[4,8,4096]{2,1,0:T(8,128)(2,1)S(1)}, bf16[4,8,4096]{2,1,0:T(8,128)(2,1)S(1)}, u32[]{:S(2)}, u32[]{:S(2)}) collective-permute-start(bf16[4,8,4096]{2,1,0:T(8,128)(2,1)S(1)} %get-tuple-element.69), channel_id=1, source_target_pairs={{0,7},{1,2},{2,1},{3,4},{4,3},{5,6},{6,5},{7,0},{8,15},{9,10},{10,... | collective-permute-start | bytes 786440 | tf_op jit(solution)/shard_map/ppermute | solution.py:28
  153.2 10.2 %collective-permute-start.30 = (bf16[4,8,4096]{2,1,0:T(8,128)(2,1)S(1)}, bf16[4,8,4096]{2,1,0:T(8,128)(2,1)S(1)}, u32[]{:S(2)}, u32[]{:S(2)}) collective-permute-start(bf16[4,8,4096]{2,1,0:T(8,128)(2,1)S(1)} %get-tuple-element.70), channel_id=1, source_target_pairs={{0,1},{1,0},{2,3},{3,2},{4,5},{5,4},{6,7},{7,6},{8,9},{9,8},{10,11... | collective-permute-start | bytes 786440 | tf_op jit(solution)/shard_map/ppermute | solution.py:16
  154.5 7.8 %copy-start.6 = (bf16[448,4096]{1,0:T(8,128)(2,1)S(1)}, bf16[448,4096]{1,0:T(8,128)(2,1)}, u32[]{:S(2)}) copy-start(bf16[448,4096]{1,0:T(8,128)(2,1)} %param.10) | copy-start | bytes 11010052
  164.6 35.2 %copy-start = (bf16[256,2,448]{0,2,1:T(8,128)(2,1)S(1)}, bf16[256,2,448]{0,2,1:T(8,128)(2,1)}, u32[]{:S(2)}) copy-start(bf16[256,2,448]{0,2,1:T(8,128)(2,1)} %param.11) | copy-start | bytes 1376260
  164.6 18.0 %collective-permute-start.36 = (bf16[896,128]{1,0:T(8,128)(2,1)S(1)}, bf16[896,128]{1,0:T(8,128)(2,1)S(1)}, u32[]{:S(2)}, u32[]{:S(2)}) collective-permute-start(bf16[896,128]{1,0:T(8,128)(2,1)S(1)} %pad_maximum_fusion.11), channel_id=1, source_target_pairs={{0,128},{128,0},{1,129},{129,1},{2,130},{130,2},{3,131},{131,3},{4... | collective-permute-start | bytes 688136 | tf_op jit(solution)/shard_map/ppermute | solution.py:16
  177.7 20.6 %collective-permute-start.35 = (bf16[4,896,128]{2,1,0:T(8,128)(2,1)S(1)}, bf16[4,896,128]{2,1,0:T(8,128)(2,1)}, u32[]{:S(2)}, u32[]{:S(2)}) collective-permute-start(bf16[4,896,128]{2,1,0:T(8,128)(2,1)S(1)} %bitcast.146), channel_id=1, source_target_pairs={{0,16},{16,0},{1,17},{17,1},{2,18},{18,2},{3,19},{19,3},{4,20},{20... | collective-permute-start | bytes 2752520 | tf_op jit(solution)/shard_map/ppermute | solution.py:16
  195.4 4.3 %collective-permute-start.37 = (bf16[4,896,128]{2,1,0:T(8,128)(2,1)S(1)}, bf16[4,896,128]{2,1,0:T(8,128)(2,1)}, u32[]{:S(2)}, u32[]{:S(2)}) collective-permute-start(bf16[4,896,128]{2,1,0:T(8,128)(2,1)S(1)} %bitcast.148), channel_id=1, source_target_pairs={{0,16},{16,0},{1,17},{17,1},{2,18},{18,2},{3,19},{19,3},{4,20},{20... | collective-permute-start | bytes 2752520 | tf_op jit(solution)/shard_map/ppermute | solution.py:16
  199.8 1.0 copy-start.4
  205.1 1.0 copy-start.2
  228.1 1.2 copy-start.3
Sparse Core Ops, SparseCore 0:
  19.1 40.2 all-gather.3

commit v3 on v2

--- a/solution.py
+++ b/solution.py
@@ -202,12 +202,13 @@
     current_far = swap(current_t, "x_hi")
     near = lax.all_gather(current_t, "y")
 
-    even, current_far = lax.optimization_barrier((gather_even(tokens), current_far))
+    even, odd = gather_z(gather_even(tokens))
+    odd, current_far = lax.optimization_barrier((odd, current_far))
     far = []
     for rows, step in ((current_far[:hidden], 1), (current_far[hidden:], 3)):
         pair = jnp.stack([rows, swap(rows, "y", step)])
         far += [pair, swap(pair, "y", 4 - step)]
-    group_rows = gather_x(*gather_z(even)).reshape(-1, width)
+    group_rows = gather_x(even, odd).reshape(-1, width)
     other_rows = swap(group_rows, "core")
 
     projected = dot(gate_up_t, group_rows, ((1,), (1,)))

time: 239 us -> 237 us (level)
  waiting for transfers between devices: 75.3 us -> 59.4 us
  starting transfers between devices: 65.3 us -> 78.4 us
  matrix products: 11.2 us -> 7.97 us
  blocking collectives: 45.7 us -> 48.2 us
  local copies, waits for them, and re-layouts: 6.07 us -> 8.49 us
    ppermute x34, waiting for transfers between devices: 62.7 us -> 36.9 us  [swap(): return lax.ppermute(value, axis, [(i, i ^ step) for i in range(size)])]
    ppermute x34, starting transfers between devices: 58.5 us -> 72.2 us  [swap(): return lax.ppermute(value, axis, [(i, i ^ step) for i in range(size)])]
    all_gather x1, waiting for transfers between devices: 0.02 us -> 7 us  [per_device(): near = lax.all_gather(current_t, 'y')]
    dot_general x5, matrix products: 11.2 us -> 7.97 us  [dot(): return lax.dot_general(a, b, (dims, ((), ())), preferred_element_type=F32)]
    ppermute x4, waiting for transfers between devices: 12.5 us -> 15.5 us  [neighbour(): lax.ppermute(value, 'z', [(i, (i + 1) % 8 if i % 2 else (i - 1) % 8) for...]
    unnamed x36 -> x28, local copies, waits for them, and re-layouts: 3.24 us -> 5.61 us
  transfers between devices with their start and end apart: 39 -> 39, of which waited for: 20 -> 18; matrix products, arithmetic and copies ran while one was open for 7% -> 6% of each run, Pallas kernels for 3% -> 3%
where the time goes in v3:
time: 237 us
  starting transfers between devices  78.4 us (33%)
  waiting for transfers between devices  59.4 us (25%)
  blocking collectives  48.2 us (20%)
  between operations  15.2 us (6%)
  Pallas kernels  13.6 us (6%)
  local copies, waits for them, and re-layouts  8.49 us (4%)
  matrix products  7.97 us (3%)
  other arithmetic  5.37 us (2%)
    ppermute x34, starting transfers between devices, swap(): return lax.ppermute(value, axis, [(i, i ^ step) for i in range(size)])  72.2 us
    ppermute x34, waiting for transfers between devices, swap(): return lax.ppermute(value, axis, [(i, i ^ step) for i in range(size)])  36.9 us
    all_gather x2, blocking collectives, per_device(): piece = lax.all_gather(piece, 'y')  24.3 us
    all_to_all x2, blocking collectives, per_device(): lax.all_to_all(jnp.broadcast_to(sums[None], (size, 8, 128)), axes, 0, 0,...  24 us
    ppermute x4, waiting for transfers between devices, neighbour(): lax.ppermute(value, 'z', [(i, (i + 1) % 8 if i % 2 else (i - 1) % 8) for...  15.5 us
    dot_general x5, matrix products, dot(): return lax.dot_general(a, b, (dims, ((), ())), preferred_element_type=F32)  7.97 us
    pallas_call x2, Pallas kernels, tangent_call(): pl.pallas_call(lambda *refs: tangent_kernel(first, *refs), out_shape=out_...  7.05 us
    all_gather x1, waiting for transfers between devices, per_device(): near = lax.all_gather(current_t, 'y')  7 us
  transfers between devices with their start and end apart: 39, of which 18 were waited for; matrix products, arithmetic and copies ran while one was open for 6% of the time, Pallas kernels for 3%

profile of v3, /device:TPU:1, one launch (start us, length us, event | category | flops | bytes accessed | tf_op | source)
XLA Modules:
  0.0 236.7 jit_solution(9498526613160998772)
XLA Ops:
  7.2 3.9 %collective-permute-start = (bf16[8,4096]{1,0:T(8,128)(2,1)}, bf16[8,4096]{1,0:T(8,128)(2,1)S(1)}, u32[]{:S(2)}, u32[]{:S(2)}) collective-permute-start(bf16[8,4096]{1,0:T(8,128)(2,1)} %param.7), channel_id=1, source_target_pairs={{0,2},{1,3},{2,0},{3,1},{4,6},{5,7},{6,4},{7,5},{8,10},{9,11},{10,... | collective-permute-start | bytes 196616 | tf_op jit(solution)/shard_map/ppermute | solution.py:16
  11.1 5.1 %collective-permute-start.1 = (bf16[8,4096]{1,0:T(8,128)(2,1)}, bf16[8,4096]{1,0:T(8,128)(2,1)S(1)}, u32[]{:S(2)}, u32[]{:S(2)}) collective-permute-start(bf16[8,4096]{1,0:T(8,128)(2,1)} %param.7), channel_id=1, source_target_pairs={{0,4},{1,5},{2,6},{3,7},{4,0},{5,1},{6,2},{7,3},{8,12},{9,13},{10,... | collective-permute-start | bytes 196616 | tf_op jit(solution)/shard_map/ppermute | solution.py:16
  16.2 2.7 %collective-permute-start.5 = (bf16[896,256]{1,0:T(8,128)(2,1)}, bf16[896,256]{1,0:T(8,128)(2,1)S(1)}, u32[]{:S(2)}, u32[]{:S(2)}) collective-permute-start(bf16[896,256]{1,0:T(8,128)(2,1)} %bitcast.150), channel_id=1, source_target_pairs={{0,128},{128,0},{1,129},{129,1},{2,130},{130,2},{3,131},{131,3},{4... | collective-permute-start | bytes 1376264 | tf_op jit(solution)/shard_map/ppermute | solution.py:16
  19.0 0.8 constant_dynamic-update-slice_fusion.6
  19.9 2.2 collective-permute-done.2
  22.0 0.9 pad_maximum_fusion.9
  22.9 1.3 collective-permute-start.6
  24.2 0.8 collective-permute-start.4
  25.4 4.2 %collective-permute-done.4 = bf16[4,8,2048]{2,1,0:T(8,128)(2,1)S(1)} collective-permute-done((bf16[4,8,2048]{2,1,0:T(8,128)(2,1)S(1)}, bf16[4,8,2048]{2,1,0:T(8,128)(2,1)S(1)}, u32[]{:S(2)}, u32[]{:S(2)}) %collective-permute-start.4) | collective-permute-done | bytes 131104 | tf_op jit(solution)/shard_map/ppermute | solution.py:28
  30.0 1.4 collective-permute-start.10
  31.4 1.9 collective-permute-start.12
  33.3 1.1 collective-permute-done.6
  34.4 5.3 %collective-permute-done.10 = bf16[448,256]{1,0:T(8,128)(2,1)S(1)} collective-permute-done((bf16[448,256]{1,0:T(8,128)(2,1)S(1)}, bf16[448,256]{1,0:T(8,128)(2,1)S(1)}, u32[]{:S(2)}, u32[]{:S(2)}) %collective-permute-start.10) | collective-permute-done | bytes 229408 | tf_op jit(solution)/shard_map/ppermute | solution.py:16
  39.7 3.4 %collective-permute-start.11 = (bf16[2,448,256]{2,1,0:T(8,128)(2,1)S(1)}, bf16[2,448,256]{2,1,0:T(8,128)(2,1)}, u32[]{:S(2)}, u32[]{:S(2)}) collective-permute-start(bf16[2,448,256]{2,1,0:T(8,128)(2,1)S(1)} %pad_maximum_fusion.5.refs_3_), channel_id=1, source_target_pairs={{0,96},{32,64},{64,32},{96,0},{1,97},{33,65},{65,33},{97,1},{2,98}... | collective-permute-start | bytes 1376264 | tf_op jit(solution)/shard_map/ppermute | solution.py:16
  43.7 6.7 %collective-permute-start.8 = (bf16[128,4096]{1,0:T(8,128)(2,1)S(1)}, bf16[128,4096]{1,0:T(8,128)(2,1)S(1)}, u32[]{:S(2)}, u32[]{:S(2)}) collective-permute-start(bf16[128,4096]{1,0:T(8,128)(2,1)S(1)} %bitcast.145), channel_id=1, source_target_pairs={{0,16},{16,0},{1,17},{17,1},{2,18},{18,2},{3,19},{19,3},{4,20},{20... | collective-permute-start | bytes 3145736 | tf_op jit(solution)/shard_map/ppermute | solution.py:16
  50.4 1.1 dynamic-slice_bitcast_fusion.1
  51.5 2.4 %collective-permute-start.9 = (bf16[128,2048]{1,0:T(8,128)(2,1)}, bf16[128,2048]{1,0:T(8,128)(2,1)}, u32[]{:S(2)}, u32[]{:S(2)}) collective-permute-start(bf16[128,2048]{1,0:T(8,128)(2,1)} %get-tuple-element.66), channel_id=1, source_target_pairs={{0,128},{128,0},{1,129},{129,1},{2,130},{130,2},{3,131},{131,3},{4... | collective-permute-start | bytes 1572872 | tf_op jit(solution)/shard_map/ppermute | solution.py:16
  53.9 2.1 convolution_bitcast_fusion
  56.0 7.0 %all-gather.4.cloned.1.call-done = bf16[4,896,256]{2,1,0:T(8,128)(2,1)} async-done(((bf16[1,896,256]{2,1,0:T(8,128)(2,1)}), bf16[4,896,256]{2,1,0:T(8,128)(2,1)}) %all-gather.4.cloned.1.call-update) | async-done | bytes 1835024 | tf_op jit(solution)/shard_map/all_gather | solution.py:203
  63.0 2.8 %convolution_convert_fusion.1 = bf16[128,4096]{1,0:T(8,128)(2,1)S(1)} fusion(bf16[448,4096]{1,0:T(8,128)(2,1)} %param.10, f32[896,128]{1,0:T(8,128)S(1)} %convolution_bitcast_fusion), kind=kOutput, calls=%fused_computation.1 | convolution fusion | flops 470630400 | bytes 5177344 | tf_op jit(solution)/shard_map/dot_general | solution.py:84
  65.8 1.1 fusion.42
  66.9 1.1 collective-permute-start.14
  68.1 2.3 pad_maximum_fusion
  70.4 1.5 copy-done.1
  71.9 2.7 %shard_map.94.refs_7_ = f32[2,448,256]{2,1,0:T(8,128)S(1)} custom-call(s32[12]{0:T(128)S(1)} %stack.194.refs_0_, bf16[128,4096]{1,0:T(8,128)(2,1)S(1)} %bitcast.147, bf16[128,4096]{1,0:T(8,128)(2,1)S(1)} %collective-permute-done.8.refs_2_, bf16[4,2,448,256]{3,2,1,0:T(8,128)(2,1)S(1)} %bitcast.159), custom_call_target="tpu_custom_call" | custom-call | flops 469762048 | bytes 1835008 | tf_op jit(solution)/shard_map/pallas_call | solution.py:132
  74.6 4.4 %shard_map.95 = (f32[2,448,128]{2,1,0:T(8,128)S(1)}, f32[2,448,128]{2,1,0:T(8,128)S(1)}) custom-call(s32[12]{0:T(128)S(1)} %stack.194.refs_0_, bf16[128,4096]{1,0:T(8,128)(2,1)S(1)} %bitcast.148, bf16[128,4096]{1,0:T(8,128)(2,1)S(1)} %collective-permute-done.8.refs_2_, bf16[2,448,256]{2,1,0:T(8,128)(2,1)S(1)} %pad_maximum_fusion.5.refs_3_, ...), custom_call_target="tpu_custom_call" | custom-call | flops 469762048 | bytes 1835008 | tf_op jit(solution)/shard_map/pallas_call | solution.py:132
  79.0 0.9 collective-permute-start.15
  80.2 1.2 fusion.14
  82.6 1.2 collective-permute-start.16
  83.8 11.0 %collective-permute-done.16 = bf16[2,4,8,4096]{3,2,1,0:T(8,128)(2,1)S(1)} collective-permute-done((bf16[2,4,8,4096]{3,2,1,0:T(8,128)(2,1)S(1)}, bf16[2,4,8,4096]{3,2,1,0:T(8,128)(2,1)S(1)}, u32[]{:S(2)}, u32[]{:S(2)}) %collective-permute-start.16) | collective-permute-done | bytes 524320 | tf_op jit(solution)/shard_map/ppermute | solution.py:16
  95.0 3.1 %collective-permute-start.18 = (bf16[4,16,2048]{2,1,0:T(8,128)(2,1)S(1)}, bf16[4,16,2048]{2,1,0:T(8,128)(2,1)S(1)}, u32[]{:S(2)}, u32[]{:S(2)}) collective-permute-start(bf16[4,16,2048]{2,1,0:T(8,128)(2,1)S(1)} %get-tuple-element.75), channel_id=1, source_target_pairs={{0,7},{1,2},{2,1},{3,4},{4,3},{5,6},{6,5},{7,0},{8,15},{9,10},{10,... | collective-permute-start | bytes 786440 | tf_op jit(solution)/shard_map/ppermute | solution.py:28
  98.1 4.4 %collective-permute-done.18 = bf16[4,16,2048]{2,1,0:T(8,128)(2,1)S(1)} collective-permute-done((bf16[4,16,2048]{2,1,0:T(8,128)(2,1)S(1)}, bf16[4,16,2048]{2,1,0:T(8,128)(2,1)S(1)}, u32[]{:S(2)}, u32[]{:S(2)}) %collective-permute-start.18) | collective-permute-done | bytes 262176 | tf_op jit(solution)/shard_map/ppermute | solution.py:28
  102.5 1.1 collective-permute-done.17
  103.7 2.9 %collective-permute-start.21 = (bf16[16,4096]{1,0:T(8,128)(2,1)S(1)}, bf16[16,4096]{1,0:T(8,128)(2,1)S(1)}, u32[]{:S(2)}, u32[]{:S(2)}) collective-permute-start(bf16[16,4096]{1,0:T(8,128)(2,1)S(1)} %get-tuple-element.72), channel_id=1, source_target_pairs={{0,6},{1,7},{2,4},{3,5},{4,2},{5,3},{6,0},{7,1},{8,14},{9,15},{10,... | collective-permute-start | bytes 393224 | tf_op jit(solution)/shard_map/ppermute | solution.py:16
  106.6 1.9 collective-permute-start.20
  108.5 1.0 collective-permute-start.19
  109.9 8.1 %collective-permute-done.20 = bf16[16,4096]{1,0:T(8,128)(2,1)S(1)} collective-permute-done((bf16[16,4096]{1,0:T(8,128)(2,1)S(1)}, bf16[16,4096]{1,0:T(8,128)(2,1)S(1)}, u32[]{:S(2)}, u32[]{:S(2)}) %collective-permute-start.20) | collective-permute-done | bytes 131104 | tf_op jit(solution)/shard_map/ppermute | solution.py:16
  118.1 4.4 %collective-permute-start.24 = (bf16[8,8192]{1,0:T(8,128)(2,1)S(1)}, bf16[8,8192]{1,0:T(8,128)(2,1)S(1)}, u32[]{:S(2)}, u32[]{:S(2)}) collective-permute-start(bf16[8,8192]{1,0:T(8,128)(2,1)S(1)} %pad_maximum_fusion.12), channel_id=1, source_target_pairs={{0,6},{1,7},{2,4},{3,5},{4,2},{5,3},{6,0},{7,1},{8,14},{9,15},{10,... | collective-permute-start | bytes 393224 | tf_op jit(solution)/shard_map/ppermute | solution.py:16
  122.8 1.9 collective-permute-start.22
  124.7 3.3 %collective-permute-start.26 = (bf16[8,8192]{1,0:T(8,128)(2,1)S(1)}, bf16[8,8192]{1,0:T(8,128)(2,1)S(1)}, u32[]{:S(2)}, u32[]{:S(2)}) collective-permute-start(bf16[8,8192]{1,0:T(8,128)(2,1)S(1)} %pad_maximum_fusion.12), channel_id=1, source_target_pairs={{0,8},{8,0},{1,9},{9,1},{2,10},{10,2},{3,11},{11,3},{4,12},{12,4},... | collective-permute-start | bytes 393224 | tf_op jit(solution)/shard_map/ppermute | solution.py:16
  128.9 1.6 collective-permute-done.23
  130.5 0.9 collective-permute-start.31
  131.5 9.6 %collective-permute-start.27 = (bf16[3,8,8192]{2,1,0:T(8,128)(2,1)S(1)}, bf16[3,8,8192]{2,1,0:T(8,128)(2,1)S(1)}, u32[]{:S(2)}, u32[]{:S(2)}) collective-permute-start(bf16[3,8,8192]{2,1,0:T(8,128)(2,1)S(1)} %pad_maximum_fusion.7), channel_id=1, source_target_pairs={{0,8},{8,0},{1,9},{9,1},{2,10},{10,2},{3,11},{11,3},{4,12},{12,4},... | collective-permute-start | bytes 1179656 | tf_op jit(solution)/shard_map/ppermute | solution.py:16
  141.3 1.5 collective-permute-done.33
  142.8 2.2 collective-permute-start.25
  145.2 1.9 collective-permute-start.34
  147.1 2.4 collective-permute-done.27
  149.6 1.2 collective-permute-done.25
  151.2 5.7 %collective-permute-done.28 = bf16[4,8,4096]{2,1,0:T(8,128)(2,1)S(1)} collective-permute-done((bf16[4,8,4096]{2,1,0:T(8,128)(2,1)S(1)}, bf16[4,8,4096]{2,1,0:T(8,128)(2,1)S(1)}, u32[]{:S(2)}, u32[]{:S(2)}) %collective-permute-start.28) | collective-permute-done | bytes 262176 | tf_op jit(solution)/shard_map/ppermute | solution.py:28
  156.9 1.1 convolution_bitcast_fusion.2
  158.1 1.2 fusion.29
  159.3 2.3 collective-permute-start.36
  161.6 11.5 %all-gather = bf16[3584,128]{1,0:T(8,128)(2,1)S(1)} all-gather(bf16[896,128]{1,0:T(8,128)(2,1)S(1)} %pad_maximum_fusion.11), channel_id=2, replica_groups=mesh['x_hi'=2,'y'=4,'core'=2,'x_lo'=2,'z'=8] {'y'}, dimensions={0}, use_global_device_ids=true | all-gather | bytes 1146880 | tf_op jit(solution)/shard_map/all_gather | solution.py:284
  173.1 6.2 %collective-permute-start.35 = (bf16[4,896,128]{2,1,0:T(8,128)(2,1)S(1)}, bf16[4,896,128]{2,1,0:T(8,128)(2,1)}, u32[]{:S(2)}, u32[]{:S(2)}) collective-permute-start(bf16[4,896,128]{2,1,0:T(8,128)(2,1)S(1)} %bitcast.154), channel_id=1, source_target_pairs={{0,16},{16,0},{1,17},{17,1},{2,18},{18,2},{3,19},{19,3},{4,20},{20... | collective-permute-start | bytes 2752520 | tf_op jit(solution)/shard_map/ppermute | solution.py:16
  179.3 12.8 %all-gather.1 = bf16[3584,128]{1,0:T(8,128)(2,1)S(1)} all-gather(bf16[896,128]{1,0:T(8,128)(2,1)S(1)} %collective-permute-done.36), channel_id=3, replica_groups=mesh['x_hi'=2,'y'=4,'core'=2,'x_lo'=2,'z'=8] {'y'}, dimensions={0}, use_global_device_ids=true | all-gather | bytes 1146880 | tf_op jit(solution)/shard_map/all_gather | solution.py:284
  192.1 2.1 collective-permute-start.37
  195.0 1.5 collective-permute-done.37.refs_3_
  196.4 1.0 copy-done.4
  197.5 4.3 %shard_map.97 = (f32[896,256]{1,0:T(8,128)S(1)}, f32[8,128]{1,0:T(8,128)S(1)}) custom-call(s32[16]{0:T(128)S(1)} %stack.185.index_ref, f32[1,1]{1,0:T(1,128)} %bitcast.144.beta_ref, bf16[16,128,256]{2,1,0:T(8,128)(2,1)S(1)} %bitcast.149, bf16[4,896,128]{2,1,0:T(8,128)(2,1)S(1)} %bitcast.155, bf16[4,896,128]{2,1,0:T(8,128)(2,1)} %collective-permute-done.35.refs_1_, ...), custom_call_target="tpu_custom_call" | custom-call | flops 1073741824 | bytes 7340032 | tf_op jit(solution)/shard_map/pallas_call | solution.py:289
  201.8 1.0 copy-done.2
  202.8 11.4 %all_to_all.10 = f32[8,8,128]{2,1,0:T(8,128)S(1)} all-to-all(f32[8,8,128]{2,1,0:T(8,128)S(1)} %broadcast_in_dim.7), channel_id=1, replica_groups=mesh['x_hi'=2,'y'=4,'core'=2,'x_lo'=2,'z'=8] {'z'}, dimensions={0} | all-to-all | bytes 65536 | tf_op jit(solution)/shard_map/all_to_all | solution.py:314
  214.2 12.6 %all_to_all.11.refs_0_ = f32[32,8,128]{2,1,0:T(8,128)S(1)} all-to-all(f32[32,8,128]{2,1,0:T(8,128)S(1)} %broadcast_in_dim.8), channel_id=1, replica_groups=mesh['x_hi'=2,'y'=4,'core'=2,'x_lo'=2,'z'=8] {'x_hi','y','core','x_lo'}, dimensions={0} | all-to-all | bytes 262144 | tf_op jit(solution)/shard_map/all_to_all | solution.py:314
  226.8 1.2 copy-done.3
  228.0 1.9 shard_map.98
  (96 shorter events, 6.2 us)
Async XLA Ops:
  7.2 55.9 %all-gather.4.cloned.1.call-start = ((), (), s32[]{:S(2)}) async-start(), calls=%async_computation.2 | async-start | bytes 2293760 | tf_op jit(solution)/shard_map/all_gather | solution.py:203
  7.2 12.6 %collective-permute-start = (bf16[8,4096]{1,0:T(8,128)(2,1)}, bf16[8,4096]{1,0:T(8,128)(2,1)S(1)}, u32[]{:S(2)}, u32[]{:S(2)}) collective-permute-start(bf16[8,4096]{1,0:T(8,128)(2,1)} %param.7), channel_id=1, source_target_pairs={{0,2},{1,3},{2,0},{3,1},{4,6},{5,7},{6,4},{7,5},{8,10},{9,11},{10,... | collective-permute-start | bytes 196616 | tf_op jit(solution)/shard_map/ppermute | solution.py:16
  11.1 8.7 %collective-permute-start.1 = (bf16[8,4096]{1,0:T(8,128)(2,1)}, bf16[8,4096]{1,0:T(8,128)(2,1)S(1)}, u32[]{:S(2)}, u32[]{:S(2)}) collective-permute-start(bf16[8,4096]{1,0:T(8,128)(2,1)} %param.7), channel_id=1, source_target_pairs={{0,4},{1,5},{2,6},{3,7},{4,0},{5,1},{6,2},{7,3},{8,12},{9,13},{10,... | collective-permute-start | bytes 196616 | tf_op jit(solution)/shard_map/ppermute | solution.py:16
  16.2 5.8 %collective-permute-start.2 = (bf16[8,4096]{1,0:T(8,128)(2,1)}, bf16[8,4096]{1,0:T(8,128)(2,1)S(1)}, u32[]{:S(2)}, u32[]{:S(2)}) collective-permute-start(bf16[8,4096]{1,0:T(8,128)(2,1)} %param.7), channel_id=1, source_target_pairs={{0,6},{1,7},{2,4},{3,5},{4,2},{5,3},{6,0},{7,1},{8,14},{9,15},{10,... | collective-permute-start | bytes 196616 | tf_op jit(solution)/shard_map/ppermute | solution.py:16
  16.2 13.4 %collective-permute-start.5 = (bf16[896,256]{1,0:T(8,128)(2,1)}, bf16[896,256]{1,0:T(8,128)(2,1)S(1)}, u32[]{:S(2)}, u32[]{:S(2)}) collective-permute-start(bf16[896,256]{1,0:T(8,128)(2,1)} %bitcast.150), channel_id=1, source_target_pairs={{0,128},{128,0},{1,129},{129,1},{2,130},{130,2},{3,131},{131,3},{4... | collective-permute-start | bytes 1376264 | tf_op jit(solution)/shard_map/ppermute | solution.py:16
  22.9 11.5 %collective-permute-start.6 = (bf16[4,8,4096]{2,1,0:T(8,128)(2,1)S(1)}, bf16[4,8,4096]{2,1,0:T(8,128)(2,1)S(1)}, u32[]{:S(2)}, u32[]{:S(2)}) collective-permute-start(bf16[4,8,4096]{2,1,0:T(8,128)(2,1)S(1)} %pad_maximum_fusion.9), channel_id=1, source_target_pairs={{0,8},{8,0},{1,9},{9,1},{2,10},{10,2},{3,11},{11,3},{4,12},{12,4},... | collective-permute-start | bytes 786440 | tf_op jit(solution)/shard_map/ppermute | solution.py:16
  24.2 5.3 %collective-permute-start.4 = (bf16[4,8,2048]{2,1,0:T(8,128)(2,1)S(1)}, bf16[4,8,2048]{2,1,0:T(8,128)(2,1)S(1)}, u32[]{:S(2)}, u32[]{:S(2)}) collective-permute-start(bf16[4,8,2048]{2,1,0:T(8,128)(2,1)S(1)} %get-tuple-element.83), channel_id=1, source_target_pairs={{0,7},{1,2},{2,1},{3,4},{4,3},{5,6},{6,5},{7,0},{8,15},{9,10},{10,... | collective-permute-start | bytes 393224 | tf_op jit(solution)/shard_map/ppermute | solution.py:28
  25.1 4.5 %collective-permute-start.3 = (bf16[4,8,2048]{2,1,0:T(8,128)(2,1)S(1)}, bf16[4,8,2048]{2,1,0:T(8,128)(2,1)S(1)}, u32[]{:S(2)}, u32[]{:S(2)}) collective-permute-start(bf16[4,8,2048]{2,1,0:T(8,128)(2,1)S(1)} %get-tuple-element.82), channel_id=1, source_target_pairs={{0,1},{1,0},{2,3},{3,2},{4,5},{5,4},{6,7},{7,6},{8,9},{9,8},{10,11... | collective-permute-start | bytes 393224 | tf_op jit(solution)/shard_map/ppermute | solution.py:16
  29.6 24.3 %copy-start.5 = (bf16[4096,2,448]{0,2,1:T(8,128)(2,1)S(1)}, bf16[4096,2,448]{0,2,1:T(8,128)(2,1)}, u32[]{:S(2)}) copy-start(bf16[4096,2,448]{0,2,1:T(8,128)(2,1)} %param.9) | copy-start | bytes 22020100
  29.7 14.0 %collective-permute-start.7 = (bf16[4,8,4096]{2,1,0:T(8,128)(2,1)S(1)}, bf16[4,8,4096]{2,1,0:T(8,128)(2,1)S(1)}, u32[]{:S(2)}, u32[]{:S(2)}) collective-permute-start(bf16[4,8,4096]{2,1,0:T(8,128)(2,1)S(1)} %pad_maximum_fusion.10), channel_id=1, source_target_pairs={{0,8},{8,0},{1,9},{9,1},{2,10},{10,2},{3,11},{11,3},{4,12},{12,4},... | collective-permute-start | bytes 786440 | tf_op jit(solution)/shard_map/ppermute | solution.py:16
  30.0 9.7 %collective-permute-start.10 = (bf16[448,256]{1,0:T(8,128)(2,1)S(1)}, bf16[448,256]{1,0:T(8,128)(2,1)S(1)}, u32[]{:S(2)}, u32[]{:S(2)}) collective-permute-start(bf16[448,256]{1,0:T(8,128)(2,1)S(1)} %get-tuple-element.79), channel_id=1, source_target_pairs={{0,32},{32,0},{64,96},{96,64},{1,33},{33,1},{65,97},{97,65},{2,34}... | collective-permute-start | bytes 688136 | tf_op jit(solution)/shard_map/ppermute | solution.py:16
  31.4 12.1 %collective-permute-start.12 = (bf16[448,256]{1,0:T(8,128)(2,1)S(1)}, bf16[448,256]{1,0:T(8,128)(2,1)S(1)}, u32[]{:S(2)}, u32[]{:S(2)}) collective-permute-start(bf16[448,256]{1,0:T(8,128)(2,1)S(1)} %get-tuple-element.78), channel_id=1, source_target_pairs={{0,96},{32,64},{64,32},{96,0},{1,97},{33,65},{65,33},{97,1},{2,98}... | collective-permute-start | bytes 688136 | tf_op jit(solution)/shard_map/ppermute | solution.py:16
  39.7 30.6 %collective-permute-start.11 = (bf16[2,448,256]{2,1,0:T(8,128)(2,1)S(1)}, bf16[2,448,256]{2,1,0:T(8,128)(2,1)}, u32[]{:S(2)}, u32[]{:S(2)}) collective-permute-start(bf16[2,448,256]{2,1,0:T(8,128)(2,1)S(1)} %pad_maximum_fusion.5.refs_3_), channel_id=1, source_target_pairs={{0,96},{32,64},{64,32},{96,0},{1,97},{33,65},{65,33},{97,1},{2,98}... | collective-permute-start | bytes 1376264 | tf_op jit(solution)/shard_map/ppermute | solution.py:16
  43.6 26.8 %collective-permute-start.13 = (bf16[2,448,256]{2,1,0:T(8,128)(2,1)S(1)}, bf16[2,448,256]{2,1,0:T(8,128)(2,1)}, u32[]{:S(2)}, u32[]{:S(2)}) collective-permute-start(bf16[2,448,256]{2,1,0:T(8,128)(2,1)S(1)} %pad_maximum_fusion.6.refs_5_), channel_id=1, source_target_pairs={{0,32},{32,0},{64,96},{96,64},{1,33},{33,1},{65,97},{97,65},{2,34}... | collective-permute-start | bytes 1376264 | tf_op jit(solution)/shard_map/ppermute | solution.py:16
  43.7 26.7 %collective-permute-start.8 = (bf16[128,4096]{1,0:T(8,128)(2,1)S(1)}, bf16[128,4096]{1,0:T(8,128)(2,1)S(1)}, u32[]{:S(2)}, u32[]{:S(2)}) collective-permute-start(bf16[128,4096]{1,0:T(8,128)(2,1)S(1)} %bitcast.145), channel_id=1, source_target_pairs={{0,16},{16,0},{1,17},{17,1},{2,18},{18,2},{3,19},{19,3},{4,20},{20... | collective-permute-start | bytes 3145736 | tf_op jit(solution)/shard_map/ppermute | solution.py:16
  51.5 16.6 %collective-permute-start.9 = (bf16[128,2048]{1,0:T(8,128)(2,1)}, bf16[128,2048]{1,0:T(8,128)(2,1)}, u32[]{:S(2)}, u32[]{:S(2)}) collective-permute-start(bf16[128,2048]{1,0:T(8,128)(2,1)} %get-tuple-element.66), channel_id=1, source_target_pairs={{0,128},{128,0},{1,129},{129,1},{2,130},{130,2},{3,131},{131,3},{4... | collective-permute-start | bytes 1572872 | tf_op jit(solution)/shard_map/ppermute | solution.py:16
  66.9 13.3 %collective-permute-start.14 = (bf16[2,4,8,4096]{3,2,1,0:T(8,128)(2,1)}, bf16[2,4,8,4096]{3,2,1,0:T(8,128)(2,1)}, u32[]{:S(2)}, u32[]{:S(2)}) collective-permute-start(bf16[2,4,8,4096]{3,2,1,0:T(8,128)(2,1)} %bitcast.46), channel_id=1, source_target_pairs={{0,8},{8,0},{1,9},{9,1},{2,10},{10,2},{3,11},{11,3},{4,12},{12,4},... | collective-permute-start | bytes 1572872 | tf_op jit(solution)/shard_map/ppermute | solution.py:16
  70.4 1.5 copy-start.1
  71.9 8.3 %copy-start.9 = (bf16[64,4096]{1,0:T(8,128)(2,1)S(1)}, bf16[64,4096]{1,0:T(8,128)(2,1)}, u32[]{:S(2)}) copy-start(bf16[64,4096]{1,0:T(8,128)(2,1)} %get-tuple-element.64) | copy-start | bytes 1572868
  74.6 7.2 %copy-start.6 = (bf16[448,4096]{1,0:T(8,128)(2,1)S(1)}, bf16[448,4096]{1,0:T(8,128)(2,1)}, u32[]{:S(2)}) copy-start(bf16[448,4096]{1,0:T(8,128)(2,1)} %param.10) | copy-start | bytes 11010052
  79.0 2.4 %collective-permute-start.15 = (f32[2,448,128]{2,1,0:T(8,128)S(1)}, f32[2,448,128]{2,1,0:T(8,128)S(1)}, u32[]{:S(2)}, u32[]{:S(2)}) collective-permute-start(f32[2,448,128]{2,1,0:T(8,128)S(1)} %get-tuple-element.40), channel_id=1, source_target_pairs={{0,16},{16,0},{1,17},{17,1},{2,18},{18,2},{3,19},{19,3},{4,20},{20... | collective-permute-start | bytes 1376264 | tf_op jit(solution)/shard_map/ppermute | solution.py:16
  82.6 12.1 %collective-permute-start.16 = (bf16[2,4,8,4096]{3,2,1,0:T(8,128)(2,1)S(1)}, bf16[2,4,8,4096]{3,2,1,0:T(8,128)(2,1)S(1)}, u32[]{:S(2)}, u32[]{:S(2)}) collective-permute-start(bf16[2,4,8,4096]{3,2,1,0:T(8,128)(2,1)S(1)} %bitcast.167), channel_id=1, source_target_pairs={{0,8},{8,0},{1,9},{9,1},{2,10},{10,2},{3,11},{11,3},{4,12},{12,4},... | collective-permute-start | bytes 1572872 | tf_op jit(solution)/shard_map/ppermute | solution.py:16
  94.9 23.2 %copy-start.10 = (bf16[8,4096]{1,0:T(8,128)(2,1)S(1)}, bf16[8,4096]{1,0:T(8,128)(2,1)}, u32[]{:S(2)}) copy-start(bf16[8,4096]{1,0:T(8,128)(2,1)} %param.8) | copy-start | bytes 196612
  94.9 33.1 %copy-start.8 = (bf16[2,128,2048]{2,1,0:T(8,128)(2,1)S(1)}, bf16[2,128,2048]{2,1,0:T(8,128)(2,1)}, u32[]{:S(2)}) copy-start(bf16[2,128,2048]{2,1,0:T(8,128)(2,1)} %pad_maximum_fusion) | copy-start | bytes 3145732
  95.0 7.5 %collective-permute-start.18 = (bf16[4,16,2048]{2,1,0:T(8,128)(2,1)S(1)}, bf16[4,16,2048]{2,1,0:T(8,128)(2,1)S(1)}, u32[]{:S(2)}, u32[]{:S(2)}) collective-permute-start(bf16[4,16,2048]{2,1,0:T(8,128)(2,1)S(1)} %get-tuple-element.75), channel_id=1, source_target_pairs={{0,7},{1,2},{2,1},{3,4},{4,3},{5,6},{6,5},{7,0},{8,15},{9,10},{10,... | collective-permute-start | bytes 786440 | tf_op jit(solution)/shard_map/ppermute | solution.py:28
  98.1 5.5 %collective-permute-start.17 = (bf16[4,16,2048]{2,1,0:T(8,128)(2,1)S(1)}, bf16[4,16,2048]{2,1,0:T(8,128)(2,1)S(1)}, u32[]{:S(2)}, u32[]{:S(2)}) collective-permute-start(bf16[4,16,2048]{2,1,0:T(8,128)(2,1)S(1)} %get-tuple-element.74), channel_id=1, source_target_pairs={{0,1},{1,0},{2,3},{3,2},{4,5},{5,4},{6,7},{7,6},{8,9},{9,8},{10,11... | collective-permute-start | bytes 786440 | tf_op jit(solution)/shard_map/ppermute | solution.py:16
  103.7 6.2 %collective-permute-start.21 = (bf16[16,4096]{1,0:T(8,128)(2,1)S(1)}, bf16[16,4096]{1,0:T(8,128)(2,1)S(1)}, u32[]{:S(2)}, u32[]{:S(2)}) collective-permute-start(bf16[16,4096]{1,0:T(8,128)(2,1)S(1)} %get-tuple-element.72), channel_id=1, source_target_pairs={{0,6},{1,7},{2,4},{3,5},{4,2},{5,3},{6,0},{7,1},{8,14},{9,15},{10,... | collective-permute-start | bytes 393224 | tf_op jit(solution)/shard_map/ppermute | solution.py:16
  106.6 11.4 %collective-permute-start.20 = (bf16[16,4096]{1,0:T(8,128)(2,1)S(1)}, bf16[16,4096]{1,0:T(8,128)(2,1)S(1)}, u32[]{:S(2)}, u32[]{:S(2)}) collective-permute-start(bf16[16,4096]{1,0:T(8,128)(2,1)S(1)} %get-tuple-element.73), channel_id=1, source_target_pairs={{0,4},{1,5},{2,6},{3,7},{4,0},{5,1},{6,2},{7,3},{8,12},{9,13},{10,... | collective-permute-start | bytes 393224 | tf_op jit(solution)/shard_map/ppermute | solution.py:16
  108.5 9.5 %collective-permute-start.19 = (bf16[16,4096]{1,0:T(8,128)(2,1)S(1)}, bf16[16,4096]{1,0:T(8,128)(2,1)S(1)}, u32[]{:S(2)}, u32[]{:S(2)}) collective-permute-start(bf16[16,4096]{1,0:T(8,128)(2,1)S(1)} %get-tuple-element.71), channel_id=1, source_target_pairs={{0,2},{1,3},{2,0},{3,1},{4,6},{5,7},{6,4},{7,5},{8,10},{9,11},{10,... | collective-permute-start | bytes 393224 | tf_op jit(solution)/shard_map/ppermute | solution.py:16
  118.1 10.1 %collective-permute-start.24 = (bf16[8,8192]{1,0:T(8,128)(2,1)S(1)}, bf16[8,8192]{1,0:T(8,128)(2,1)S(1)}, u32[]{:S(2)}, u32[]{:S(2)}) collective-permute-start(bf16[8,8192]{1,0:T(8,128)(2,1)S(1)} %pad_maximum_fusion.12), channel_id=1, source_target_pairs={{0,6},{1,7},{2,4},{3,5},{4,2},{5,3},{6,0},{7,1},{8,14},{9,15},{10,... | collective-permute-start | bytes 393224 | tf_op jit(solution)/shard_map/ppermute | solution.py:16
  122.5 8.0 %collective-permute-start.23 = (bf16[8,8192]{1,0:T(8,128)(2,1)S(1)}, bf16[8,8192]{1,0:T(8,128)(2,1)S(1)}, u32[]{:S(2)}, u32[]{:S(2)}) collective-permute-start(bf16[8,8192]{1,0:T(8,128)(2,1)S(1)} %pad_maximum_fusion.12), channel_id=1, source_target_pairs={{0,4},{1,5},{2,6},{3,7},{4,0},{5,1},{6,2},{7,3},{8,12},{9,13},{10,... | collective-permute-start | bytes 393224 | tf_op jit(solution)/shard_map/ppermute | solution.py:16
  122.8 8.7 %collective-permute-start.22 = (bf16[8,8192]{1,0:T(8,128)(2,1)S(1)}, bf16[8,8192]{1,0:T(8,128)(2,1)S(1)}, u32[]{:S(2)}, u32[]{:S(2)}) collective-permute-start(bf16[8,8192]{1,0:T(8,128)(2,1)S(1)} %pad_maximum_fusion.12), channel_id=1, source_target_pairs={{0,2},{1,3},{2,0},{3,1},{4,6},{5,7},{6,4},{7,5},{8,10},{9,11},{10,... | collective-permute-start | bytes 393224 | tf_op jit(solution)/shard_map/ppermute | solution.py:16
  124.7 22.4 %collective-permute-start.26 = (bf16[8,8192]{1,0:T(8,128)(2,1)S(1)}, bf16[8,8192]{1,0:T(8,128)(2,1)S(1)}, u32[]{:S(2)}, u32[]{:S(2)}) collective-permute-start(bf16[8,8192]{1,0:T(8,128)(2,1)S(1)} %pad_maximum_fusion.12), channel_id=1, source_target_pairs={{0,8},{8,0},{1,9},{9,1},{2,10},{10,2},{3,11},{11,3},{4,12},{12,4},... | collective-permute-start | bytes 393224 | tf_op jit(solution)/shard_map/ppermute | solution.py:16
  128.1 14.7 %collective-permute-start.33 = (bf16[2,128,512]{2,1,0:T(8,128)(2,1)S(1)}, bf16[2,128,512]{2,1,0:T(8,128)(2,1)S(1)}, u32[]{:S(2)}, u32[]{:S(2)}) collective-permute-start(bf16[2,128,512]{2,1,0:T(8,128)(2,1)S(1)} %get-tuple-element.58), channel_id=1, source_target_pairs={{0,96},{32,64},{64,32},{96,0},{1,97},{33,65},{65,33},{97,1},{2,98}... | collective-permute-start | bytes 786440 | tf_op jit(solution)/shard_map/ppermute | solution.py:16
  128.2 16.7 %collective-permute-start.32 = (bf16[2,128,512]{2,1,0:T(8,128)(2,1)S(1)}, bf16[2,128,512]{2,1,0:T(8,128)(2,1)S(1)}, u32[]{:S(2)}, u32[]{:S(2)}) collective-permute-start(bf16[2,128,512]{2,1,0:T(8,128)(2,1)S(1)} %get-tuple-element.59), channel_id=1, source_target_pairs={{0,64},{32,96},{64,0},{96,32},{1,65},{33,97},{65,1},{97,33},{2,66}... | collective-permute-start | bytes 786440 | tf_op jit(solution)/shard_map/ppermute | solution.py:16
  130.5 14.5 %collective-permute-start.31 = (bf16[2,128,512]{2,1,0:T(8,128)(2,1)S(1)}, bf16[2,128,512]{2,1,0:T(8,128)(2,1)S(1)}, u32[]{:S(2)}, u32[]{:S(2)}) collective-permute-start(bf16[2,128,512]{2,1,0:T(8,128)(2,1)S(1)} %get-tuple-element.60), channel_id=1, source_target_pairs={{0,32},{32,0},{64,96},{96,64},{1,33},{33,1},{65,97},{97,65},{2,34}... | collective-permute-start | bytes 786440 | tf_op jit(solution)/shard_map/ppermute | solution.py:16
  131.5 18.0 %collective-permute-start.27 = (bf16[3,8,8192]{2,1,0:T(8,128)(2,1)S(1)}, bf16[3,8,8192]{2,1,0:T(8,128)(2,1)S(1)}, u32[]{:S(2)}, u32[]{:S(2)}) collective-permute-start(bf16[3,8,8192]{2,1,0:T(8,128)(2,1)S(1)} %pad_maximum_fusion.7), channel_id=1, source_target_pairs={{0,8},{8,0},{1,9},{9,1},{2,10},{10,2},{3,11},{11,3},{4,12},{12,4},... | collective-permute-start | bytes 1179656 | tf_op jit(solution)/shard_map/ppermute | solution.py:16
  142.8 8.1 %collective-permute-start.25 = (bf16[4,8,4096]{2,1,0:T(8,128)(2,1)S(1)}, bf16[4,8,4096]{2,1,0:T(8,128)(2,1)S(1)}, u32[]{:S(2)}, u32[]{:S(2)}) collective-permute-start(bf16[4,8,4096]{2,1,0:T(8,128)(2,1)S(1)} %get-tuple-element.67), channel_id=1, source_target_pairs={{0,7},{1,2},{2,1},{3,4},{4,3},{5,6},{6,5},{7,0},{8,15},{9,10},{10,... | collective-permute-start | bytes 786440 | tf_op jit(solution)/shard_map/ppermute | solution.py:28
  145.0 13.1 %collective-permute-start.29 = (bf16[4,8,4096]{2,1,0:T(8,128)(2,1)S(1)}, bf16[4,8,4096]{2,1,0:T(8,128)(2,1)S(1)}, u32[]{:S(2)}, u32[]{:S(2)}) collective-permute-start(bf16[4,8,4096]{2,1,0:T(8,128)(2,1)S(1)} %get-tuple-element.68), channel_id=1, source_target_pairs={{0,1},{1,0},{2,3},{3,2},{4,5},{5,4},{6,7},{7,6},{8,9},{9,8},{10,11... | collective-permute-start | bytes 786440 | tf_op jit(solution)/shard_map/ppermute | solution.py:16
  145.2 11.7 %copy-start.7 = (bf16[448,4096]{1,0:T(8,128)(2,1)S(1)}, bf16[448,4096]{1,0:T(8,128)(2,1)}, u32[]{:S(2)}) copy-start(bf16[448,4096]{1,0:T(8,128)(2,1)} %param.10) | copy-start | bytes 11010052
  145.2 5.8 %collective-permute-start.34 = (bf16[2,4,128,256]{3,2,0,1:T(8,128)(2,1)S(1)}, bf16[2,4,128,256]{3,2,0,1:T(8,128)(2,1)S(1)}, u32[]{:S(2)}, u32[]{:S(2)}) collective-permute-start(bf16[2,4,128,256]{3,2,0,1:T(8,128)(2,1)S(1)} %get-tuple-element.56), channel_id=1, source_target_pairs={{0,16},{16,0},{1,17},{17,1},{2,18},{18,2},{3,19},{19,3},{4,20},{20... | collective-permute-start | bytes 1572872 | tf_op jit(solution)/shard_map/ppermute | solution.py:16
  149.5 7.4 %collective-permute-start.28 = (bf16[4,8,4096]{2,1,0:T(8,128)(2,1)S(1)}, bf16[4,8,4096]{2,1,0:T(8,128)(2,1)S(1)}, u32[]{:S(2)}, u32[]{:S(2)}) collective-permute-start(bf16[4,8,4096]{2,1,0:T(8,128)(2,1)S(1)} %get-tuple-element.69), channel_id=1, source_target_pairs={{0,7},{1,2},{2,1},{3,4},{4,3},{5,6},{6,5},{7,0},{8,15},{9,10},{10,... | collective-permute-start | bytes 786440 | tf_op jit(solution)/shard_map/ppermute | solution.py:28
  150.9 7.2 %collective-permute-start.30 = (bf16[4,8,4096]{2,1,0:T(8,128)(2,1)S(1)}, bf16[4,8,4096]{2,1,0:T(8,128)(2,1)S(1)}, u32[]{:S(2)}, u32[]{:S(2)}) collective-permute-start(bf16[4,8,4096]{2,1,0:T(8,128)(2,1)S(1)} %get-tuple-element.70), channel_id=1, source_target_pairs={{0,1},{1,0},{2,3},{3,2},{4,5},{5,4},{6,7},{7,6},{8,9},{9,8},{10,11... | collective-permute-start | bytes 786440 | tf_op jit(solution)/shard_map/ppermute | solution.py:16
  158.1 38.4 %copy-start = (bf16[256,2,448]{0,2,1:T(8,128)(2,1)S(1)}, bf16[256,2,448]{0,2,1:T(8,128)(2,1)}, u32[]{:S(2)}) copy-start(bf16[256,2,448]{0,2,1:T(8,128)(2,1)} %param.11) | copy-start | bytes 1376260
  159.3 20.0 %collective-permute-start.36 = (bf16[896,128]{1,0:T(8,128)(2,1)S(1)}, bf16[896,128]{1,0:T(8,128)(2,1)S(1)}, u32[]{:S(2)}, u32[]{:S(2)}) collective-permute-start(bf16[896,128]{1,0:T(8,128)(2,1)S(1)} %pad_maximum_fusion.11), channel_id=1, source_target_pairs={{0,128},{128,0},{1,129},{129,1},{2,130},{130,2},{3,131},{131,3},{4... | collective-permute-start | bytes 688136 | tf_op jit(solution)/shard_map/ppermute | solution.py:16
  173.1 21.9 %collective-permute-start.35 = (bf16[4,896,128]{2,1,0:T(8,128)(2,1)S(1)}, bf16[4,896,128]{2,1,0:T(8,128)(2,1)}, u32[]{:S(2)}, u32[]{:S(2)}) collective-permute-start(bf16[4,896,128]{2,1,0:T(8,128)(2,1)S(1)} %bitcast.154), channel_id=1, source_target_pairs={{0,16},{16,0},{1,17},{17,1},{2,18},{18,2},{3,19},{19,3},{4,20},{20... | collective-permute-start | bytes 2752520 | tf_op jit(solution)/shard_map/ppermute | solution.py:16
  192.1 4.4 %collective-permute-start.37 = (bf16[4,896,128]{2,1,0:T(8,128)(2,1)S(1)}, bf16[4,896,128]{2,1,0:T(8,128)(2,1)}, u32[]{:S(2)}, u32[]{:S(2)}) collective-permute-start(bf16[4,896,128]{2,1,0:T(8,128)(2,1)S(1)} %bitcast.156), channel_id=1, source_target_pairs={{0,16},{16,0},{1,17},{17,1},{2,18},{18,2},{3,19},{19,3},{4,20},{20... | collective-permute-start | bytes 2752520 | tf_op jit(solution)/shard_map/ppermute | solution.py:16
  196.4 1.0 copy-start.4
  201.8 1.0 copy-start.2
  226.8 1.2 copy-start.3
Sparse Core Ops, SparseCore 0:
  19.1 43.8 all-gather.3
